TPU v7x, 32 devices: a whole 2x2x4 slice. The times are simulated.
32 devices in a mesh: src: 4 (over y, x), tgt: 8 (over z, core).
Axes of the slice: x: 2, y: 2, z: 4, core: 2. Of those that a mesh axis runs over, the one named last changes fastest.
Arguments:
- incident: bfloat16 [4, 1024, 2048], P('src', 'tgt'), may hold values from -6 to 6
- factors: bfloat16 [12, 4, 1024, 32, 128], P(None, 'src', 'tgt'), may hold values from -0.5 to 0.5
- near_blocks: bfloat16 [4, 1024, 32, 512], P('src', 'tgt'), may hold values from -0.25 to 0.25
- near_lists: int32 [4, 1024, 8], P('src', 'tgt'), may hold values from 0 to 8
Outputs:
- scattered: float32 [4, 1024, 2048], P('src', 'tgt')
Inputs may be any that keep to these rules, and one draw needn't show every extreme that they name: `near_lists`: offset o of block q names source block q + o - 4 of the same row; offsets may repeat within a list.
All inputs are finite; a program needn't handle non-finite values.
Results may differ from a plain program's by a relative error of at most 0.014.
Values may be sent and summed in bfloat16 or wider, within the bound.
No kernel may reach another device: no remote copies, remote signals or barrier semaphores. Data moves between devices by JAX's collectives and lax.ppermute only.
A program may use at most 128 MiB of HBM per device.

v0:
```python
import jax
import jax.numpy as jnp
from jax import lax
from jax.sharding import PartitionSpec as P

HW = 4


def padded(x, sides, width):
    for axis, dim in sides:
        count, length = (lax.axis_size(axis), x.shape[dim])
        up = [(i, (i + 1) % count) for i in range(count - 1)]
        down = [(j, i) for i, j in up]
        last = lax.slice_in_dim(x, length - width, length, axis=dim)
        leading = lax.slice_in_dim(x, 0, width, axis=dim)
        before = lax.ppermute(last, axis, up)
        after = lax.ppermute(leading, axis, down)
        x = jnp.concatenate([before, x, after], axis=dim)
    return x


def from_partner(block, axis, bit):
    count = lax.axis_size(axis)
    route = []
    for low in range(count):
        high = low | 1 << bit
        if high != low and high < count:
            route += [(low, high), (high, low)]
    return lax.ppermute(block, axis, route)


def join_parts(products, fields):
    first = products[:, :, 0]
    second = products[:, :, 1]
    real_part = first[..., :fields] - second[..., fields:]
    imag_part = first[..., fields:] + second[..., :fields]
    return jnp.concatenate([real_part, imag_part], axis=-1)


def mix_level(own_part, partner, weights):
    nblock, rows = (weights.shape[0], weights.shape[1])
    stacked = jnp.concatenate([own_part, partner], axis=1)
    mats = weights.reshape(nblock, rows, 2, 2 * rows)
    products = jnp.einsum("bipc,bcf->bipf", mats, stacked, preferred_element_type=jnp.float32)
    return join_parts(products, own_part.shape[2] // 2)


def local_flip(vector, step_bit):
    dims_old = vector.shape
    size_bit = 2**step_bit
    dims_new = (dims_old[0] // (2 * size_bit), 2, size_bit) + dims_old[1:]
    return jnp.flip(vector.reshape(dims_new), axis=1).reshape(dims_old)


def per_device(incident, factors, near_blocks, near_lists):
    src_bits = lax.axis_size("src").bit_length() - 1
    tgt_bits = lax.axis_size("tgt").bit_length() - 1
    groups = lax.axis_size("tgt")
    blocks = incident.shape[1]
    rank_rows = near_blocks.shape[2]
    row_width = incident.shape[2] // rank_rows
    fields = row_width // 2
    near_count = near_lists.shape[2]
    levels_all = factors.shape[0]
    lows = blocks // groups
    low_bits = lows.bit_length() - 1
    window = padded(incident, (("tgt", 1),), HW)
    window = window.reshape(blocks + 2 * HW, rank_rows, row_width)
    near_index = jnp.arange(blocks, dtype=jnp.int32)[:, None] + near_lists[0]
    gathered = window[near_index]
    near_mats = near_blocks[0].reshape(blocks, rank_rows, near_count, 2, rank_rows)
    near_products = jnp.einsum(
        "bikpj,bkjf->bipf", near_mats, gathered, preferred_element_type=jnp.float32
    )
    near_part = join_parts(near_products, fields)
    vector = incident[0].reshape(blocks, rank_rows, row_width)
    weights = factors[:, 0]
    level = 0
    for step_bit in range(src_bits):
        partner = from_partner(vector, "src", step_bit)
        vector = mix_level(vector, partner, weights[level]).astype(jnp.bfloat16)
        level += 1
    for step_bit in range(low_bits):
        vector = mix_level(vector, local_flip(vector, step_bit), weights[level]).astype(
            jnp.bfloat16
        )
        level += 1
    moved = lax.all_to_all(
        vector.reshape(groups, lows, rank_rows, row_width),
        "tgt",
        split_axis=0,
        concat_axis=0,
        tiled=True,
    )
    vector = moved.reshape(blocks, rank_rows, row_width)
    for step_bit in range(tgt_bits):
        vector = mix_level(vector, local_flip(vector, low_bits + step_bit), weights[level]).astype(
            jnp.bfloat16
        )
        level += 1
    result = None
    for step_bit in range(tgt_bits):
        partner = from_partner(vector, "tgt", step_bit)
        mixed = mix_level(vector, partner, weights[level])
        level += 1
        if level == levels_all:
            result = mixed
        else:
            vector = mixed.astype(jnp.bfloat16)
    total = near_part + result
    return total.reshape(1, blocks, rank_rows * row_width)


def solution(mesh):
    return jax.shard_map(
        per_device,
        mesh=mesh,
        in_specs=(
            P("src", "tgt", None),
            P(None, "src", "tgt", None, None),
            P("src", "tgt", None, None),
            P("src", "tgt", None),
        ),
        out_specs=P("src", "tgt", None),
        check_vma=False,
    )
```

profile of v0, /device:TPU:0, one launch (start us, length us, event | category | flops | bytes accessed | tf_op | source)
XLA Modules:
  0.0 317.5 jit_solution(7161919861617456451)
XLA Ops:
  2.0 2.9 collective-permute-start.2
  5.0 3.4 %copy.69 = bf16[128,32,64]{2,1,0:T(8,128)(2,1)} copy(bf16[128,32,64]{0,2,1:T(8,128)(2,1)} %bitcast.11) | data formatting | bytes 1048576 | tf_op jit(solution)/shard_map/reshape;squeeze | solution.py:76
  8.4 9.2 %fusion.78 = (bf16[1,1,128,32,128]{4,3,2,1,0:T(8,128)(2,1)S(1)}, bf16[1,1,128,32,128]{4,3,2,1,0:T(8,128)(2,1)}, bf16[1,1,128,32,128]{4,3,2,1,0:T(8,128)(2,1)}, b...) fusion(bf16[12,1,128,32,128]{4,3,2,1,0:T(8,128)(2,1)} %param.5), kind=kLoop, calls=%fused_computation.172 | loop fusion | bytes 25165824 | tf_op jit(solution)/shard_map/slice | solution.py:81
  19.2 3.9 %copy.72 = bf16[128,32,2,64]{3,1,2,0:T(8,128)(2,1)S(1)} copy(bf16[128,32,2,64]{0,3,2,1:T(8,128)(2,1)} %bitcast.250) | data formatting | bytes 2097152 | tf_op jit(solution)/shard_map/reshape;squeeze | solution.py:43
  23.2 3.3 %copy.70 = bf16[128,32,64]{2,1,0:T(8,128)(2,1)} copy(bf16[128,32,64]{0,2,1:T(8,128)(2,1)} %collective-permute-done.2) | data formatting | bytes 1048576 | tf_op jit(solution)/shard_map/ppermute | solution.py:29
  32.1 3.0 copy.74
  39.3 4.7 %copy.89 = bf16[128,32,2,64]{3,1,2,0:T(8,128)(2,1)} copy(bf16[128,32,2,64]{0,3,2,1:T(8,128)(2,1)} %bitcast.251) | data formatting | bytes 2097152 | tf_op jit(solution)/shard_map/reshape;squeeze | solution.py:43
  46.7 4.7 %copy.86 = bf16[128,32,2,64]{3,1,2,0:T(8,128)(2,1)} copy(bf16[128,32,2,64]{0,3,2,1:T(8,128)(2,1)} %bitcast.252) | data formatting | bytes 2097152 | tf_op jit(solution)/shard_map/reshape;squeeze | solution.py:43
  54.0 16.2 %copy.83 = bf16[128,32,2,64]{3,1,2,0:T(8,128)(2,1)} copy(bf16[128,32,2,64]{0,3,2,1:T(8,128)(2,1)} %bitcast.253) | data formatting | bytes 2097152 | tf_op jit(solution)/shard_map/reshape;squeeze | solution.py:43
  72.8 4.8 %copy.80 = bf16[128,32,2,64]{3,1,2,0:T(8,128)(2,1)} copy(bf16[128,32,2,64]{0,3,2,1:T(8,128)(2,1)} %bitcast.254) | data formatting | bytes 2097152 | tf_op jit(solution)/shard_map/reshape;squeeze | solution.py:43
  80.2 4.7 %copy.77 = bf16[128,32,2,64]{3,1,2,0:T(8,128)(2,1)} copy(bf16[128,32,2,64]{0,3,2,1:T(8,128)(2,1)} %bitcast.255) | data formatting | bytes 2097152 | tf_op jit(solution)/shard_map/reshape;squeeze | solution.py:43
  84.9 3.3 %copy.75 = bf16[128,32,64]{2,1,0:T(8,128)(2,1)} copy(bf16[128,32,64]{0,2,1:T(8,128)(2,1)} %collective-permute-done.3) | data formatting | bytes 1048576 | tf_op jit(solution)/shard_map/ppermute | solution.py:29
  88.2 2.9 convolution_bitcast_fusion.10
  113.8 3.3 %convolution_bitcast_fusion.7 = f32[128,32,2,64]{3,1,2,0:T(8,128)S(1)} fusion(bf16[128,32,2,64]{3,1,2,0:T(8,128)(2,1)} %copy.86, bf16[128,32,64]{2,1,0:T(8,128)(2,1)} %bitcast.246, bf16[128,32,32]{2,1,0:T(8,128)(2,1)S(1)} %get-tuple-element.50, bf16[128,32,32]{2,1,0:T(8,128)(2,1)S(1)} %get-tuple-element.49), kind=kOutput, calls=%fused_computation.8 | convolution fusion | flops 70254592 | bytes 4194304 | tf_op jit(solution)/shard_map/bipc,bcf->bipf/dot_general | solution.py:44
  129.5 4.9 %all-to-all-start = ((bf16[8,2,16384]{2,1,0:T(2,128)(2,1)}), bf16[8,2,16384]{2,1,0:T(2,128)(2,1)}, u32[]{:S(2)}, u32[]{:S(2)}) async-start(bf16[8,2,16384]{2,1,0:T(2,128)(2,1)} %reshape.217), calls=%async_computation | async-start | bytes 1048576 | tf_op jit(solution)/shard_map/all_to_all | solution.py:88
  135.4 3.8 %copy.98 = bf16[128,32,2,64]{3,1,2,0:T(8,128)(2,1)} copy(bf16[128,32,2,64]{0,3,2,1:T(8,128)(2,1)S(1)} %bitcast.256) | data formatting | bytes 2097152 | tf_op jit(solution)/shard_map/reshape;squeeze | solution.py:43
  140.2 3.7 %copy.95 = bf16[128,32,2,64]{3,1,2,0:T(8,128)(2,1)} copy(bf16[128,32,2,64]{0,3,2,1:T(8,128)(2,1)S(1)} %bitcast.257) | data formatting | bytes 2097152 | tf_op jit(solution)/shard_map/reshape;squeeze | solution.py:43
  144.9 3.0 copy.92
  173.1 3.0 copy.100
  182.5 4.7 %copy.103 = bf16[128,32,2,64]{3,1,2,0:T(8,128)(2,1)} copy(bf16[128,32,2,64]{0,3,2,1:T(8,128)(2,1)} %bitcast.259) | data formatting | bytes 2097152 | tf_op jit(solution)/shard_map/reshape;squeeze | solution.py:43
  199.0 7.9 %copy.65 = bf16[1,128,32,512]{1,3,2,0:T(8,128)(2,1)} copy(bf16[1,128,32,512]{3,2,1,0:T(8,128)(2,1)} %param.6) | data formatting | bytes 8388608 | tf_op args[2]
  206.9 23.2 %copy.66 = bf16[128,32,8,2,32]{4,1,2,3,0:T(8,128)(2,1)} copy(bf16[128,32,8,2,32]{0,4,3,2,1:T(8,128)(2,1)} %bitcast.227) | data formatting | bytes 8388608 | tf_op jit(solution)/shard_map/reshape;squeeze | solution.py:71
  231.9 4.8 %copy.108 = bf16[128,32,2,64]{3,1,2,0:T(8,128)(2,1)} copy(bf16[128,32,2,64]{0,3,2,1:T(8,128)(2,1)} %bitcast.260) | data formatting | bytes 2097152 | tf_op jit(solution)/shard_map/reshape;squeeze | solution.py:43
  238.3 5.0 %copy.130 = bf16[128,32,2,64]{3,1,0,2:T(8,128)(2,1)} copy(bf16[128,32,2,64]{0,3,2,1:T(8,128)(2,1)} %bitcast.261) | data formatting | bytes 2097152 | tf_op jit(solution)/shard_map/reshape;squeeze | solution.py:43
  246.5 9.9 %gather_fusion = bf16[1024,32,64]{2,1,0:T(8,128)(2,1)} fusion(bf16[136,32,64]{2,1,0:T(8,128)(2,1)S(1)} %reshape.185, s32[1024]{0:T(1024)S(1)} %broadcast_clamp_fusion), kind=kCustom, calls=%fused_computation | custom fusion | bytes 8392704 | tf_op jit(solution)/shard_map/gather | solution.py:70
  268.7 12.8 %convolution_bitcast_fusion.12 = f32[128,32,2,64]{3,1,2,0:T(8,128)} fusion(bf16[128,8,32,64,1]{3,2,1,4,0:T(8,128)(2,1)} %bitcast.226, bf16[128,32,8,2,32]{4,1,2,3,0:T(8,128)(2,1)} %copy.66), kind=kOutput, calls=%fused_computation.13 | convolution fusion | flops 268435456 | bytes 10485760 | tf_op jit(solution)/shard_map/bikpj,bkjf->bipf/dot_general | solution.py:72
  281.6 4.1 %slice_bitcast_fusion.25 = (f32[128,32,64]{2,1,0:T(8,128)S(1)}, f32[128,32,64]{2,1,0:T(8,128)}) fusion(f32[128,32,2,64]{3,1,2,0:T(8,128)} %convolution_bitcast_fusion.12), kind=kLoop, calls=%fused_computation.87 | loop fusion | bytes 4194304 | tf_op jit(solution)/shard_map/squeeze | solution.py:33
  285.6 6.6 %collective-permute-done.6 = bf16[128,32,64]{0,2,1:T(8,128)(2,1)} collective-permute-done((bf16[128,32,64]{0,2,1:T(8,128)(2,1)}, bf16[128,32,64]{0,2,1:T(8,128)(2,1)}, u32[]{:S(2)}, u32[]{:S(2)}) %collective-permute-start.6) | collective-permute-done | bytes 524320 | tf_op jit(solution)/shard_map/ppermute | solution.py:29
  292.2 3.3 %copy.111 = bf16[128,32,64]{2,1,0:T(8,128)(2,1)} copy(bf16[128,32,64]{0,2,1:T(8,128)(2,1)} %collective-permute-done.6) | data formatting | bytes 1048576 | tf_op jit(solution)/shard_map/ppermute | solution.py:29
  295.5 3.2 %convolution_bitcast_fusion = f32[128,32,2,64]{3,1,0,2:T(8,128)S(1)} fusion(bf16[128,32,2,64]{3,1,0,2:T(8,128)(2,1)} %copy.130, bf16[128,32,64]{2,1,0:T(8,128)(2,1)} %copy.111, bf16[128,32,32]{2,1,0:T(8,128)(2,1)} %copy-done.1, bf16[128,32,32]{2,1,0:T(8,128)(2,1)S(1)} %get-tuple-element.21), kind=kOutput, calls=%fused_computation.1 | convolution fusion | flops 70254592 | bytes 4194304 | tf_op jit(solution)/shard_map/bipc,bcf->bipf/dot_general | solution.py:44
  301.2 9.0 %slice_subtract_fusion = (f32[128,32,32]{2,1,0:T(8,128)}, f32[128,32,32]{2,1,0:T(8,128)}, f32[128,32,32]{2,1,0:T(8,128)}, f32[128,32,32]{2,1,0:T(8,128)}) fusion(f32[128,32,64]{2,1,0:T(8,128)} %get-tuple-element.20, f32[128,32,64]{2,1,0:T(8,128)} %get-tuple-element.19, f32[128,32,64]{2,1,0:T(8,128)S(1)} %copy-done, f32[128,32,64]{2,1,0:T(8,128)S(1)} %get-tuple-element.67), kind=kLoop, calls=%fused_computation.15 | loop fusion | flops 524288 | bytes 6291456 | tf_op jit(solution)/shard_map/sub | solution.py:35
  310.1 4.6 %maximum_add_fusion = f32[128,32,64]{2,1,0:T(8,128)S(1)} fusion(f32[128,32,32]{2,1,0:T(8,128)} %get-tuple-element.71, f32[128,32,32]{2,1,0:T(8,128)} %get-tuple-element.72, f32[128,32,32]{2,1,0:T(8,128)} %get-tuple-element.18, f32[128,32,32]{2,1,0:T(8,128)} %get-tuple-element.17), kind=kLoop, calls=%fused_computation.88 | loop fusion | flops 786432 | bytes 3145728 | tf_op jit(solution)/shard_map/add | solution.py:110
  (109 shorter events, 128.9 us)
Async XLA Ops:
  2.0 21.1 %collective-permute-start.2 = (bf16[128,32,64]{0,2,1:T(8,128)(2,1)}, bf16[128,32,64]{0,2,1:T(8,128)(2,1)}, u32[]{:S(2)}, u32[]{:S(2)}) collective-permute-start(bf16[128,32,64]{0,2,1:T(8,128)(2,1)} %bitcast.11), channel_id=1, source_target_pairs={{0,8},{8,0},{16,24},{24,16},{1,9},{9,1},{17,25},{25,17},{2,10},{10... | collective-permute-start | bytes 1572872 | tf_op jit(solution)/shard_map/ppermute | solution.py:29
  35.1 49.8 %collective-permute-start.3 = (bf16[128,32,64]{0,2,1:T(8,128)(2,1)}, bf16[128,32,64]{0,2,1:T(8,128)(2,1)}, u32[]{:S(2)}, u32[]{:S(2)}) collective-permute-start(bf16[128,32,64]{0,2,1:T(8,128)(2,1)} %copy.74), channel_id=1, source_target_pairs={{0,16},{16,0},{8,24},{24,8},{1,17},{17,1},{9,25},{25,9},{2,18},{18... | collective-permute-start | bytes 1572872 | tf_op jit(solution)/shard_map/ppermute | solution.py:29
  128.0 6.4 %copy-start.6 = (bf16[1,1,128,32,128]{4,3,2,1,0:T(8,128)(2,1)S(1)}, bf16[1,1,128,32,128]{4,3,2,1,0:T(8,128)(2,1)}, u32[]{:S(2)}) copy-start(bf16[1,1,128,32,128]{4,3,2,1,0:T(8,128)(2,1)} %get-tuple-element.8) | copy-start | bytes 3145732
  129.5 20.3 %all-to-all-start = ((bf16[8,2,16384]{2,1,0:T(2,128)(2,1)}), bf16[8,2,16384]{2,1,0:T(2,128)(2,1)}, u32[]{:S(2)}, u32[]{:S(2)}) async-start(bf16[8,2,16384]{2,1,0:T(2,128)(2,1)} %reshape.217), calls=%async_computation | async-start | bytes 1048576 | tf_op jit(solution)/shard_map/all_to_all | solution.py:88
  135.4 3.8 %copy-start.5 = (bf16[1,1,128,32,128]{4,3,2,1,0:T(8,128)(2,1)S(1)}, bf16[1,1,128,32,128]{4,3,2,1,0:T(8,128)(2,1)}, u32[]{:S(2)}) copy-start(bf16[1,1,128,32,128]{4,3,2,1,0:T(8,128)(2,1)} %get-tuple-element.9) | copy-start | bytes 3145732
  171.5 9.1 %copy-start.4 = (bf16[1,1,128,32,128]{4,3,2,1,0:T(8,128)(2,1)S(1)}, bf16[1,1,128,32,128]{4,3,2,1,0:T(8,128)(2,1)}, u32[]{:S(2)}) copy-start(bf16[1,1,128,32,128]{4,3,2,1,0:T(8,128)(2,1)} %get-tuple-element.7) | copy-start | bytes 3145732
  176.1 11.2 %collective-permute-start.4 = (bf16[128,32,64]{0,2,1:T(8,128)(2,1)}, bf16[128,32,64]{0,2,1:T(8,128)(2,1)}, u32[]{:S(2)}, u32[]{:S(2)}) collective-permute-start(bf16[128,32,64]{0,2,1:T(8,128)(2,1)} %copy.100), channel_id=1, source_target_pairs={{0,1},{1,0},{2,3},{3,2},{4,5},{5,4},{6,7},{7,6},{8,9},{9,8},{10,11... | collective-permute-start | bytes 1572872 | tf_op jit(solution)/shard_map/ppermute | solution.py:29
  176.9 66.5 %collective-permute-start = (bf16[1,4,2048]{2,1,0:T(4,128)(2,1)S(1)}, bf16[1,4,2048]{2,1,0:T(4,128)(2,1)S(1)}, u32[]{:S(2)}, u32[]{:S(2)}) collective-permute-start(bf16[1,4,2048]{2,1,0:T(4,128)(2,1)S(1)} %get-tuple-element.69), channel_id=1, source_target_pairs={{0,1},{1,2},{2,3},{3,4},{4,5},{5,6},{6,7},{8,9},{9,10},{10,11},{11... | collective-permute-start | bytes 49160 | tf_op jit(solution)/shard_map/ppermute | solution.py:16
  179.3 64.1 %collective-permute-start.1 = (bf16[1,4,2048]{2,1,0:T(4,128)(2,1)S(1)}, bf16[1,4,2048]{2,1,0:T(4,128)(2,1)S(1)}, u32[]{:S(2)}, u32[]{:S(2)}) collective-permute-start(bf16[1,4,2048]{2,1,0:T(4,128)(2,1)S(1)} %get-tuple-element.70), channel_id=1, source_target_pairs={{1,0},{2,1},{3,2},{4,3},{5,4},{6,5},{7,6},{9,8},{10,9},{11,10},{12... | collective-permute-start | bytes 49160 | tf_op jit(solution)/shard_map/ppermute | solution.py:17
  194.1 4.7 %copy-start.8 = (s32[1,128,8]{1,2,0:T(8,128)S(1)}, s32[1,128,8]{1,2,0:T(8,128)}, u32[]{:S(2)}) copy-start(s32[1,128,8]{1,2,0:T(8,128)} %param.7) | copy-start | bytes 12292
  196.5 59.8 %collective-permute-start.5 = (bf16[128,32,64]{0,2,1:T(8,128)(2,1)}, bf16[128,32,64]{0,2,1:T(8,128)(2,1)}, u32[]{:S(2)}, u32[]{:S(2)}) collective-permute-start(bf16[128,32,64]{0,2,1:T(8,128)(2,1)} %copy.105), channel_id=1, source_target_pairs={{0,2},{2,0},{1,3},{3,1},{4,6},{6,4},{5,7},{7,5},{8,10},{10,8},{9,1... | collective-permute-start | bytes 1572872 | tf_op jit(solution)/shard_map/ppermute | solution.py:29
  206.9 23.2 %copy-start.3 = (bf16[1,1,128,32,128]{4,3,2,1,0:T(8,128)(2,1)S(1)}, bf16[1,1,128,32,128]{4,3,2,1,0:T(8,128)(2,1)}, u32[]{:S(2)}) copy-start(bf16[1,1,128,32,128]{4,3,2,1,0:T(8,128)(2,1)} %get-tuple-element.6) | copy-start | bytes 3145732
  231.9 4.8 %copy-start.2 = (bf16[1,1,128,32,128]{4,3,2,1,0:T(8,128)(2,1)S(1)}, bf16[1,1,128,32,128]{4,3,2,1,0:T(8,128)(2,1)}, u32[]{:S(2)}) copy-start(bf16[1,1,128,32,128]{4,3,2,1,0:T(8,128)(2,1)} %get-tuple-element.16) | copy-start | bytes 3145732
  238.3 5.0 %copy-start.7 = (bf16[1,128,2048]{2,1,0:T(8,128)(2,1)S(1)}, bf16[1,128,2048]{2,1,0:T(8,128)(2,1)}, u32[]{:S(2)}) copy-start(bf16[1,128,2048]{2,1,0:T(8,128)(2,1)} %param.4) | copy-start | bytes 1572868
  263.1 1.0 copy-start.1
  266.6 25.6 %collective-permute-start.6 = (bf16[128,32,64]{0,2,1:T(8,128)(2,1)}, bf16[128,32,64]{0,2,1:T(8,128)(2,1)}, u32[]{:S(2)}, u32[]{:S(2)}) collective-permute-start(bf16[128,32,64]{0,2,1:T(8,128)(2,1)} %copy.110), channel_id=1, source_target_pairs={{0,4},{4,0},{1,5},{5,1},{2,6},{6,2},{3,7},{7,3},{8,12},{12,8},{9,1... | collective-permute-start | bytes 1572872 | tf_op jit(solution)/shard_map/ppermute | solution.py:29
  298.7 2.4 copy-start
where the time goes:
time: 323 us; the launch traced here: 318 us
  local copies, waits for them, and re-layouts  204 us (63%)
  matrix products  45.5 us (14%)
  other arithmetic  41.8 us (13%)
  starting transfers between devices  17.4 us (5%)
  waiting for transfers between devices  8.56 us (3%)
    another operation x12, local copies, waits for them, and re-layouts, mix_level(): mats = weights.reshape(nblock, rows, 2, 2 * rows)  64.1 us
    unnamed x34, local copies, waits for them, and re-layouts  38.2 us
    dot_general x12, matrix products, mix_level(): jnp.einsum('bipc,bcf->bipf', mats, stacked, preferred_element_type=jnp.fl...  32.6 us
    another operation x1, local copies, waits for them, and re-layouts, per_device(): near_blocks[0].reshape(blocks, rank_rows, near_count, 2, rank_rows)  23.2 us
    ppermute x5, local copies, waits for them, and re-layouts, from_partner(): return lax.ppermute(block, axis, route)  14.9 us
    concatenate x11, other arithmetic, join_parts(): return jnp.concatenate([real_part, imag_part], axis=-1)  14.4 us
    rev x7, local copies, waits for them, and re-layouts, local_flip(): return jnp.flip(vector.reshape(dims_new), axis=1).reshape(dims_old)  12.9 us
    another operation x11, other arithmetic  12.9 us
  transfers between devices with their start and end apart: 8, of which 2 were waited for; matrix products, arithmetic and copies ran while one was open for 54% of the time, Pallas kernels for 0%

commit v1 on v0

v1 whole, which is shorter than its diff:
```python
import functools

import jax
import jax.numpy as jnp
from jax import lax
from jax.experimental import pallas as pl
from jax.experimental.pallas import tpu as pltpu
from jax.sharding import PartitionSpec as P

HW = 4
BF = jnp.bfloat16
F32 = jnp.float32
VMEM_LIMIT = 40 * 1024 * 1024


def lane_of(x):
    return lax.broadcasted_iota(jnp.int32, x.shape, 1)


def half_swap(x):
    return pltpu.roll(x, x.shape[1] // 2, 1)


def times_i(x):
    width = x.shape[1]
    quarter = width // 4
    low = pltpu.roll(x, quarter, 1)
    high = pltpu.roll(x, width - quarter, 1)
    return jnp.where(lane_of(x) % (2 * quarter) < quarter, -high, low)


def pick_diag(res):
    rows = res.shape[0] // 2
    top, bottom = res[:rows], res[rows:]
    return jnp.where(lane_of(top) < res.shape[1] // 2, top, bottom)


def with_turn(x):
    return x, times_i(x.astype(F32)).astype(BF)


def mix(own, own_i, other, other_i, weights):
    stacked = jnp.concatenate([own, other, own_i, other_i], axis=0)
    res = lax.dot_general(
        weights, stacked, (((1,), (0,)), ((), ())), preferred_element_type=F32
    )
    return pick_diag(res)


def take_weights(w_ref, group, m, lows):
    w = w_ref[0, pl.ds(group * lows + 2 * m, 2)]
    return w.reshape(2 * w.shape[1], w.shape[2])


def params():
    return pltpu.CompilerParams(vmem_limit_bytes=VMEM_LIMIT)


def cost(blocks):
    return pl.CostEstimate(
        flops=blocks * 2 * 64 * 128 * 64, bytes_accessed=blocks * 16384, transcendentals=0
    )


def full(shape):
    zeros = (0,) * len(shape)
    return pl.BlockSpec(shape, lambda i, t: zeros)


def chunk_weights(factors, level, r, groups_in, lows):
    _, _, rows, cols = factors.shape
    return pl.BlockSpec(
        (1, groups_in * lows, rows, cols), lambda i, t: (level, (t[0] // groups_in) ^ r, 0, 0)
    )


def call(kernel, tgt_index, arrays, in_specs, out_shapes, out_specs, scratch, blocks, aliases=None):
    return pl.pallas_call(
        kernel,
        out_shape=out_shapes,
        grid_spec=pltpu.PrefetchScalarGridSpec(
            num_scalar_prefetch=1,
            grid=(1,),
            in_specs=in_specs,
            out_specs=out_specs,
            scratch_shapes=scratch,
        ),
        compiler_params=params(),
        cost_estimate=cost(blocks),
        input_output_aliases=aliases or {},
    )(tgt_index, *arrays)


def convert_kernel(G, lows, t, inc_ref, out_ref, wide, tall):
    half = lows // 2
    rank = out_ref.shape[2]
    for j in range(rank // 2):
        wide[j] = inc_ref[:, pl.ds(j * 128, 128)].astype(F32)
    for b in range(G):
        group = (t[0] % G) ^ b
        for j in range(rank // 2):
            even = wide[j, pl.ds(group * lows, half, stride=2), :]
            odd = wide[j, pl.ds(group * lows + 1, half, stride=2), :]
            low = lane_of(even) < 64
            tall[pl.ds(b * half * rank + 2 * j, half, stride=rank), :] = jnp.where(
                low, even, half_swap(odd)
            )
            tall[pl.ds(b * half * rank + 2 * j + 1, half, stride=rank), :] = jnp.where(
                low, half_swap(even), odd
            )
    out_ref[...] = tall[...].astype(BF).reshape(out_ref.shape)


def level_kernel(G, lows, flip, t, own_ref, other_ref, w_ref, out_ref):
    half = lows // 2
    for b in range(G):
        group = (t[0] % G) ^ b
        for m in range(half):
            own, own_i = with_turn(own_ref[b, m])
            other, other_i = with_turn(other_ref[b ^ flip, m])
            out_ref[b, m] = mix(
                own, own_i, other, other_i, take_weights(w_ref, group, m, lows)
            ).astype(BF)


def split_kernel(G, lows, low_bits, t, own_ref, other_ref, *rest):
    w_refs = rest[: 1 + low_bits]
    out_refs = rest[1 + low_bits : 1 + low_bits + G]
    half = lows // 2
    for b in range(G):
        group = (t[0] % G) ^ b
        values = []
        for m in range(half):
            own, own_i = with_turn(own_ref[b, m])
            other, other_i = with_turn(other_ref[b, m])
            values.append(
                mix(own, own_i, other, other_i, take_weights(w_refs[0], group, m, lows))
            )
        for bit in range(low_bits):
            pairs = [(x.astype(BF), times_i(x).astype(BF)) for x in values]
            new = []
            for m in range(half):
                own, own_i = pairs[m]
                if bit == 0:
                    other32 = half_swap(own.astype(F32))
                    other, other_i = other32.astype(BF), times_i(other32).astype(BF)
                else:
                    other, other_i = pairs[m ^ (1 << (bit - 1))]
                new.append(
                    mix(own, own_i, other, other_i, take_weights(w_refs[1 + bit], group, m, lows))
                )
            values = new
        for m in range(half):
            out_refs[b][m] = values[m].astype(BF)


def group_kernel(G, lows, groups, t, *refs):
    bits = groups.bit_length() - 1
    ins = refs[:groups]
    w_refs = refs[groups : groups + bits]
    outs = refs[groups + bits : groups + bits + groups // G]
    half = lows // 2

    def one(m):
        values = None
        pairs = [with_turn(ins[g][m]) for g in range(groups)]
        for bit in range(bits):
            values = [
                mix(
                    *pairs[g],
                    *pairs[g ^ (1 << bit)],
                    take_weights(w_refs[bit], t[0] ^ g, m, lows),
                )
                for g in range(groups)
            ]
            if bit < bits - 1:
                pairs = [(x.astype(BF), times_i(x).astype(BF)) for x in values]
        for g in range(groups):
            outs[g // G][g % G, m] = values[g].astype(BF)

    def body(m, carry):
        one(m)
        return carry

    lax.fori_loop(0, half, body, 0)


def final_kernel(G, lows, flip, t, own_ref, other_ref, w_ref, near_ref, *rest):
    out_ref, tall, wide = rest[-3:]
    half = lows // 2
    rank = own_ref.shape[2]
    for b in range(G):
        group = (t[0] % G) ^ b
        for m in range(half):
            own, own_i = with_turn(own_ref[b, m])
            other, other_i = with_turn(other_ref[b ^ flip, m])
            tall[pl.ds((b * half + m) * rank, rank), :] = (
                mix(own, own_i, other, other_i, take_weights(w_ref, group, m, lows))
                + near_ref[group * half + m]
            )
    for b in range(G):
        group = (t[0] % G) ^ b
        for j in range(rank // 2):
            first = tall[pl.ds(b * half * rank + 2 * j, half, stride=rank), :]
            second = tall[pl.ds(b * half * rank + 2 * j + 1, half, stride=rank), :]
            low = lane_of(first) < 64
            wide[j, pl.ds(group * lows, half, stride=2), :] = jnp.where(
                low, first, half_swap(second)
            )
            wide[j, pl.ds(group * lows + 1, half, stride=2), :] = jnp.where(
                low, half_swap(first), second
            )
    for j in range(rank // 2):
        out_ref[:, pl.ds(j * 128, 128)] = wide[j]


def near_kernel(G, lows, chunks, count, near_count, t, lists, *refs):
    v_refs = refs[:chunks]
    below_ref, above_ref, mats_ref, out_ref, window = refs[chunks : chunks + 5]
    half = lows // 2
    rank = v_refs[0].shape[2]

    def put(place, x):
        wide = x.astype(F32)
        low = lane_of(wide) < 64
        swapped = half_swap(wide)
        for side, dup in enumerate((jnp.where(low, wide, swapped), jnp.where(low, swapped, wide))):
            window[place + side, 0:rank, :] = dup.astype(BF)
            window[place + side, rank : 2 * rank, :] = times_i(dup).astype(BF)

    @pl.when(pl.program_id(0) == 0)
    def _():
        for e in range(HW // 2):
            put(2 * e, below_ref[e])
            put(HW + G * chunks * lows + 2 * e, above_ref[e])
        for r in range(chunks):
            for b in range(G):
                group = t[0] ^ (r * G + b)
                for m in range(half):
                    put(HW + group * lows + 2 * m, v_refs[r][b, m])

    base = pl.program_id(0) * count
    last = None
    for n in range(count):
        parts = [window[base + n + lists[base + n, k]] for k in range(near_count)]
        stacked = jnp.concatenate(parts, axis=0)
        res = lax.dot_general(
            mats_ref[n], stacked, (((1,), (0,)), ((), ())), preferred_element_type=F32
        )
        if n % 2 == 0:
            last = res
        else:
            out_ref[n // 2] = jnp.where(lane_of(res) < 64, last, res)


def near_field(tgt_index, lists, mats, chunks, below, above, G, lows):
    blocks, rank, cols = mats.shape
    near_count = lists.shape[1]
    count = 16
    v_shape = chunks[0].shape

    def spec(shape):
        zeros = (0,) * len(shape)
        return pl.BlockSpec(shape, lambda i, t, o: zeros)

    return pl.pallas_call(
        functools.partial(near_kernel, G, lows, len(chunks), count, near_count),
        out_shape=jax.ShapeDtypeStruct((blocks // 2, rank, 128), F32),
        grid_spec=pltpu.PrefetchScalarGridSpec(
            num_scalar_prefetch=2,
            grid=(blocks // count,),
            in_specs=[spec(v_shape) for _ in chunks]
            + [spec(below.shape), spec(above.shape)]
            + [pl.BlockSpec((count, rank, cols), lambda i, t, o: (i, 0, 0))],
            out_specs=pl.BlockSpec((count // 2, rank, 128), lambda i, t, o: (i, 0, 0)),
            scratch_shapes=[pltpu.VMEM((blocks + 2 * HW, 2 * rank, 128), BF)],
        ),
        compiler_params=params(),
        cost_estimate=pl.CostEstimate(
            flops=2 * blocks * rank * cols * 128, bytes_accessed=mats.size * 2, transcendentals=0
        ),
    )(tgt_index, lists, *chunks, below, above, mats)


def swapped_with(x, axis, distance):
    count = lax.axis_size(axis)
    return lax.ppermute(x, axis, [(i, i ^ distance) for i in range(count)])


def per_device(incident, factors, near_blocks, near_lists):
    groups = lax.axis_size("tgt")
    src_bits = lax.axis_size("src").bit_length() - 1
    tgt_bits = groups.bit_length() - 1
    blocks = incident.shape[1]
    rank = near_blocks.shape[2]
    lows = blocks // groups
    half = lows // 2
    low_bits = lows.bit_length() - 1
    G = 2
    chunks = groups // G
    order = list(range(chunks))[::-1]
    tgt_index = lax.axis_index("tgt").astype(jnp.int32).reshape(1)
    weights = factors[:, 0]
    chunk_shape = (G, half, rank, 128)
    chunk_out = jax.ShapeDtypeStruct(chunk_shape, BF)
    group_out = jax.ShapeDtypeStruct(chunk_shape[1:], BF)

    def chunk_rows(r, width):
        return pl.BlockSpec((G * lows, width), lambda i, t: ((t[0] // G) ^ r, 0))

    def wspec(level, r):
        return chunk_weights(weights, level, r, G, lows)

    def level_call(level, r, own, other, flip=0):
        return call(
            functools.partial(level_kernel, G, lows, flip),
            tgt_index,
            (own, other, weights),
            [full(chunk_shape), full(chunk_shape), wspec(level, r)],
            chunk_out,
            full(chunk_shape),
            [],
            G * lows,
        )

    width = incident.shape[2]
    v = [None] * chunks
    for r in order:
        v[r] = call(
            functools.partial(convert_kernel, G, lows),
            tgt_index,
            (incident[0],),
            [chunk_rows(r, width)],
            chunk_out,
            full(chunk_shape),
            [
                pltpu.VMEM((rank // 2, G * lows, 128), F32),
                pltpu.VMEM((G * half * rank, 128), F32),
            ],
            G * lows,
        )
    start = list(v)

    level = 0
    for bit in range(src_bits - 1):
        for r in order:
            v[r] = level_call(level, r, v[r], swapped_with(v[r], "src", 1 << bit))
        level += 1
    arrived = [None] * groups
    for r in order:
        partner = swapped_with(v[r], "src", 1 << (src_bits - 1))
        parts = call(
            functools.partial(split_kernel, G, lows, low_bits),
            tgt_index,
            (v[r], partner) + (weights,) * (1 + low_bits),
            [full(chunk_shape), full(chunk_shape)]
            + [wspec(level + k, r) for k in range(1 + low_bits)],
            [group_out] * G,
            [full(chunk_shape[1:])] * G,
            [],
            (1 + low_bits) * G * lows,
        )
        for b in range(G):
            g = r * G + b
            arrived[g] = swapped_with(parts[b], "tgt", g) if g else parts[b]
    level += 1 + low_bits

    edge = HW // 2
    ups = [(i, i + 1) for i in range(groups - 1)]
    downs = [(i + 1, i) for i in range(groups - 1)]
    rows_in = incident[0]
    first, last = edge_pairs(rows_in, rank)
    below = lax.ppermute(last, "tgt", ups)
    above = lax.ppermute(first, "tgt", downs)
    near = near_field(tgt_index, near_lists[0], near_blocks[0], start, below, above, G, lows)

    v = call(
        functools.partial(group_kernel, G, lows, groups),
        tgt_index,
        tuple(arrived) + (weights,) * tgt_bits,
        [full(chunk_shape[1:])] * groups
        + [
            pl.BlockSpec((1, blocks, rank, 128), functools.partial(lambda l, i, t: (l, 0, 0, 0), level + k))
            for k in range(tgt_bits)
        ],
        [chunk_out] * chunks,
        [full(chunk_shape)] * chunks,
        [],
        tgt_bits * blocks,
    )
    v = list(v)
    level += tgt_bits
    for bit in range(tgt_bits - 1):
        distance = 1 << bit
        others = [swapped_with(v[r ^ (distance // G)], "tgt", distance) for r in range(chunks)]
        v = [level_call(level, r, v[r], others[r], distance % G) for r in range(chunks)]
        level += 1
    out = None
    distance = 1 << (tgt_bits - 1)
    others = [swapped_with(v[r ^ (distance // G)], "tgt", distance) for r in range(chunks)]
    for r in range(chunks):
        partner = others[r]
        arrays = (v[r], partner, weights, near)
        specs = [
            full(chunk_shape),
            full(chunk_shape),
            wspec(level, r),
            pl.BlockSpec(
                (G * half, rank, 128), functools.partial(lambda r, i, t: ((t[0] // G) ^ r, 0, 0), r)
            ),
        ]
        aliases = None
        if out is not None:
            arrays += (out,)
            specs += [pl.BlockSpec(memory_space=pl.ANY)]
            aliases = {5: 0}
        out = call(
            functools.partial(final_kernel, G, lows, distance % G),
            tgt_index,
            arrays,
            specs,
            jax.ShapeDtypeStruct((blocks, width), F32),
            chunk_rows(r, width),
            [
                pltpu.VMEM((G * half * rank, 128), F32),
                pltpu.VMEM((rank // 2, G * lows, 128), F32),
            ],
            G * lows,
            aliases,
        )
    return out[None]


def edge_pairs(rows_in, rank):
    def pairs(x):
        x = x.reshape(HW // 2, 2, rank, -1)
        return jnp.swapaxes(x, 1, 2).reshape(HW // 2, rank, -1)

    return pairs(rows_in[:HW]), pairs(rows_in[-HW:])


def solution(mesh):
    return jax.shard_map(
        per_device,
        mesh=mesh,
        in_specs=(
            P("src", "tgt", None),
            P(None, "src", "tgt", None, None),
            P("src", "tgt", None, None),
            P("src", "tgt", None),
        ),
        out_specs=P("src", "tgt", None),
        check_vma=False,
    )
```

time: 323 us -> 116 us (0.36)
  the two profiles are of different devices: /device:TPU:0 before, /device:TPU:9 now
where the time goes in v1:
time: 116 us; the launch traced here: 115 us
  starting transfers between devices  38.1 us (33%)
  Pallas kernels  35.6 us (31%)
  local copies, waits for them, and re-layouts  22.9 us (20%)
  waiting for transfers between devices  18.6 us (16%)
    ppermute x27, starting transfers between devices, swapped_with(): return lax.ppermute(x, axis, [(i, i ^ distance) for i in range(count)])  31.3 us
    pallas_call x25, Pallas kernels, call(): pl.pallas_call(kernel, out_shape=out_shapes, grid_spec=pltpu.PrefetchScal...  25.4 us
    unnamed x15, local copies, waits for them, and re-layouts  21.6 us
    pallas_call x1, Pallas kernels, near_field(): pl.pallas_call(functools.partial(near_kernel, G, lows, len(chunks), count...  10.2 us
    ppermute x27, waiting for transfers between devices, swapped_with(): return lax.ppermute(x, axis, [(i, i ^ distance) for i in range(count)])  9.83 us
    ppermute x1, waiting for transfers between devices, per_device(): below = lax.ppermute(last, 'tgt', ups)  5.04 us
    ppermute x1, starting transfers between devices, per_device(): below = lax.ppermute(last, 'tgt', ups)  4.88 us
    ppermute x1, waiting for transfers between devices, per_device(): above = lax.ppermute(first, 'tgt', downs)  3.76 us
  transfers between devices with their start and end apart: 29, of which 8 were waited for; matrix products, arithmetic and copies ran while one was open for 1% of the time, Pallas kernels for 24%

profile of v1, /device:TPU:9, one launch (start us, length us, event | category | flops | bytes accessed | tf_op | source)
XLA Modules:
  0.0 115.5 jit_solution(5579792793237207620)
XLA Ops:
  1.3 1.3 %collective-permute-start.7 = (bf16[2,8,32,128]{3,2,1,0:T(8,128)(2,1)S(1)}, bf16[2,8,32,128]{3,2,1,0:T(8,128)(2,1)S(1)}, u32[]{:S(2)}, u32[]{:S(2)}) collective-permute-start(bf16[2,8,32,128]{3,2,1,0:T(8,128)(2,1)S(1)} %shard_map.52.own_ref.refs_2_), channel_id=1, source_target_pairs={{0,8},{8,0},{16,24},{24,16},{1,9},{9,1},{17,25},{25,17},{2,10},{10... | collective-permute-start | bytes 393224 | tf_op jit(solution)/shard_map/ppermute | solution.py:287
  3.4 1.3 %collective-permute-start.3 = (bf16[2,8,32,128]{3,2,1,0:T(8,128)(2,1)S(1)}, bf16[2,8,32,128]{3,2,1,0:T(8,128)(2,1)S(1)}, u32[]{:S(2)}, u32[]{:S(2)}) collective-permute-start(bf16[2,8,32,128]{3,2,1,0:T(8,128)(2,1)S(1)} %shard_map.49.own_ref.refs_1_), channel_id=1, source_target_pairs={{0,8},{8,0},{16,24},{24,16},{1,9},{9,1},{17,25},{25,17},{2,10},{10... | collective-permute-start | bytes 393224 | tf_op jit(solution)/shard_map/ppermute | solution.py:287
  5.7 4.6 %copy-done = bf16[12,1,128,32,128]{4,3,2,1,0:T(8,128)(2,1)S(1)} copy-done((bf16[12,1,128,32,128]{4,3,2,1,0:T(8,128)(2,1)S(1)}, bf16[12,1,128,32,128]{4,3,2,1,0:T(8,128)(2,1)}, u32[]{:S(2)}) %copy-start) | copy-done | bytes 12582936
  10.7 1.3 %collective-permute-start.8 = (bf16[2,8,32,128]{3,2,1,0:T(8,128)(2,1)S(1)}, bf16[2,8,32,128]{3,2,1,0:T(8,128)(2,1)S(1)}, u32[]{:S(2)}, u32[]{:S(2)}) collective-permute-start(bf16[2,8,32,128]{3,2,1,0:T(8,128)(2,1)S(1)} %shard_map.53.own_ref), channel_id=1, source_target_pairs={{0,16},{8,24},{16,0},{24,8},{1,17},{9,25},{17,1},{25,9},{2,18},{10... | collective-permute-start | bytes 393224 | tf_op jit(solution)/shard_map/ppermute | solution.py:287
  13.0 1.3 %collective-permute-start.4 = (bf16[2,8,32,128]{3,2,1,0:T(8,128)(2,1)S(1)}, bf16[2,8,32,128]{3,2,1,0:T(8,128)(2,1)S(1)}, u32[]{:S(2)}, u32[]{:S(2)}) collective-permute-start(bf16[2,8,32,128]{3,2,1,0:T(8,128)(2,1)S(1)} %shard_map.50.own_ref), channel_id=1, source_target_pairs={{0,16},{8,24},{16,0},{24,8},{1,17},{9,25},{17,1},{25,9},{2,18},{10... | collective-permute-start | bytes 393224 | tf_op jit(solution)/shard_map/ppermute | solution.py:287
  14.3 4.6 %copy-done.1 = bf16[12,1,128,32,128]{4,3,2,1,0:T(8,128)(2,1)S(1)} copy-done((bf16[12,1,128,32,128]{4,3,2,1,0:T(8,128)(2,1)S(1)}, bf16[12,1,128,32,128]{4,3,2,1,0:T(8,128)(2,1)}, u32[]{:S(2)}) %copy-start.1) | copy-done | bytes 12582936
  20.4 4.6 %copy-done.2 = bf16[12,1,128,32,128]{4,3,2,1,0:T(8,128)(2,1)S(1)} copy-done((bf16[12,1,128,32,128]{4,3,2,1,0:T(8,128)(2,1)S(1)}, bf16[12,1,128,32,128]{4,3,2,1,0:T(8,128)(2,1)}, u32[]{:S(2)}) %copy-start.2) | copy-done | bytes 12582936
  25.0 2.4 %shard_map.54 = (bf16[8,32,128]{2,1,0:T(8,128)(2,1)S(1)}, bf16[8,32,128]{2,1,0:T(8,128)(2,1)S(1)}) custom-call(s32[1]{0:T(128)} %bitcast.t, bf16[2,8,32,128]{3,2,1,0:T(8,128)(2,1)S(1)} %shard_map.53.own_ref, bf16[2,8,32,128]{3,2,1,0:T(8,128)(2,1)S(1)} %collective-permute-done.8.other_ref, bf16[12,128,32,128]{3,2,1,0:T(8,128)(2,1)S(1)} %bitcast.16, ...), custom_call_target="tpu_custom_call" | custom-call | flops 167772160 | bytes 2621440 | tf_op jit(solution)/shard_map/pallas_call | solution.py:78
  27.3 5.2 %collective-permute-start.10 = (bf16[8,32,128]{2,1,0:T(8,128)(2,1)S(1)}, bf16[8,32,128]{2,1,0:T(8,128)(2,1)S(1)}, u32[]{:S(2)}, u32[]{:S(2)}) collective-permute-start(bf16[8,32,128]{2,1,0:T(8,128)(2,1)S(1)} %get-tuple-element.22), channel_id=1, source_target_pairs={{0,5},{1,4},{2,7},{3,6},{4,1},{5,0},{6,3},{7,2},{8,13},{9,12},{10,... | collective-permute-start | bytes 196616 | tf_op jit(solution)/shard_map/ppermute | solution.py:287
  32.5 2.4 %shard_map.57 = (bf16[8,32,128]{2,1,0:T(8,128)(2,1)S(1)}, bf16[8,32,128]{2,1,0:T(8,128)(2,1)S(1)}) custom-call(s32[1]{0:T(128)} %bitcast.t, bf16[2,8,32,128]{3,2,1,0:T(8,128)(2,1)S(1)} %shard_map.56.own_ref, bf16[2,8,32,128]{3,2,1,0:T(8,128)(2,1)S(1)} %collective-permute-done.12.other_ref, bf16[12,128,32,128]{3,2,1,0:T(8,128)(2,1)S(1)} %bitcast.21, ...), custom_call_target="tpu_custom_call" | custom-call | flops 167772160 | bytes 2621440 | tf_op jit(solution)/shard_map/pallas_call | solution.py:78
  35.0 2.4 %shard_map.51 = (bf16[8,32,128]{2,1,0:T(8,128)(2,1)S(1)}, bf16[8,32,128]{2,1,0:T(8,128)(2,1)S(1)}) custom-call(s32[1]{0:T(128)} %bitcast.t, bf16[2,8,32,128]{3,2,1,0:T(8,128)(2,1)S(1)} %shard_map.50.own_ref, bf16[2,8,32,128]{3,2,1,0:T(8,128)(2,1)S(1)} %collective-permute-done.4.other_ref, bf16[12,128,32,128]{3,2,1,0:T(8,128)(2,1)S(1)} %bitcast.26, ...), custom_call_target="tpu_custom_call" | custom-call | flops 167772160 | bytes 2621440 | tf_op jit(solution)/shard_map/pallas_call | solution.py:78
  37.4 1.3 %collective-permute-start.5 = (bf16[8,32,128]{2,1,0:T(8,128)(2,1)S(1)}, bf16[8,32,128]{2,1,0:T(8,128)(2,1)S(1)}, u32[]{:S(2)}, u32[]{:S(2)}) collective-permute-start(bf16[8,32,128]{2,1,0:T(8,128)(2,1)S(1)} %get-tuple-element.19), channel_id=1, source_target_pairs={{0,2},{1,3},{2,0},{3,1},{4,6},{5,7},{6,4},{7,5},{8,10},{9,11},{10,... | collective-permute-start | bytes 196616 | tf_op jit(solution)/shard_map/ppermute | solution.py:287
  38.7 2.5 %collective-permute-start.6 = (bf16[8,32,128]{2,1,0:T(8,128)(2,1)S(1)}, bf16[8,32,128]{2,1,0:T(8,128)(2,1)S(1)}, u32[]{:S(2)}, u32[]{:S(2)}) collective-permute-start(bf16[8,32,128]{2,1,0:T(8,128)(2,1)S(1)} %get-tuple-element.20), channel_id=1, source_target_pairs={{0,3},{1,2},{2,1},{3,0},{4,7},{5,6},{6,5},{7,4},{8,11},{9,10},{10,... | collective-permute-start | bytes 196616 | tf_op jit(solution)/shard_map/ppermute | solution.py:287
  41.2 2.4 %shard_map.48 = (bf16[8,32,128]{2,1,0:T(8,128)(2,1)S(1)}, bf16[8,32,128]{2,1,0:T(8,128)(2,1)S(1)}) custom-call(s32[1]{0:T(128)} %bitcast.t, bf16[2,8,32,128]{3,2,1,0:T(8,128)(2,1)S(1)} %shard_map.47.own_ref, bf16[2,8,32,128]{3,2,1,0:T(8,128)(2,1)S(1)} %collective-permute-done.1.other_ref, bf16[12,128,32,128]{3,2,1,0:T(8,128)(2,1)S(1)} %bitcast.31, ...), custom_call_target="tpu_custom_call" | custom-call | flops 167772160 | bytes 2621440 | tf_op jit(solution)/shard_map/pallas_call | solution.py:78
  43.6 1.6 %collective-permute-start.9 = (bf16[8,32,128]{2,1,0:T(8,128)(2,1)S(1)}, bf16[8,32,128]{2,1,0:T(8,128)(2,1)S(1)}, u32[]{:S(2)}, u32[]{:S(2)}) collective-permute-start(bf16[8,32,128]{2,1,0:T(8,128)(2,1)S(1)} %get-tuple-element.21), channel_id=1, source_target_pairs={{0,4},{1,5},{2,6},{3,7},{4,0},{5,1},{6,2},{7,3},{8,12},{9,13},{10,... | collective-permute-start | bytes 196616 | tf_op jit(solution)/shard_map/ppermute | solution.py:287
  45.5 2.7 %collective-permute-done.9.refs_4_ = bf16[8,32,128]{2,1,0:T(8,128)(2,1)S(1)} collective-permute-done((bf16[8,32,128]{2,1,0:T(8,128)(2,1)S(1)}, bf16[8,32,128]{2,1,0:T(8,128)(2,1)S(1)}, u32[]{:S(2)}, u32[]{:S(2)}) %collective-permute-start.9) | collective-permute-done | bytes 65568 | tf_op jit(solution)/shard_map/ppermute | solution.py:287
  48.3 6.1 %shard_map.58 = (bf16[2,8,32,128]{3,2,1,0:T(8,128)(2,1)S(1)}, bf16[2,8,32,128]{3,2,1,0:T(8,128)(2,1)S(1)}, bf16[2,8,32,128]{3,2,1,0:T(8,128)(2,1)S(1)}, bf16[2,8,32,128]{3,2,1,0:T(8,128)(2,1)S(1)}) custom-call(s32[1]{0:T(128)} %bitcast.t, bf16[8,32,128]{2,1,0:T(8,128)(2,1)S(1)} %get-tuple-element.17.refs_0_, ...), custom_call_target="tpu_custom_call" | custom-call | flops 402653184 | bytes 6291456 | tf_op jit(solution)/shard_map/pallas_call | solution.py:78
  56.6 1.6 %collective-permute-start.24 = (bf16[2,8,32,128]{3,2,1,0:T(8,128)(2,1)S(1)}, bf16[2,8,32,128]{3,2,1,0:T(8,128)(2,1)S(1)}, u32[]{:S(2)}, u32[]{:S(2)}) collective-permute-start(bf16[2,8,32,128]{3,2,1,0:T(8,128)(2,1)S(1)} %shard_map.59.own_ref), channel_id=1, source_target_pairs={{0,2},{1,3},{2,0},{3,1},{4,6},{5,7},{6,4},{7,5},{8,10},{9,11},{10,... | collective-permute-start | bytes 393224 | tf_op jit(solution)/shard_map/ppermute | solution.py:287
  59.0 1.5 %collective-permute-start.25 = (bf16[2,8,32,128]{3,2,1,0:T(8,128)(2,1)S(1)}, bf16[2,8,32,128]{3,2,1,0:T(8,128)(2,1)S(1)}, u32[]{:S(2)}, u32[]{:S(2)}) collective-permute-start(bf16[2,8,32,128]{3,2,1,0:T(8,128)(2,1)S(1)} %shard_map.62.own_ref), channel_id=1, source_target_pairs={{0,2},{1,3},{2,0},{3,1},{4,6},{5,7},{6,4},{7,5},{8,10},{9,11},{10,... | collective-permute-start | bytes 393224 | tf_op jit(solution)/shard_map/ppermute | solution.py:287
  62.0 2.5 %collective-permute-start.28 = (bf16[2,8,32,128]{3,2,1,0:T(8,128)(2,1)S(1)}, bf16[2,8,32,128]{3,2,1,0:T(8,128)(2,1)S(1)}, u32[]{:S(2)}, u32[]{:S(2)}) collective-permute-start(bf16[2,8,32,128]{3,2,1,0:T(8,128)(2,1)S(1)} %shard_map.66.own_ref), channel_id=1, source_target_pairs={{0,4},{1,5},{2,6},{3,7},{4,0},{5,1},{6,2},{7,3},{8,12},{9,13},{10,... | collective-permute-start | bytes 393224 | tf_op jit(solution)/shard_map/ppermute | solution.py:287
  64.8 2.5 %collective-permute-start.27 = (bf16[2,8,32,128]{3,2,1,0:T(8,128)(2,1)S(1)}, bf16[2,8,32,128]{3,2,1,0:T(8,128)(2,1)S(1)}, u32[]{:S(2)}, u32[]{:S(2)}) collective-permute-start(bf16[2,8,32,128]{3,2,1,0:T(8,128)(2,1)S(1)} %shard_map.61.own_ref), channel_id=1, source_target_pairs={{0,4},{1,5},{2,6},{3,7},{4,0},{5,1},{6,2},{7,3},{8,12},{9,13},{10,... | collective-permute-start | bytes 393224 | tf_op jit(solution)/shard_map/ppermute | solution.py:287
  67.3 4.4 %collective-permute-done.25.other_ref = bf16[2,8,32,128]{3,2,1,0:T(8,128)(2,1)S(1)} collective-permute-done((bf16[2,8,32,128]{3,2,1,0:T(8,128)(2,1)S(1)}, bf16[2,8,32,128]{3,2,1,0:T(8,128)(2,1)S(1)}, u32[]{:S(2)}, u32[]{:S(2)}) %collective-permute-start.25) | collective-permute-done | bytes 131104 | tf_op jit(solution)/shard_map/ppermute | solution.py:287
  72.1 1.5 %collective-permute-start.26 = (bf16[2,8,32,128]{3,2,1,0:T(8,128)(2,1)S(1)}, bf16[2,8,32,128]{3,2,1,0:T(8,128)(2,1)S(1)}, u32[]{:S(2)}, u32[]{:S(2)}) collective-permute-start(bf16[2,8,32,128]{3,2,1,0:T(8,128)(2,1)S(1)} %shard_map.67.own_ref), channel_id=1, source_target_pairs={{0,4},{1,5},{2,6},{3,7},{4,0},{5,1},{6,2},{7,3},{8,12},{9,13},{10,... | collective-permute-start | bytes 393224 | tf_op jit(solution)/shard_map/ppermute | solution.py:287
  75.0 1.6 %collective-permute-start.21 = (bf16[2,8,32,128]{3,2,1,0:T(8,128)(2,1)S(1)}, bf16[2,8,32,128]{3,2,1,0:T(8,128)(2,1)S(1)}, u32[]{:S(2)}, u32[]{:S(2)}) collective-permute-start(bf16[2,8,32,128]{3,2,1,0:T(8,128)(2,1)S(1)} %shard_map.64.own_ref), channel_id=1, source_target_pairs={{0,4},{1,5},{2,6},{3,7},{4,0},{5,1},{6,2},{7,3},{8,12},{9,13},{10,... | collective-permute-start | bytes 393224 | tf_op jit(solution)/shard_map/ppermute | solution.py:287
  77.6 4.9 %collective-permute-start.22 = (bf16[2,32,128]{2,1,0:T(8,128)(2,1)S(1)}, bf16[2,32,128]{2,1,0:T(8,128)(2,1)S(1)}, u32[]{:S(2)}, u32[]{:S(2)}) collective-permute-start(bf16[2,32,128]{2,1,0:T(8,128)(2,1)S(1)} %reshape.21), channel_id=1, source_target_pairs={{0,1},{1,2},{2,3},{3,4},{4,5},{5,6},{6,7},{8,9},{9,10},{10,11},{11... | collective-permute-start | bytes 49160 | tf_op jit(solution)/shard_map/ppermute | solution.py:373
  82.8 5.0 %collective-permute-done.22.refs_4_ = bf16[2,32,128]{2,1,0:T(8,128)(2,1)S(1)} collective-permute-done((bf16[2,32,128]{2,1,0:T(8,128)(2,1)S(1)}, bf16[2,32,128]{2,1,0:T(8,128)(2,1)S(1)}, u32[]{:S(2)}, u32[]{:S(2)}) %collective-permute-start.22) | collective-permute-done | bytes 16416 | tf_op jit(solution)/shard_map/ppermute | solution.py:373
  87.8 1.9 %collective-permute-start.23 = (bf16[2,32,128]{2,1,0:T(8,128)(2,1)S(1)}, bf16[2,32,128]{2,1,0:T(8,128)(2,1)S(1)}, u32[]{:S(2)}, u32[]{:S(2)}) collective-permute-start(bf16[2,32,128]{2,1,0:T(8,128)(2,1)S(1)} %reshape.23), channel_id=1, source_target_pairs={{1,0},{2,1},{3,2},{4,3},{5,4},{6,5},{7,6},{9,8},{10,9},{11,10},{12... | collective-permute-start | bytes 49160 | tf_op jit(solution)/shard_map/ppermute | solution.py:374
  89.8 3.8 %collective-permute-done.23.refs_5_ = bf16[2,32,128]{2,1,0:T(8,128)(2,1)S(1)} collective-permute-done((bf16[2,32,128]{2,1,0:T(8,128)(2,1)S(1)}, bf16[2,32,128]{2,1,0:T(8,128)(2,1)S(1)}, u32[]{:S(2)}, u32[]{:S(2)}) %collective-permute-start.23) | collective-permute-done | bytes 16416 | tf_op jit(solution)/shard_map/ppermute | solution.py:374
  93.6 2.2 %copy-done.5 = bf16[1,128,32,512]{3,2,1,0:T(8,128)(2,1)S(1)} copy-done((bf16[1,128,32,512]{3,2,1,0:T(8,128)(2,1)S(1)}, bf16[1,128,32,512]{3,2,1,0:T(8,128)(2,1)}, u32[]{:S(2)}) %copy-start.5) | copy-done | bytes 4194328
  95.8 10.2 %shard_map.65.near_ref = f32[64,32,128]{2,1,0:T(8,128)S(1)} custom-call(s32[1]{0:T(128)} %bitcast.t, s32[128,8]{1,0:T(8,128)S(1)} %bitcast.56, bf16[2,8,32,128]{3,2,1,0:T(8,128)(2,1)S(1)} %shard_map.46.own_ref.refs_0_, bf16[2,8,32,128]{3,2,1,0:T(8,128)(2,1)S(1)} %shard_map.49.own_ref.refs_1_, bf16[2,8,32,128]{3,2,1,0:T(8,128)(2,1)S(1)} %shard_map.52.own_ref.refs_2_, ...), custom_call_target="tpu_custom_call" | custom-call | flops 536870912 | bytes 4194304 | tf_op jit(solution)/shard_map/pallas_call | solution.py:266
  106.0 4.6 %copy-done.3 = bf16[12,1,128,32,128]{4,3,2,1,0:T(8,128)(2,1)S(1)} copy-done((bf16[12,1,128,32,128]{4,3,2,1,0:T(8,128)(2,1)S(1)}, bf16[12,1,128,32,128]{4,3,2,1,0:T(8,128)(2,1)}, u32[]{:S(2)}) %copy-start.3) | copy-done | bytes 12582936
  111.8 1.2 %shard_map.69.rest_0_ = f32[128,2048]{1,0:T(8,128)} custom-call(s32[1]{0:T(128)} %bitcast.t, bf16[2,8,32,128]{3,2,1,0:T(8,128)(2,1)S(1)} %shard_map.64.own_ref, bf16[2,8,32,128]{3,2,1,0:T(8,128)(2,1)S(1)} %collective-permute-done.27.other_ref, bf16[12,128,32,128]{3,2,1,0:T(8,128)(2,1)S(1)} %bitcast.48, ...), custom_call_target="tpu_custom_call", output_to_operand_aliasing={{}: (5, {})} | custom-call | flops 33554432 | bytes 524288 | tf_op jit(solution)/shard_map/pallas_call | solution.py:78
  (74 shorter events, 18.1 us)
Async XLA Ops:
  1.3 4.4 %collective-permute-start.7 = (bf16[2,8,32,128]{3,2,1,0:T(8,128)(2,1)S(1)}, bf16[2,8,32,128]{3,2,1,0:T(8,128)(2,1)S(1)}, u32[]{:S(2)}, u32[]{:S(2)}) collective-permute-start(bf16[2,8,32,128]{3,2,1,0:T(8,128)(2,1)S(1)} %shard_map.52.own_ref.refs_2_), channel_id=1, source_target_pairs={{0,8},{8,0},{16,24},{24,16},{1,9},{9,1},{17,25},{25,17},{2,10},{10... | collective-permute-start | bytes 393224 | tf_op jit(solution)/shard_map/ppermute | solution.py:287
  2.8 9.1 %collective-permute-start.11 = (bf16[2,8,32,128]{3,2,1,0:T(8,128)(2,1)S(1)}, bf16[2,8,32,128]{3,2,1,0:T(8,128)(2,1)S(1)}, u32[]{:S(2)}, u32[]{:S(2)}) collective-permute-start(bf16[2,8,32,128]{3,2,1,0:T(8,128)(2,1)S(1)} %shard_map.55.own_ref.refs_3_), channel_id=1, source_target_pairs={{0,8},{8,0},{16,24},{24,16},{1,9},{9,1},{17,25},{25,17},{2,10},{10... | collective-permute-start | bytes 393224 | tf_op jit(solution)/shard_map/ppermute | solution.py:287
  3.4 9.2 %collective-permute-start.3 = (bf16[2,8,32,128]{3,2,1,0:T(8,128)(2,1)S(1)}, bf16[2,8,32,128]{3,2,1,0:T(8,128)(2,1)S(1)}, u32[]{:S(2)}, u32[]{:S(2)}) collective-permute-start(bf16[2,8,32,128]{3,2,1,0:T(8,128)(2,1)S(1)} %shard_map.49.own_ref.refs_1_), channel_id=1, source_target_pairs={{0,8},{8,0},{16,24},{24,16},{1,9},{9,1},{17,25},{25,17},{2,10},{10... | collective-permute-start | bytes 393224 | tf_op jit(solution)/shard_map/ppermute | solution.py:287
  4.9 9.3 %collective-permute-start = (bf16[2,8,32,128]{3,2,1,0:T(8,128)(2,1)S(1)}, bf16[2,8,32,128]{3,2,1,0:T(8,128)(2,1)S(1)}, u32[]{:S(2)}, u32[]{:S(2)}) collective-permute-start(bf16[2,8,32,128]{3,2,1,0:T(8,128)(2,1)S(1)} %shard_map.46.own_ref.refs_0_), channel_id=1, source_target_pairs={{0,8},{8,0},{16,24},{24,16},{1,9},{9,1},{17,25},{25,17},{2,10},{10... | collective-permute-start | bytes 393224 | tf_op jit(solution)/shard_map/ppermute | solution.py:287
  10.7 9.7 %collective-permute-start.8 = (bf16[2,8,32,128]{3,2,1,0:T(8,128)(2,1)S(1)}, bf16[2,8,32,128]{3,2,1,0:T(8,128)(2,1)S(1)}, u32[]{:S(2)}, u32[]{:S(2)}) collective-permute-start(bf16[2,8,32,128]{3,2,1,0:T(8,128)(2,1)S(1)} %shard_map.53.own_ref), channel_id=1, source_target_pairs={{0,16},{8,24},{16,0},{24,8},{1,17},{9,25},{17,1},{25,9},{2,18},{10... | collective-permute-start | bytes 393224 | tf_op jit(solution)/shard_map/ppermute | solution.py:287
  12.3 20.2 %collective-permute-start.12 = (bf16[2,8,32,128]{3,2,1,0:T(8,128)(2,1)S(1)}, bf16[2,8,32,128]{3,2,1,0:T(8,128)(2,1)S(1)}, u32[]{:S(2)}, u32[]{:S(2)}) collective-permute-start(bf16[2,8,32,128]{3,2,1,0:T(8,128)(2,1)S(1)} %shard_map.56.own_ref), channel_id=1, source_target_pairs={{0,16},{8,24},{16,0},{24,8},{1,17},{9,25},{17,1},{25,9},{2,18},{10... | collective-permute-start | bytes 393224 | tf_op jit(solution)/shard_map/ppermute | solution.py:287
  13.0 22.1 %collective-permute-start.4 = (bf16[2,8,32,128]{3,2,1,0:T(8,128)(2,1)S(1)}, bf16[2,8,32,128]{3,2,1,0:T(8,128)(2,1)S(1)}, u32[]{:S(2)}, u32[]{:S(2)}) collective-permute-start(bf16[2,8,32,128]{3,2,1,0:T(8,128)(2,1)S(1)} %shard_map.50.own_ref), channel_id=1, source_target_pairs={{0,16},{8,24},{16,0},{24,8},{1,17},{9,25},{17,1},{25,9},{2,18},{10... | collective-permute-start | bytes 393224 | tf_op jit(solution)/shard_map/ppermute | solution.py:287
  14.3 4.6 %copy-start.1 = (bf16[12,1,128,32,128]{4,3,2,1,0:T(8,128)(2,1)S(1)}, bf16[12,1,128,32,128]{4,3,2,1,0:T(8,128)(2,1)}, u32[]{:S(2)}) copy-start(bf16[12,1,128,32,128]{4,3,2,1,0:T(8,128)(2,1)} %param.5) | copy-start | bytes 37748740
  19.2 19.5 %collective-permute-start.1 = (bf16[2,8,32,128]{3,2,1,0:T(8,128)(2,1)S(1)}, bf16[2,8,32,128]{3,2,1,0:T(8,128)(2,1)S(1)}, u32[]{:S(2)}, u32[]{:S(2)}) collective-permute-start(bf16[2,8,32,128]{3,2,1,0:T(8,128)(2,1)S(1)} %shard_map.47.own_ref), channel_id=1, source_target_pairs={{0,16},{8,24},{16,0},{24,8},{1,17},{9,25},{17,1},{25,9},{2,18},{10... | collective-permute-start | bytes 393224 | tf_op jit(solution)/shard_map/ppermute | solution.py:287
  27.3 16.2 %collective-permute-start.10 = (bf16[8,32,128]{2,1,0:T(8,128)(2,1)S(1)}, bf16[8,32,128]{2,1,0:T(8,128)(2,1)S(1)}, u32[]{:S(2)}, u32[]{:S(2)}) collective-permute-start(bf16[8,32,128]{2,1,0:T(8,128)(2,1)S(1)} %get-tuple-element.22), channel_id=1, source_target_pairs={{0,5},{1,4},{2,7},{3,6},{4,1},{5,0},{6,3},{7,2},{8,13},{9,12},{10,... | collective-permute-start | bytes 196616 | tf_op jit(solution)/shard_map/ppermute | solution.py:287
  34.9 10.3 %collective-permute-start.13 = (bf16[8,32,128]{2,1,0:T(8,128)(2,1)S(1)}, bf16[8,32,128]{2,1,0:T(8,128)(2,1)S(1)}, u32[]{:S(2)}, u32[]{:S(2)}) collective-permute-start(bf16[8,32,128]{2,1,0:T(8,128)(2,1)S(1)} %get-tuple-element.23), channel_id=1, source_target_pairs={{0,6},{1,7},{2,4},{3,5},{4,2},{5,3},{6,0},{7,1},{8,14},{9,15},{10,... | collective-permute-start | bytes 196616 | tf_op jit(solution)/shard_map/ppermute | solution.py:287
  35.0 10.6 %collective-permute-start.14 = (bf16[8,32,128]{2,1,0:T(8,128)(2,1)S(1)}, bf16[8,32,128]{2,1,0:T(8,128)(2,1)S(1)}, u32[]{:S(2)}, u32[]{:S(2)}) collective-permute-start(bf16[8,32,128]{2,1,0:T(8,128)(2,1)S(1)} %get-tuple-element.24), channel_id=1, source_target_pairs={{0,7},{1,6},{2,5},{3,4},{4,3},{5,2},{6,1},{7,0},{8,15},{9,14},{10,... | collective-permute-start | bytes 196616 | tf_op jit(solution)/shard_map/ppermute | solution.py:287
  37.4 8.1 %collective-permute-start.5 = (bf16[8,32,128]{2,1,0:T(8,128)(2,1)S(1)}, bf16[8,32,128]{2,1,0:T(8,128)(2,1)S(1)}, u32[]{:S(2)}, u32[]{:S(2)}) collective-permute-start(bf16[8,32,128]{2,1,0:T(8,128)(2,1)S(1)} %get-tuple-element.19), channel_id=1, source_target_pairs={{0,2},{1,3},{2,0},{3,1},{4,6},{5,7},{6,4},{7,5},{8,10},{9,11},{10,... | collective-permute-start | bytes 196616 | tf_op jit(solution)/shard_map/ppermute | solution.py:287
  38.7 6.9 %collective-permute-start.6 = (bf16[8,32,128]{2,1,0:T(8,128)(2,1)S(1)}, bf16[8,32,128]{2,1,0:T(8,128)(2,1)S(1)}, u32[]{:S(2)}, u32[]{:S(2)}) collective-permute-start(bf16[8,32,128]{2,1,0:T(8,128)(2,1)S(1)} %get-tuple-element.20), channel_id=1, source_target_pairs={{0,3},{1,2},{2,1},{3,0},{4,7},{5,6},{6,5},{7,4},{8,11},{9,10},{10,... | collective-permute-start | bytes 196616 | tf_op jit(solution)/shard_map/ppermute | solution.py:287
  43.6 4.7 %collective-permute-start.9 = (bf16[8,32,128]{2,1,0:T(8,128)(2,1)S(1)}, bf16[8,32,128]{2,1,0:T(8,128)(2,1)S(1)}, u32[]{:S(2)}, u32[]{:S(2)}) collective-permute-start(bf16[8,32,128]{2,1,0:T(8,128)(2,1)S(1)} %get-tuple-element.21), channel_id=1, source_target_pairs={{0,4},{1,5},{2,6},{3,7},{4,0},{5,1},{6,2},{7,3},{8,12},{9,13},{10,... | collective-permute-start | bytes 196616 | tf_op jit(solution)/shard_map/ppermute | solution.py:287
  45.2 3.1 %collective-permute-start.2 = (bf16[8,32,128]{2,1,0:T(8,128)(2,1)S(1)}, bf16[8,32,128]{2,1,0:T(8,128)(2,1)S(1)}, u32[]{:S(2)}, u32[]{:S(2)}) collective-permute-start(bf16[8,32,128]{2,1,0:T(8,128)(2,1)S(1)} %get-tuple-element.18), channel_id=1, source_target_pairs={{0,1},{1,0},{2,3},{3,2},{4,5},{5,4},{6,7},{7,6},{8,9},{9,8},{10,11... | collective-permute-start | bytes 196616 | tf_op jit(solution)/shard_map/ppermute | solution.py:287
  54.3 1.9 %collective-permute-start.15 = (bf16[2,8,32,128]{3,2,1,0:T(8,128)(2,1)S(1)}, bf16[2,8,32,128]{3,2,1,0:T(8,128)(2,1)S(1)}, u32[]{:S(2)}, u32[]{:S(2)}) collective-permute-start(bf16[2,8,32,128]{3,2,1,0:T(8,128)(2,1)S(1)} %get-tuple-element.25.own_ref), channel_id=1, source_target_pairs={{0,1},{1,0},{2,3},{3,2},{4,5},{5,4},{6,7},{7,6},{8,9},{9,8},{10,11... | collective-permute-start | bytes 393224 | tf_op jit(solution)/shard_map/ppermute | solution.py:287
  55.3 3.0 %collective-permute-start.16 = (bf16[2,8,32,128]{3,2,1,0:T(8,128)(2,1)S(1)}, bf16[2,8,32,128]{3,2,1,0:T(8,128)(2,1)S(1)}, u32[]{:S(2)}, u32[]{:S(2)}) collective-permute-start(bf16[2,8,32,128]{3,2,1,0:T(8,128)(2,1)S(1)} %get-tuple-element.26.own_ref), channel_id=1, source_target_pairs={{0,1},{1,0},{2,3},{3,2},{4,5},{5,4},{6,7},{7,6},{8,9},{9,8},{10,11... | collective-permute-start | bytes 393224 | tf_op jit(solution)/shard_map/ppermute | solution.py:287
  55.3 3.3 %collective-permute-start.18 = (bf16[2,8,32,128]{3,2,1,0:T(8,128)(2,1)S(1)}, bf16[2,8,32,128]{3,2,1,0:T(8,128)(2,1)S(1)}, u32[]{:S(2)}, u32[]{:S(2)}) collective-permute-start(bf16[2,8,32,128]{3,2,1,0:T(8,128)(2,1)S(1)} %get-tuple-element.27.own_ref), channel_id=1, source_target_pairs={{0,1},{1,0},{2,3},{3,2},{4,5},{5,4},{6,7},{7,6},{8,9},{9,8},{10,11... | collective-permute-start | bytes 393224 | tf_op jit(solution)/shard_map/ppermute | solution.py:287
  55.8 4.8 %collective-permute-start.19 = (bf16[2,8,32,128]{3,2,1,0:T(8,128)(2,1)S(1)}, bf16[2,8,32,128]{3,2,1,0:T(8,128)(2,1)S(1)}, u32[]{:S(2)}, u32[]{:S(2)}) collective-permute-start(bf16[2,8,32,128]{3,2,1,0:T(8,128)(2,1)S(1)} %get-tuple-element.28.own_ref), channel_id=1, source_target_pairs={{0,1},{1,0},{2,3},{3,2},{4,5},{5,4},{6,7},{7,6},{8,9},{9,8},{10,11... | collective-permute-start | bytes 393224 | tf_op jit(solution)/shard_map/ppermute | solution.py:287
  56.6 5.0 %collective-permute-start.24 = (bf16[2,8,32,128]{3,2,1,0:T(8,128)(2,1)S(1)}, bf16[2,8,32,128]{3,2,1,0:T(8,128)(2,1)S(1)}, u32[]{:S(2)}, u32[]{:S(2)}) collective-permute-start(bf16[2,8,32,128]{3,2,1,0:T(8,128)(2,1)S(1)} %shard_map.59.own_ref), channel_id=1, source_target_pairs={{0,2},{1,3},{2,0},{3,1},{4,6},{5,7},{6,4},{7,5},{8,10},{9,11},{10,... | collective-permute-start | bytes 393224 | tf_op jit(solution)/shard_map/ppermute | solution.py:287
  58.6 5.9 %collective-permute-start.17 = (bf16[2,8,32,128]{3,2,1,0:T(8,128)(2,1)S(1)}, bf16[2,8,32,128]{3,2,1,0:T(8,128)(2,1)S(1)}, u32[]{:S(2)}, u32[]{:S(2)}) collective-permute-start(bf16[2,8,32,128]{3,2,1,0:T(8,128)(2,1)S(1)} %shard_map.60.own_ref), channel_id=1, source_target_pairs={{0,2},{1,3},{2,0},{3,1},{4,6},{5,7},{6,4},{7,5},{8,10},{9,11},{10,... | collective-permute-start | bytes 393224 | tf_op jit(solution)/shard_map/ppermute | solution.py:287
  59.0 12.7 %collective-permute-start.25 = (bf16[2,8,32,128]{3,2,1,0:T(8,128)(2,1)S(1)}, bf16[2,8,32,128]{3,2,1,0:T(8,128)(2,1)S(1)}, u32[]{:S(2)}, u32[]{:S(2)}) collective-permute-start(bf16[2,8,32,128]{3,2,1,0:T(8,128)(2,1)S(1)} %shard_map.62.own_ref), channel_id=1, source_target_pairs={{0,2},{1,3},{2,0},{3,1},{4,6},{5,7},{6,4},{7,5},{8,10},{9,11},{10,... | collective-permute-start | bytes 393224 | tf_op jit(solution)/shard_map/ppermute | solution.py:287
  60.9 13.8 %collective-permute-start.20 = (bf16[2,8,32,128]{3,2,1,0:T(8,128)(2,1)S(1)}, bf16[2,8,32,128]{3,2,1,0:T(8,128)(2,1)S(1)}, u32[]{:S(2)}, u32[]{:S(2)}) collective-permute-start(bf16[2,8,32,128]{3,2,1,0:T(8,128)(2,1)S(1)} %shard_map.63.own_ref), channel_id=1, source_target_pairs={{0,2},{1,3},{2,0},{3,1},{4,6},{5,7},{6,4},{7,5},{8,10},{9,11},{10,... | collective-permute-start | bytes 393224 | tf_op jit(solution)/shard_map/ppermute | solution.py:287
  62.0 44.0 %collective-permute-start.28 = (bf16[2,8,32,128]{3,2,1,0:T(8,128)(2,1)S(1)}, bf16[2,8,32,128]{3,2,1,0:T(8,128)(2,1)S(1)}, u32[]{:S(2)}, u32[]{:S(2)}) collective-permute-start(bf16[2,8,32,128]{3,2,1,0:T(8,128)(2,1)S(1)} %shard_map.66.own_ref), channel_id=1, source_target_pairs={{0,4},{1,5},{2,6},{3,7},{4,0},{5,1},{6,2},{7,3},{8,12},{9,13},{10,... | collective-permute-start | bytes 393224 | tf_op jit(solution)/shard_map/ppermute | solution.py:287
  64.8 24.9 %copy-start.6 = (s32[1,128,8]{1,2,0:T(8,128)S(1)}, s32[1,128,8]{1,2,0:T(8,128)}, u32[]{:S(2)}) copy-start(s32[1,128,8]{1,2,0:T(8,128)} %param.7) | copy-start | bytes 12292
  64.8 47.0 %collective-permute-start.27 = (bf16[2,8,32,128]{3,2,1,0:T(8,128)(2,1)S(1)}, bf16[2,8,32,128]{3,2,1,0:T(8,128)(2,1)S(1)}, u32[]{:S(2)}, u32[]{:S(2)}) collective-permute-start(bf16[2,8,32,128]{3,2,1,0:T(8,128)(2,1)S(1)} %shard_map.61.own_ref), channel_id=1, source_target_pairs={{0,4},{1,5},{2,6},{3,7},{4,0},{5,1},{6,2},{7,3},{8,12},{9,13},{10,... | collective-permute-start | bytes 393224 | tf_op jit(solution)/shard_map/ppermute | solution.py:287
  72.1 40.9 %collective-permute-start.26 = (bf16[2,8,32,128]{3,2,1,0:T(8,128)(2,1)S(1)}, bf16[2,8,32,128]{3,2,1,0:T(8,128)(2,1)S(1)}, u32[]{:S(2)}, u32[]{:S(2)}) collective-permute-start(bf16[2,8,32,128]{3,2,1,0:T(8,128)(2,1)S(1)} %shard_map.67.own_ref), channel_id=1, source_target_pairs={{0,4},{1,5},{2,6},{3,7},{4,0},{5,1},{6,2},{7,3},{8,12},{9,13},{10,... | collective-permute-start | bytes 393224 | tf_op jit(solution)/shard_map/ppermute | solution.py:287
  75.0 39.2 %collective-permute-start.21 = (bf16[2,8,32,128]{3,2,1,0:T(8,128)(2,1)S(1)}, bf16[2,8,32,128]{3,2,1,0:T(8,128)(2,1)S(1)}, u32[]{:S(2)}, u32[]{:S(2)}) collective-permute-start(bf16[2,8,32,128]{3,2,1,0:T(8,128)(2,1)S(1)} %shard_map.64.own_ref), channel_id=1, source_target_pairs={{0,4},{1,5},{2,6},{3,7},{4,0},{5,1},{6,2},{7,3},{8,12},{9,13},{10,... | collective-permute-start | bytes 393224 | tf_op jit(solution)/shard_map/ppermute | solution.py:287
  77.6 10.2 %collective-permute-start.22 = (bf16[2,32,128]{2,1,0:T(8,128)(2,1)S(1)}, bf16[2,32,128]{2,1,0:T(8,128)(2,1)S(1)}, u32[]{:S(2)}, u32[]{:S(2)}) collective-permute-start(bf16[2,32,128]{2,1,0:T(8,128)(2,1)S(1)} %reshape.21), channel_id=1, source_target_pairs={{0,1},{1,2},{2,3},{3,4},{4,5},{5,6},{6,7},{8,9},{9,10},{10,11},{11... | collective-permute-start | bytes 49160 | tf_op jit(solution)/shard_map/ppermute | solution.py:373
  87.8 5.8 %collective-permute-start.23 = (bf16[2,32,128]{2,1,0:T(8,128)(2,1)S(1)}, bf16[2,32,128]{2,1,0:T(8,128)(2,1)S(1)}, u32[]{:S(2)}, u32[]{:S(2)}) collective-permute-start(bf16[2,32,128]{2,1,0:T(8,128)(2,1)S(1)} %reshape.23), channel_id=1, source_target_pairs={{1,0},{2,1},{3,2},{4,3},{5,4},{6,5},{7,6},{9,8},{10,9},{11,10},{12... | collective-permute-start | bytes 49160 | tf_op jit(solution)/shard_map/ppermute | solution.py:374
  106.0 4.6 %copy-start.3 = (bf16[12,1,128,32,128]{4,3,2,1,0:T(8,128)(2,1)S(1)}, bf16[12,1,128,32,128]{4,3,2,1,0:T(8,128)(2,1)}, u32[]{:S(2)}) copy-start(bf16[12,1,128,32,128]{4,3,2,1,0:T(8,128)(2,1)} %param.5) | copy-start | bytes 37748740
  (4 other events, 12.4 us)

commit v2 on v1

--- a/solution.py
+++ b/solution.py
@@ -10,7 +10,8 @@
 HW = 4
 BF = jnp.bfloat16
 F32 = jnp.float32
-VMEM_LIMIT = 40 * 1024 * 1024
+CONV_US = 2.5
+VMEM_LIMIT = 16 * 1024 * 1024
 
 
 def lane_of(x):
@@ -36,7 +37,7 @@
 
 
 def with_turn(x):
-    return x, times_i(x.astype(F32)).astype(BF)
+    return x, times_i(x)
 
 
 def mix(own, own_i, other, other_i, weights):
@@ -48,7 +49,7 @@
 
 
 def take_weights(w_ref, group, m, lows):
-    w = w_ref[0, pl.ds(group * lows + 2 * m, 2)]
+    w = w_ref[pl.ds(group * lows + 2 * m, 2)]
     return w.reshape(2 * w.shape[1], w.shape[2])
 
 
@@ -56,10 +57,8 @@
     return pltpu.CompilerParams(vmem_limit_bytes=VMEM_LIMIT)
 
 
-def cost(blocks):
-    return pl.CostEstimate(
-        flops=blocks * 2 * 64 * 128 * 64, bytes_accessed=blocks * 16384, transcendentals=0
-    )
+def cost(us):
+    return pl.CostEstimate(flops=0, bytes_accessed=int(us * 3.6e6), transcendentals=0)
 
 
 def full(shape):
@@ -67,14 +66,14 @@
     return pl.BlockSpec(shape, lambda i, t: zeros)
 
 
-def chunk_weights(factors, level, r, groups_in, lows):
-    _, _, rows, cols = factors.shape
+def chunk_weights(weights, level, r, groups_in, lows):
+    _, _, rows, cols = weights.shape
     return pl.BlockSpec(
-        (1, groups_in * lows, rows, cols), lambda i, t: (level, (t[0] // groups_in) ^ r, 0, 0)
+        (None, groups_in * lows, rows, cols), lambda i, t: (level, (t[0] // groups_in) ^ r, 0, 0)
     )
 
 
-def call(kernel, tgt_index, arrays, in_specs, out_shapes, out_specs, scratch, blocks, aliases=None):
+def call(kernel, tgt_index, arrays, in_specs, out_shapes, out_specs, scratch, us, aliases=None):
     return pl.pallas_call(
         kernel,
         out_shape=out_shapes,
@@ -86,7 +85,7 @@
             scratch_shapes=scratch,
         ),
         compiler_params=params(),
-        cost_estimate=cost(blocks),
+        cost_estimate=cost(us),
         input_output_aliases=aliases or {},
     )(tgt_index, *arrays)
 
@@ -111,6 +110,38 @@
     out_ref[...] = tall[...].astype(BF).reshape(out_ref.shape)
 
 
+def edge_kernel(rows, first_ref, last_ref, first_out, last_out, wide, tall):
+    pairs, rank, _ = first_out.shape
+    for ref, out, start in ((first_ref, first_out, 0), (last_ref, last_out, rows - HW)):
+        for j in range(rank // 2):
+            wide[j] = ref[:, pl.ds(j * 128, 128)].astype(F32)
+        for j in range(rank // 2):
+            even = wide[j, pl.ds(start, pairs, stride=2), :]
+            odd = wide[j, pl.ds(start + 1, pairs, stride=2), :]
+            low = lane_of(even) < 64
+            tall[pl.ds(2 * j, pairs, stride=rank), :] = jnp.where(low, even, half_swap(odd))
+            tall[pl.ds(2 * j + 1, pairs, stride=rank), :] = jnp.where(low, half_swap(even), odd)
+        out[...] = tall[...].astype(BF).reshape(out.shape)
+
+
+def edge_pairs(incident, rank):
+    blocks, width = incident.shape
+    rows, pairs = 16, HW // 2
+    shape = jax.ShapeDtypeStruct((pairs, rank, 128), BF)
+    return pl.pallas_call(
+        functools.partial(edge_kernel, rows),
+        grid=(1,),
+        in_specs=[
+            pl.BlockSpec((rows, width), lambda i: (0, 0)),
+            pl.BlockSpec((rows, width), lambda i: (blocks // rows - 1, 0)),
+        ],
+        out_specs=[pl.BlockSpec(shape.shape, lambda i: (0, 0, 0))] * 2,
+        out_shape=[shape] * 2,
+        scratch_shapes=[pltpu.VMEM((rank // 2, rows, 128), F32), pltpu.VMEM((pairs * rank, 128), F32)],
+        compiler_params=params(),
+    )(incident, incident)
+
+
 def level_kernel(G, lows, flip, t, own_ref, other_ref, w_ref, out_ref):
     half = lows // 2
     for b in range(G):
@@ -127,31 +158,26 @@
     w_refs = rest[: 1 + low_bits]
     out_refs = rest[1 + low_bits : 1 + low_bits + G]
     half = lows // 2
-    for b in range(G):
-        group = (t[0] % G) ^ b
-        values = []
-        for m in range(half):
-            own, own_i = with_turn(own_ref[b, m])
-            other, other_i = with_turn(other_ref[b, m])
-            values.append(
-                mix(own, own_i, other, other_i, take_weights(w_refs[0], group, m, lows))
-            )
-        for bit in range(low_bits):
-            pairs = [(x.astype(BF), times_i(x).astype(BF)) for x in values]
-            new = []
-            for m in range(half):
-                own, own_i = pairs[m]
-                if bit == 0:
-                    other32 = half_swap(own.astype(F32))
-                    other, other_i = other32.astype(BF), times_i(other32).astype(BF)
-                else:
-                    other, other_i = pairs[m ^ (1 << (bit - 1))]
-                new.append(
-                    mix(own, own_i, other, other_i, take_weights(w_refs[1 + bit], group, m, lows))
-                )
-            values = new
-        for m in range(half):
-            out_refs[b][m] = values[m].astype(BF)
+    keys = [(b, m) for b in range(G) for m in range(half)]
+    groups = [(t[0] % G) ^ b for b in range(G)]
+    pairs = {key: with_turn(own_ref[key]) for key in keys}
+    others = {key: with_turn(other_ref[key]) for key in keys}
+    for bit in range(-1, low_bits):
+        if bit == 0:
+            others = {key: with_turn(half_swap(pairs[key][0])) for key in keys}
+        elif bit > 0:
+            others = {(b, m): pairs[b, m ^ (1 << (bit - 1))] for b, m in keys}
+        values = {
+            (b, m): mix(
+                *pairs[b, m],
+                *others[b, m],
+                take_weights(w_refs[1 + bit], groups[b], m, lows),
+            ).astype(BF)
+            for b, m in keys
+        }
+        pairs = {key: with_turn(x) for key, x in values.items()} if bit < low_bits - 1 else values
+    for b, m in keys:
+        out_refs[b][m] = pairs[b, m]
 
 
 def group_kernel(G, lows, groups, t, *refs):
@@ -161,28 +187,28 @@
     outs = refs[groups + bits : groups + bits + groups // G]
     half = lows // 2
 
-    def one(m):
+    width = max(1, min(half, 32 // groups))
+    keys = [(k, g) for k in range(width) for g in range(groups)]
+
+    def body(step, carry):
         values = None
-        pairs = [with_turn(ins[g][m]) for g in range(groups)]
+        pairs = {(k, g): with_turn(ins[g][step * width + k]) for k, g in keys}
         for bit in range(bits):
-            values = [
-                mix(
-                    *pairs[g],
-                    *pairs[g ^ (1 << bit)],
-                    take_weights(w_refs[bit], t[0] ^ g, m, lows),
+            values = {
+                (k, g): mix(
+                    *pairs[k, g],
+                    *pairs[k, g ^ (1 << bit)],
+                    take_weights(w_refs[bit], t[0] ^ g, step * width + k, lows),
                 )
-                for g in range(groups)
-            ]
+                for k, g in keys
+            }
             if bit < bits - 1:
-                pairs = [(x.astype(BF), times_i(x).astype(BF)) for x in values]
-        for g in range(groups):
-            outs[g // G][g % G, m] = values[g].astype(BF)
-
-    def body(m, carry):
-        one(m)
+                pairs = {key: with_turn(x.astype(BF)) for key, x in values.items()}
+        for k, g in keys:
+            outs[g // G][g % G, step * width + k] = values[k, g].astype(BF)
         return carry
 
-    lax.fori_loop(0, half, body, 0)
+    lax.fori_loop(0, half // width, body, 0)
 
 
 def final_kernel(G, lows, flip, t, own_ref, other_ref, w_ref, near_ref, *rest):
@@ -220,24 +246,38 @@
     half = lows // 2
     rank = v_refs[0].shape[2]
 
-    def put(place, x):
-        wide = x.astype(F32)
-        low = lane_of(wide) < 64
-        swapped = half_swap(wide)
-        for side, dup in enumerate((jnp.where(low, wide, swapped), jnp.where(low, swapped, wide))):
-            window[place + side, 0:rank, :] = dup.astype(BF)
-            window[place + side, rank : 2 * rank, :] = times_i(dup).astype(BF)
+    row = lax.broadcasted_iota(jnp.int32, (128, 512), 0)
+    col = lax.broadcasted_iota(jnp.int32, (128, 512), 1)
+    turned = (col // 128) % 2 == 1
+    low = col % 64 < 32
+    lane = col % 64 + jnp.where(turned, jnp.where(low, 32, -32), 0)
+    sign = jnp.where(turned & low, -1.0, 1.0)
+    spread = jnp.where(row == col // 256 * 64 + lane, sign, 0.0).astype(BF)
+
+    def put(places, x):
+        wide = lax.dot_general(
+            x.reshape(len(places) * rank, 128),
+            spread,
+            (((1,), (0,)), ((), ())),
+            preferred_element_type=F32,
+        ).astype(BF)
+        for e, place in enumerate(places):
+            for side in range(2):
+                for turn in range(2):
+                    first = 256 * side + 128 * turn
+                    window[place + side, rank * turn : rank * (turn + 1), :] = wide[
+                        e * rank : (e + 1) * rank, first : first + 128
+                    ]
 
     @pl.when(pl.program_id(0) == 0)
     def _():
-        for e in range(HW // 2):
-            put(2 * e, below_ref[e])
-            put(HW + G * chunks * lows + 2 * e, above_ref[e])
+        put([2 * e for e in range(HW // 2)], below_ref[...])
+        after = HW + G * chunks * lows
+        put([after + 2 * e for e in range(HW // 2)], above_ref[...])
         for r in range(chunks):
             for b in range(G):
                 group = t[0] ^ (r * G + b)
-                for m in range(half):
-                    put(HW + group * lows + 2 * m, v_refs[r][b, m])
+                put([HW + group * lows + 2 * m for m in range(half)], v_refs[r][b])
 
     base = pl.program_id(0) * count
     last = None
@@ -256,7 +296,7 @@
 def near_field(tgt_index, lists, mats, chunks, below, above, G, lows):
     blocks, rank, cols = mats.shape
     near_count = lists.shape[1]
-    count = 16
+    count = 32
     v_shape = chunks[0].shape
 
     def spec(shape):
@@ -276,9 +316,7 @@
             scratch_shapes=[pltpu.VMEM((blocks + 2 * HW, 2 * rank, 128), BF)],
         ),
         compiler_params=params(),
-        cost_estimate=pl.CostEstimate(
-            flops=2 * blocks * rank * cols * 128, bytes_accessed=mats.size * 2, transcendentals=0
-        ),
+        cost_estimate=cost(6.0),
     )(tgt_index, lists, *chunks, below, above, mats)
 
 
@@ -301,6 +339,11 @@
     order = list(range(chunks))[::-1]
     tgt_index = lax.axis_index("tgt").astype(jnp.int32).reshape(1)
     weights = factors[:, 0]
+    ends = {0: factors[:1, 0], factors.shape[0] - 1: factors[-1:, 0]}
+
+    def level_weights(level):
+        return (ends[level], 0) if level in ends else (weights, level)
+
     chunk_shape = (G, half, rank, 128)
     chunk_out = jax.ShapeDtypeStruct(chunk_shape, BF)
     group_out = jax.ShapeDtypeStruct(chunk_shape[1:], BF)
@@ -312,17 +355,23 @@
         return chunk_weights(weights, level, r, G, lows)
 
     def level_call(level, r, own, other, flip=0):
+        array, level = level_weights(level)
         return call(
             functools.partial(level_kernel, G, lows, flip),
             tgt_index,
-            (own, other, weights),
+            (own, other, array),
             [full(chunk_shape), full(chunk_shape), wspec(level, r)],
             chunk_out,
             full(chunk_shape),
             [],
-            G * lows,
+            0.4,
         )
 
+    ups = [(i, i + 1) for i in range(groups - 1)]
+    downs = [(i + 1, i) for i in range(groups - 1)]
+    first, last = edge_pairs(incident[0], rank)
+    below = lax.ppermute(last, "tgt", ups)
+    above = lax.ppermute(first, "tgt", downs)
     width = incident.shape[2]
     v = [None] * chunks
     for r in order:
@@ -337,14 +386,17 @@
                 pltpu.VMEM((rank // 2, G * lows, 128), F32),
                 pltpu.VMEM((G * half * rank, 128), F32),
             ],
-            G * lows,
+            CONV_US,
         )
     start = list(v)
 
     level = 0
     for bit in range(src_bits - 1):
-        for r in order:
-            v[r] = level_call(level, r, v[r], swapped_with(v[r], "src", 1 << bit))
+        others = [swapped_with(v[r], "src", 1 << bit) for r in order]
+        if bit == 0:
+            others[-1], below, above = lax.optimization_barrier((others[-1], below, above))
+        for r, other in zip(order, others):
+            v[r] = level_call(level, r, v[r], other)
         level += 1
     arrived = [None] * groups
     for r in order:
@@ -358,20 +410,13 @@
             [group_out] * G,
             [full(chunk_shape[1:])] * G,
             [],
-            (1 + low_bits) * G * lows,
+            1.5,
         )
         for b in range(G):
             g = r * G + b
             arrived[g] = swapped_with(parts[b], "tgt", g) if g else parts[b]
     level += 1 + low_bits
 
-    edge = HW // 2
-    ups = [(i, i + 1) for i in range(groups - 1)]
-    downs = [(i + 1, i) for i in range(groups - 1)]
-    rows_in = incident[0]
-    first, last = edge_pairs(rows_in, rank)
-    below = lax.ppermute(last, "tgt", ups)
-    above = lax.ppermute(first, "tgt", downs)
     near = near_field(tgt_index, near_lists[0], near_blocks[0], start, below, above, G, lows)
 
     v = call(
@@ -380,13 +425,15 @@
         tuple(arrived) + (weights,) * tgt_bits,
         [full(chunk_shape[1:])] * groups
         + [
-            pl.BlockSpec((1, blocks, rank, 128), functools.partial(lambda l, i, t: (l, 0, 0, 0), level + k))
+            pl.BlockSpec(
+                (None, blocks, rank, 128), functools.partial(lambda l, i, t: (l, 0, 0, 0), level + k)
+            )
             for k in range(tgt_bits)
         ],
         [chunk_out] * chunks,
         [full(chunk_shape)] * chunks,
         [],
-        tgt_bits * blocks,
+        2.5,
     )
     v = list(v)
     level += tgt_bits
@@ -400,11 +447,11 @@
     others = [swapped_with(v[r ^ (distance // G)], "tgt", distance) for r in range(chunks)]
     for r in range(chunks):
         partner = others[r]
-        arrays = (v[r], partner, weights, near)
+        arrays = (v[r], partner, level_weights(level)[0], near)
         specs = [
             full(chunk_shape),
             full(chunk_shape),
-            wspec(level, r),
+            wspec(level_weights(level)[1], r),
             pl.BlockSpec(
                 (G * half, rank, 128), functools.partial(lambda r, i, t: ((t[0] // G) ^ r, 0, 0), r)
             ),
@@ -425,18 +472,10 @@
                 pltpu.VMEM((G * half * rank, 128), F32),
                 pltpu.VMEM((rank // 2, G * lows, 128), F32),
             ],
-            G * lows,
+            1.2,
             aliases,
         )
     return out[None]
-
-
-def edge_pairs(rows_in, rank):
-    def pairs(x):
-        x = x.reshape(HW // 2, 2, rank, -1)
-        return jnp.swapaxes(x, 1, 2).reshape(HW // 2, rank, -1)
-
-    return pairs(rows_in[:HW]), pairs(rows_in[-HW:])
 
 
 def solution(mesh):

time: 116 us -> 79.4 us (0.68)
  the two profiles are of different devices: /device:TPU:9 before, /device:TPU:0 now
where the time goes in v2:
time: 79.4 us; the launch traced here: 79.1 us
  starting transfers between devices  31.7 us (40%)
  Pallas kernels  23.2 us (29%)
  waiting for transfers between devices  17.5 us (22%)
  local copies, waits for them, and re-layouts  6.43 us (8%)
    ppermute x27, starting transfers between devices, swapped_with(): return lax.ppermute(x, axis, [(i, i ^ distance) for i in range(count)])  29.1 us
    pallas_call x25, Pallas kernels, call(): pl.pallas_call(kernel, out_shape=out_shapes, grid_spec=pltpu.PrefetchScal...  17.6 us
    ppermute x27, waiting for transfers between devices, swapped_with(): return lax.ppermute(x, axis, [(i, i ^ distance) for i in range(count)])  16.8 us
    pallas_call x1, Pallas kernels, near_field(): pl.pallas_call(functools.partial(near_kernel, G, lows, len(chunks), count...  5.5 us
    unnamed x11, local copies, waits for them, and re-layouts  4.53 us
    squeeze x1, local copies, waits for them, and re-layouts, per_device(): ends = {0: factors[:1, 0], factors.shape[0] - 1: factors[-1:, 0]}  1.9 us
  transfers between devices with their start and end apart: 29, of which 12 were waited for; matrix products, arithmetic and copies ran while one was open for 3% of the time, Pallas kernels for 25%

profile of v2, /device:TPU:0, one launch (start us, length us, event | category | flops | bytes accessed | tf_op | source)
XLA Modules:
  0.0 79.1 jit_solution(3689604183147358702)
XLA Ops:
  0.0 1.2 %copy-done.1 = bf16[1,128,2048]{2,1,0:T(8,128)(2,1)S(1)} copy-done((bf16[1,128,2048]{2,1,0:T(8,128)(2,1)S(1)}, bf16[1,128,2048]{2,1,0:T(8,128)(2,1)}, u32[]{:S(2)}) %copy-start.1) | copy-done | bytes 524312
  1.5 3.0 %collective-permute-start.13 = (bf16[2,8,32,128]{3,2,1,0:T(8,128)(2,1)S(1)}, bf16[2,8,32,128]{3,2,1,0:T(8,128)(2,1)S(1)}, u32[]{:S(2)}, u32[]{:S(2)}) collective-permute-start(bf16[2,8,32,128]{3,2,1,0:T(8,128)(2,1)S(1)} %shard_map.56.own_ref.refs_3_), channel_id=1, source_target_pairs={{0,8},{8,0},{16,24},{24,16},{1,9},{9,1},{17,25},{25,17},{2,10},{10... | collective-permute-start | bytes 393224 | tf_op jit(solution)/shard_map/ppermute | solution.py:325
  5.1 2.1 %collective-permute-start.5 = (bf16[2,8,32,128]{3,2,1,0:T(8,128)(2,1)S(1)}, bf16[2,8,32,128]{3,2,1,0:T(8,128)(2,1)S(1)}, u32[]{:S(2)}, u32[]{:S(2)}) collective-permute-start(bf16[2,8,32,128]{3,2,1,0:T(8,128)(2,1)S(1)} %shard_map.50.own_ref.refs_1_), channel_id=1, source_target_pairs={{0,8},{8,0},{16,24},{24,16},{1,9},{9,1},{17,25},{25,17},{2,10},{10... | collective-permute-start | bytes 393224 | tf_op jit(solution)/shard_map/ppermute | solution.py:325
  7.5 1.9 %slice_bitcast_fusion = (bf16[1,128,32,128]{3,2,1,0:T(8,128)(2,1)S(1)}, bf16[1,128,32,128]{3,2,1,0:T(8,128)(2,1)S(1)}) fusion(bf16[12,1,128,32,128]{4,3,2,1,0:T(8,128)(2,1)} %param.5), kind=kLoop, calls=%fused_computation | loop fusion | bytes 4194304 | tf_op jit(solution)/shard_map/squeeze | solution.py:342
  9.7 2.1 %collective-permute-start.14 = (bf16[2,8,32,128]{3,2,1,0:T(8,128)(2,1)S(1)}, bf16[2,8,32,128]{3,2,1,0:T(8,128)(2,1)S(1)}, u32[]{:S(2)}, u32[]{:S(2)}) collective-permute-start(bf16[2,8,32,128]{3,2,1,0:T(8,128)(2,1)S(1)} %shard_map.57.own_ref), channel_id=1, source_target_pairs={{0,16},{8,24},{16,0},{24,8},{1,17},{9,25},{17,1},{25,9},{2,18},{10... | collective-permute-start | bytes 393224 | tf_op jit(solution)/shard_map/ppermute | solution.py:325
  13.0 1.3 %collective-permute-start.1 = (bf16[2,32,128]{2,1,0:T(8,128)(2,1)S(1)}, bf16[2,32,128]{2,1,0:T(8,128)(2,1)S(1)}, u32[]{:S(2)}, u32[]{:S(2)}) collective-permute-start(bf16[2,32,128]{2,1,0:T(8,128)(2,1)S(1)} %get-tuple-element.22), channel_id=1, source_target_pairs={{0,1},{1,2},{2,3},{3,4},{4,5},{5,6},{6,7},{8,9},{9,10},{10,11},{11... | collective-permute-start | bytes 49160 | tf_op jit(solution)/shard_map/ppermute | solution.py:373
  14.3 1.3 %collective-permute-start.2 = (bf16[2,32,128]{2,1,0:T(8,128)(2,1)S(1)}, bf16[2,32,128]{2,1,0:T(8,128)(2,1)S(1)}, u32[]{:S(2)}, u32[]{:S(2)}) collective-permute-start(bf16[2,32,128]{2,1,0:T(8,128)(2,1)S(1)} %get-tuple-element.23), channel_id=1, source_target_pairs={{1,0},{2,1},{3,2},{4,3},{5,4},{6,5},{7,6},{9,8},{10,9},{11,10},{12... | collective-permute-start | bytes 49160 | tf_op jit(solution)/shard_map/ppermute | solution.py:374
  16.8 1.6 %collective-permute-start.6 = (bf16[2,8,32,128]{3,2,1,0:T(8,128)(2,1)S(1)}, bf16[2,8,32,128]{3,2,1,0:T(8,128)(2,1)S(1)}, u32[]{:S(2)}, u32[]{:S(2)}) collective-permute-start(bf16[2,8,32,128]{3,2,1,0:T(8,128)(2,1)S(1)} %shard_map.51.own_ref), channel_id=1, source_target_pairs={{0,16},{8,24},{16,0},{24,8},{1,17},{9,25},{17,1},{25,9},{2,18},{10... | collective-permute-start | bytes 393224 | tf_op jit(solution)/shard_map/ppermute | solution.py:325
  20.1 1.4 %shard_map.58 = (bf16[8,32,128]{2,1,0:T(8,128)(2,1)S(1)}, bf16[8,32,128]{2,1,0:T(8,128)(2,1)S(1)}) custom-call(s32[1]{0:T(128)} %bitcast.t, bf16[2,8,32,128]{3,2,1,0:T(8,128)(2,1)S(1)} %shard_map.57.own_ref, bf16[2,8,32,128]{3,2,1,0:T(8,128)(2,1)S(1)} %collective-permute-done.14.other_ref, bf16[12,128,32,128]{3,2,1,0:T(8,128)(2,1)S(1)} %bitcast.10, ...), custom_call_target="tpu_custom_call" | custom-call | bytes 5400000 | tf_op jit(solution)/shard_map/pallas_call | solution.py:77
  21.5 5.9 %collective-permute-start.15 = (bf16[8,32,128]{2,1,0:T(8,128)(2,1)S(1)}, bf16[8,32,128]{2,1,0:T(8,128)(2,1)S(1)}, u32[]{:S(2)}, u32[]{:S(2)}) collective-permute-start(bf16[8,32,128]{2,1,0:T(8,128)(2,1)S(1)} %get-tuple-element.31), channel_id=1, source_target_pairs={{0,6},{1,7},{2,4},{3,5},{4,2},{5,3},{6,0},{7,1},{8,14},{9,15},{10,... | collective-permute-start | bytes 196616 | tf_op jit(solution)/shard_map/ppermute | solution.py:325
  27.5 1.4 %shard_map.55 = (bf16[8,32,128]{2,1,0:T(8,128)(2,1)S(1)}, bf16[8,32,128]{2,1,0:T(8,128)(2,1)S(1)}) custom-call(s32[1]{0:T(128)} %bitcast.t, bf16[2,8,32,128]{3,2,1,0:T(8,128)(2,1)S(1)} %shard_map.54.own_ref, bf16[2,8,32,128]{3,2,1,0:T(8,128)(2,1)S(1)} %collective-permute-done.10.other_ref, bf16[12,128,32,128]{3,2,1,0:T(8,128)(2,1)S(1)} %bitcast.15, ...), custom_call_target="tpu_custom_call" | custom-call | bytes 5400000 | tf_op jit(solution)/shard_map/pallas_call | solution.py:77
  29.5 2.0 %collective-permute-start.12 = (bf16[8,32,128]{2,1,0:T(8,128)(2,1)S(1)}, bf16[8,32,128]{2,1,0:T(8,128)(2,1)S(1)}, u32[]{:S(2)}, u32[]{:S(2)}) collective-permute-start(bf16[8,32,128]{2,1,0:T(8,128)(2,1)S(1)} %get-tuple-element.30), channel_id=1, source_target_pairs={{0,5},{1,4},{2,7},{3,6},{4,1},{5,0},{6,3},{7,2},{8,13},{9,12},{10,... | collective-permute-start | bytes 196616 | tf_op jit(solution)/shard_map/ppermute | solution.py:325
  31.4 1.4 %shard_map.52 = (bf16[8,32,128]{2,1,0:T(8,128)(2,1)S(1)}, bf16[8,32,128]{2,1,0:T(8,128)(2,1)S(1)}) custom-call(s32[1]{0:T(128)} %bitcast.t, bf16[2,8,32,128]{3,2,1,0:T(8,128)(2,1)S(1)} %shard_map.51.own_ref, bf16[2,8,32,128]{3,2,1,0:T(8,128)(2,1)S(1)} %collective-permute-done.6.other_ref, bf16[12,128,32,128]{3,2,1,0:T(8,128)(2,1)S(1)} %bitcast.24, ...), custom_call_target="tpu_custom_call" | custom-call | bytes 5400000 | tf_op jit(solution)/shard_map/pallas_call | solution.py:77
  32.8 1.8 %collective-permute-start.7 = (bf16[8,32,128]{2,1,0:T(8,128)(2,1)S(1)}, bf16[8,32,128]{2,1,0:T(8,128)(2,1)S(1)}, u32[]{:S(2)}, u32[]{:S(2)}) collective-permute-start(bf16[8,32,128]{2,1,0:T(8,128)(2,1)S(1)} %get-tuple-element.27), channel_id=1, source_target_pairs={{0,2},{1,3},{2,0},{3,1},{4,6},{5,7},{6,4},{7,5},{8,10},{9,11},{10,... | collective-permute-start | bytes 196616 | tf_op jit(solution)/shard_map/ppermute | solution.py:325
  34.7 1.4 %shard_map.49 = (bf16[8,32,128]{2,1,0:T(8,128)(2,1)S(1)}, bf16[8,32,128]{2,1,0:T(8,128)(2,1)S(1)}) custom-call(s32[1]{0:T(128)} %bitcast.t, bf16[2,8,32,128]{3,2,1,0:T(8,128)(2,1)S(1)} %shard_map.48.own_ref, bf16[2,8,32,128]{3,2,1,0:T(8,128)(2,1)S(1)} %collective-permute-done.3.other_ref, bf16[12,128,32,128]{3,2,1,0:T(8,128)(2,1)S(1)} %bitcast.25, ...), custom_call_target="tpu_custom_call" | custom-call | bytes 5400000 | tf_op jit(solution)/shard_map/pallas_call | solution.py:77
  36.6 1.3 %collective-permute-done.11.refs_4_ = bf16[8,32,128]{2,1,0:T(8,128)(2,1)S(1)} collective-permute-done((bf16[8,32,128]{2,1,0:T(8,128)(2,1)S(1)}, bf16[8,32,128]{2,1,0:T(8,128)(2,1)S(1)}, u32[]{:S(2)}, u32[]{:S(2)}) %collective-permute-start.11) | collective-permute-done | bytes 65568 | tf_op jit(solution)/shard_map/ppermute | solution.py:325
  39.7 1.3 %collective-permute-done.8.refs_3_ = bf16[8,32,128]{2,1,0:T(8,128)(2,1)S(1)} collective-permute-done((bf16[8,32,128]{2,1,0:T(8,128)(2,1)S(1)}, bf16[8,32,128]{2,1,0:T(8,128)(2,1)S(1)}, u32[]{:S(2)}, u32[]{:S(2)}) %collective-permute-start.8) | collective-permute-done | bytes 65568 | tf_op jit(solution)/shard_map/ppermute | solution.py:325
  41.1 2.1 %shard_map.59 = (bf16[2,8,32,128]{3,2,1,0:T(8,128)(2,1)S(1)}, bf16[2,8,32,128]{3,2,1,0:T(8,128)(2,1)S(1)}, bf16[2,8,32,128]{3,2,1,0:T(8,128)(2,1)S(1)}, bf16[2,8,32,128]{3,2,1,0:T(8,128)(2,1)S(1)}) custom-call(s32[1]{0:T(128)} %bitcast.t, bf16[8,32,128]{2,1,0:T(8,128)(2,1)S(1)} %get-tuple-element.25.refs_0_, ...), custom_call_target="tpu_custom_call" | custom-call | bytes 9000000 | tf_op jit(solution)/shard_map/pallas_call | solution.py:77
  45.3 2.1 %collective-permute-start.19 = (bf16[2,8,32,128]{3,2,1,0:T(8,128)(2,1)S(1)}, bf16[2,8,32,128]{3,2,1,0:T(8,128)(2,1)S(1)}, u32[]{:S(2)}, u32[]{:S(2)}) collective-permute-start(bf16[2,8,32,128]{3,2,1,0:T(8,128)(2,1)S(1)} %shard_map.61.own_ref), channel_id=1, source_target_pairs={{0,2},{1,3},{2,0},{3,1},{4,6},{5,7},{6,4},{7,5},{8,10},{9,11},{10,... | collective-permute-start | bytes 393224 | tf_op jit(solution)/shard_map/ppermute | solution.py:325
  48.2 2.1 %collective-permute-start.22 = (bf16[2,8,32,128]{3,2,1,0:T(8,128)(2,1)S(1)}, bf16[2,8,32,128]{3,2,1,0:T(8,128)(2,1)S(1)}, u32[]{:S(2)}, u32[]{:S(2)}) collective-permute-start(bf16[2,8,32,128]{3,2,1,0:T(8,128)(2,1)S(1)} %shard_map.64.own_ref), channel_id=1, source_target_pairs={{0,2},{1,3},{2,0},{3,1},{4,6},{5,7},{6,4},{7,5},{8,10},{9,11},{10,... | collective-permute-start | bytes 393224 | tf_op jit(solution)/shard_map/ppermute | solution.py:325
  51.6 1.4 %collective-permute-start.28 = (bf16[2,8,32,128]{3,2,1,0:T(8,128)(2,1)S(1)}, bf16[2,8,32,128]{3,2,1,0:T(8,128)(2,1)S(1)}, u32[]{:S(2)}, u32[]{:S(2)}) collective-permute-start(bf16[2,8,32,128]{3,2,1,0:T(8,128)(2,1)S(1)} %shard_map.67.own_ref), channel_id=1, source_target_pairs={{0,4},{1,5},{2,6},{3,7},{4,0},{5,1},{6,2},{7,3},{8,12},{9,13},{10,... | collective-permute-start | bytes 393224 | tf_op jit(solution)/shard_map/ppermute | solution.py:325
  53.0 2.4 %collective-permute-done.19.other_ref = bf16[2,8,32,128]{3,2,1,0:T(8,128)(2,1)S(1)} collective-permute-done((bf16[2,8,32,128]{3,2,1,0:T(8,128)(2,1)S(1)}, bf16[2,8,32,128]{3,2,1,0:T(8,128)(2,1)S(1)}, u32[]{:S(2)}, u32[]{:S(2)}) %collective-permute-start.19) | collective-permute-done | bytes 131104 | tf_op jit(solution)/shard_map/ppermute | solution.py:325
  55.9 5.3 %collective-permute-done.25.other_ref = bf16[2,8,32,128]{3,2,1,0:T(8,128)(2,1)S(1)} collective-permute-done((bf16[2,8,32,128]{3,2,1,0:T(8,128)(2,1)S(1)}, bf16[2,8,32,128]{3,2,1,0:T(8,128)(2,1)S(1)}, u32[]{:S(2)}, u32[]{:S(2)}) %collective-permute-start.25) | collective-permute-done | bytes 131104 | tf_op jit(solution)/shard_map/ppermute | solution.py:325
  61.7 1.6 %collective-permute-done.22.other_ref = bf16[2,8,32,128]{3,2,1,0:T(8,128)(2,1)S(1)} collective-permute-done((bf16[2,8,32,128]{3,2,1,0:T(8,128)(2,1)S(1)}, bf16[2,8,32,128]{3,2,1,0:T(8,128)(2,1)S(1)}, u32[]{:S(2)}, u32[]{:S(2)}) %collective-permute-start.22) | collective-permute-done | bytes 131104 | tf_op jit(solution)/shard_map/ppermute | solution.py:325
  63.6 1.4 %collective-permute-start.23 = (bf16[2,8,32,128]{3,2,1,0:T(8,128)(2,1)S(1)}, bf16[2,8,32,128]{3,2,1,0:T(8,128)(2,1)S(1)}, u32[]{:S(2)}, u32[]{:S(2)}) collective-permute-start(bf16[2,8,32,128]{3,2,1,0:T(8,128)(2,1)S(1)} %shard_map.65.own_ref), channel_id=1, source_target_pairs={{0,4},{1,5},{2,6},{3,7},{4,0},{5,1},{6,2},{7,3},{8,12},{9,13},{10,... | collective-permute-start | bytes 393224 | tf_op jit(solution)/shard_map/ppermute | solution.py:325
  65.1 2.2 %copy-done.3 = bf16[1,128,32,512]{3,2,1,0:T(8,128)(2,1)S(1)} copy-done((bf16[1,128,32,512]{3,2,1,0:T(8,128)(2,1)S(1)}, bf16[1,128,32,512]{3,2,1,0:T(8,128)(2,1)}, u32[]{:S(2)}) %copy-start.3) | copy-done | bytes 4194328
  67.3 5.5 %shard_map.66.near_ref = f32[64,32,128]{2,1,0:T(8,128)S(1)} custom-call(s32[1]{0:T(128)} %bitcast.t, s32[128,8]{1,0:T(8,128)S(1)} %bitcast.48, bf16[2,8,32,128]{3,2,1,0:T(8,128)(2,1)S(1)} %shard_map.46.own_ref.refs_0_, bf16[2,8,32,128]{3,2,1,0:T(8,128)(2,1)S(1)} %shard_map.50.own_ref.refs_1_, bf16[2,8,32,128]{3,2,1,0:T(8,128)(2,1)S(1)} %shard_map.53.own_ref.refs_2_, ...), custom_call_target="tpu_custom_call" | custom-call | bytes 21600000 | tf_op jit(solution)/shard_map/pallas_call | solution.py:306
  72.8 1.2 %shard_map.69.rest_0_ = f32[128,2048]{1,0:T(8,128)} custom-call(s32[1]{0:T(128)} %bitcast.t, bf16[2,8,32,128]{3,2,1,0:T(8,128)(2,1)S(1)} %shard_map.68.own_ref, bf16[2,8,32,128]{3,2,1,0:T(8,128)(2,1)S(1)} %collective-permute-done.28.other_ref, bf16[1,128,32,128]{3,2,1,0:T(8,128)(2,1)S(1)} %get-tuple-element.39.w_ref, f32[64,32,128]{2,1,0:T(8,128)S(1)} %shard_map.66.near_ref), custom_call_target="tpu_custom_call" | custom-call | bytes 4320000 | tf_op jit(solution)/shard_map/pallas_call | solution.py:77
  74.0 1.2 %shard_map.70.rest_0_ = f32[128,2048]{1,0:T(8,128)} custom-call(s32[1]{0:T(128)} %bitcast.t, bf16[2,8,32,128]{3,2,1,0:T(8,128)(2,1)S(1)} %shard_map.65.own_ref, bf16[2,8,32,128]{3,2,1,0:T(8,128)(2,1)S(1)} %collective-permute-done.27.other_ref, bf16[1,128,32,128]{3,2,1,0:T(8,128)(2,1)S(1)} %get-tuple-element.39.w_ref, ...), custom_call_target="tpu_custom_call", output_to_operand_aliasing={{}: (5, {})} | custom-call | bytes 4320000 | tf_op jit(solution)/shard_map/pallas_call | solution.py:77
  75.2 1.1 %collective-permute-done.26.other_ref = bf16[2,8,32,128]{3,2,1,0:T(8,128)(2,1)S(1)} collective-permute-done((bf16[2,8,32,128]{3,2,1,0:T(8,128)(2,1)S(1)}, bf16[2,8,32,128]{3,2,1,0:T(8,128)(2,1)S(1)}, u32[]{:S(2)}, u32[]{:S(2)}) %collective-permute-start.26) | collective-permute-done | bytes 131104 | tf_op jit(solution)/shard_map/ppermute | solution.py:325
  76.3 1.2 %shard_map.71.rest_0_ = f32[128,2048]{1,0:T(8,128)} custom-call(s32[1]{0:T(128)} %bitcast.t, bf16[2,8,32,128]{3,2,1,0:T(8,128)(2,1)S(1)} %shard_map.67.own_ref, bf16[2,8,32,128]{3,2,1,0:T(8,128)(2,1)S(1)} %collective-permute-done.26.other_ref, bf16[1,128,32,128]{3,2,1,0:T(8,128)(2,1)S(1)} %get-tuple-element.39.w_ref, ...), custom_call_target="tpu_custom_call", output_to_operand_aliasing={{}: (5, {})} | custom-call | bytes 4320000 | tf_op jit(solution)/shard_map/pallas_call | solution.py:77
  77.9 1.2 %shard_map.72 = f32[128,2048]{1,0:T(8,128)} custom-call(s32[1]{0:T(128)} %bitcast.t, bf16[2,8,32,128]{3,2,1,0:T(8,128)(2,1)S(1)} %shard_map.62.own_ref, bf16[2,8,32,128]{3,2,1,0:T(8,128)(2,1)S(1)} %collective-permute-done.23.other_ref, bf16[1,128,32,128]{3,2,1,0:T(8,128)(2,1)S(1)} %get-tuple-element.39.w_ref, ...), custom_call_target="tpu_custom_call", output_to_operand_aliasing={{}: (5, {})} | custom-call | bytes 4320000 | tf_op jit(solution)/shard_map/pallas_call | solution.py:77
  (65 shorter events, 14.3 us)
Async XLA Ops:
  0.0 20.1 %copy-start = (bf16[12,1,128,32,128]{4,3,2,1,0:T(8,128)(2,1)S(1)}, bf16[12,1,128,32,128]{4,3,2,1,0:T(8,128)(2,1)}, u32[]{:S(2)}) copy-start(bf16[12,1,128,32,128]{4,3,2,1,0:T(8,128)(2,1)} %param.5) | copy-start | bytes 37748740
  1.5 7.9 %collective-permute-start.13 = (bf16[2,8,32,128]{3,2,1,0:T(8,128)(2,1)S(1)}, bf16[2,8,32,128]{3,2,1,0:T(8,128)(2,1)S(1)}, u32[]{:S(2)}, u32[]{:S(2)}) collective-permute-start(bf16[2,8,32,128]{3,2,1,0:T(8,128)(2,1)S(1)} %shard_map.56.own_ref.refs_3_), channel_id=1, source_target_pairs={{0,8},{8,0},{16,24},{24,16},{1,9},{9,1},{17,25},{25,17},{2,10},{10... | collective-permute-start | bytes 393224 | tf_op jit(solution)/shard_map/ppermute | solution.py:325
  4.7 9.6 %collective-permute-start.9 = (bf16[2,8,32,128]{3,2,1,0:T(8,128)(2,1)S(1)}, bf16[2,8,32,128]{3,2,1,0:T(8,128)(2,1)S(1)}, u32[]{:S(2)}, u32[]{:S(2)}) collective-permute-start(bf16[2,8,32,128]{3,2,1,0:T(8,128)(2,1)S(1)} %shard_map.53.own_ref.refs_2_), channel_id=1, source_target_pairs={{0,8},{8,0},{16,24},{24,16},{1,9},{9,1},{17,25},{25,17},{2,10},{10... | collective-permute-start | bytes 393224 | tf_op jit(solution)/shard_map/ppermute | solution.py:325
  5.1 10.9 %collective-permute-start.5 = (bf16[2,8,32,128]{3,2,1,0:T(8,128)(2,1)S(1)}, bf16[2,8,32,128]{3,2,1,0:T(8,128)(2,1)S(1)}, u32[]{:S(2)}, u32[]{:S(2)}) collective-permute-start(bf16[2,8,32,128]{3,2,1,0:T(8,128)(2,1)S(1)} %shard_map.50.own_ref.refs_1_), channel_id=1, source_target_pairs={{0,8},{8,0},{16,24},{24,16},{1,9},{9,1},{17,25},{25,17},{2,10},{10... | collective-permute-start | bytes 393224 | tf_op jit(solution)/shard_map/ppermute | solution.py:325
  7.4 11.8 %collective-permute-start = (bf16[2,8,32,128]{3,2,1,0:T(8,128)(2,1)S(1)}, bf16[2,8,32,128]{3,2,1,0:T(8,128)(2,1)S(1)}, u32[]{:S(2)}, u32[]{:S(2)}) collective-permute-start(bf16[2,8,32,128]{3,2,1,0:T(8,128)(2,1)S(1)} %shard_map.46.own_ref.refs_0_), channel_id=1, source_target_pairs={{0,8},{8,0},{16,24},{24,16},{1,9},{9,1},{17,25},{25,17},{2,10},{10... | collective-permute-start | bytes 393224 | tf_op jit(solution)/shard_map/ppermute | solution.py:325
  9.7 10.4 %collective-permute-start.14 = (bf16[2,8,32,128]{3,2,1,0:T(8,128)(2,1)S(1)}, bf16[2,8,32,128]{3,2,1,0:T(8,128)(2,1)S(1)}, u32[]{:S(2)}, u32[]{:S(2)}) collective-permute-start(bf16[2,8,32,128]{3,2,1,0:T(8,128)(2,1)S(1)} %shard_map.57.own_ref), channel_id=1, source_target_pairs={{0,16},{8,24},{16,0},{24,8},{1,17},{9,25},{17,1},{25,9},{2,18},{10... | collective-permute-start | bytes 393224 | tf_op jit(solution)/shard_map/ppermute | solution.py:325
  13.0 3.8 %collective-permute-start.1 = (bf16[2,32,128]{2,1,0:T(8,128)(2,1)S(1)}, bf16[2,32,128]{2,1,0:T(8,128)(2,1)S(1)}, u32[]{:S(2)}, u32[]{:S(2)}) collective-permute-start(bf16[2,32,128]{2,1,0:T(8,128)(2,1)S(1)} %get-tuple-element.22), channel_id=1, source_target_pairs={{0,1},{1,2},{2,3},{3,4},{4,5},{5,6},{6,7},{8,9},{9,10},{10,11},{11... | collective-permute-start | bytes 49160 | tf_op jit(solution)/shard_map/ppermute | solution.py:373
  14.3 4.9 %collective-permute-start.2 = (bf16[2,32,128]{2,1,0:T(8,128)(2,1)S(1)}, bf16[2,32,128]{2,1,0:T(8,128)(2,1)S(1)}, u32[]{:S(2)}, u32[]{:S(2)}) collective-permute-start(bf16[2,32,128]{2,1,0:T(8,128)(2,1)S(1)} %get-tuple-element.23), channel_id=1, source_target_pairs={{1,0},{2,1},{3,2},{4,3},{5,4},{6,5},{7,6},{9,8},{10,9},{11,10},{12... | collective-permute-start | bytes 49160 | tf_op jit(solution)/shard_map/ppermute | solution.py:374
  16.0 11.5 %collective-permute-start.10 = (bf16[2,8,32,128]{3,2,1,0:T(8,128)(2,1)S(1)}, bf16[2,8,32,128]{3,2,1,0:T(8,128)(2,1)S(1)}, u32[]{:S(2)}, u32[]{:S(2)}) collective-permute-start(bf16[2,8,32,128]{3,2,1,0:T(8,128)(2,1)S(1)} %shard_map.54.own_ref), channel_id=1, source_target_pairs={{0,16},{8,24},{16,0},{24,8},{1,17},{9,25},{17,1},{25,9},{2,18},{10... | collective-permute-start | bytes 393224 | tf_op jit(solution)/shard_map/ppermute | solution.py:325
  16.8 12.6 %collective-permute-start.6 = (bf16[2,8,32,128]{3,2,1,0:T(8,128)(2,1)S(1)}, bf16[2,8,32,128]{3,2,1,0:T(8,128)(2,1)S(1)}, u32[]{:S(2)}, u32[]{:S(2)}) collective-permute-start(bf16[2,8,32,128]{3,2,1,0:T(8,128)(2,1)S(1)} %shard_map.51.own_ref), channel_id=1, source_target_pairs={{0,16},{8,24},{16,0},{24,8},{1,17},{9,25},{17,1},{25,9},{2,18},{10... | collective-permute-start | bytes 393224 | tf_op jit(solution)/shard_map/ppermute | solution.py:325
  19.5 13.3 %collective-permute-start.3 = (bf16[2,8,32,128]{3,2,1,0:T(8,128)(2,1)S(1)}, bf16[2,8,32,128]{3,2,1,0:T(8,128)(2,1)S(1)}, u32[]{:S(2)}, u32[]{:S(2)}) collective-permute-start(bf16[2,8,32,128]{3,2,1,0:T(8,128)(2,1)S(1)} %shard_map.48.own_ref), channel_id=1, source_target_pairs={{0,16},{8,24},{16,0},{24,8},{1,17},{9,25},{17,1},{25,9},{2,18},{10... | collective-permute-start | bytes 393224 | tf_op jit(solution)/shard_map/ppermute | solution.py:325
  21.5 14.5 %collective-permute-start.15 = (bf16[8,32,128]{2,1,0:T(8,128)(2,1)S(1)}, bf16[8,32,128]{2,1,0:T(8,128)(2,1)S(1)}, u32[]{:S(2)}, u32[]{:S(2)}) collective-permute-start(bf16[8,32,128]{2,1,0:T(8,128)(2,1)S(1)} %get-tuple-element.31), channel_id=1, source_target_pairs={{0,6},{1,7},{2,4},{3,5},{4,2},{5,3},{6,0},{7,1},{8,14},{9,15},{10,... | collective-permute-start | bytes 196616 | tf_op jit(solution)/shard_map/ppermute | solution.py:325
  27.5 8.9 %collective-permute-start.16 = (bf16[8,32,128]{2,1,0:T(8,128)(2,1)S(1)}, bf16[8,32,128]{2,1,0:T(8,128)(2,1)S(1)}, u32[]{:S(2)}, u32[]{:S(2)}) collective-permute-start(bf16[8,32,128]{2,1,0:T(8,128)(2,1)S(1)} %get-tuple-element.32), channel_id=1, source_target_pairs={{0,7},{1,6},{2,5},{3,4},{4,3},{5,2},{6,1},{7,0},{8,15},{9,14},{10,... | collective-permute-start | bytes 196616 | tf_op jit(solution)/shard_map/ppermute | solution.py:325
  28.9 9.0 %collective-permute-start.11 = (bf16[8,32,128]{2,1,0:T(8,128)(2,1)S(1)}, bf16[8,32,128]{2,1,0:T(8,128)(2,1)S(1)}, u32[]{:S(2)}, u32[]{:S(2)}) collective-permute-start(bf16[8,32,128]{2,1,0:T(8,128)(2,1)S(1)} %get-tuple-element.29), channel_id=1, source_target_pairs={{0,4},{1,5},{2,6},{3,7},{4,0},{5,1},{6,2},{7,3},{8,12},{9,13},{10,... | collective-permute-start | bytes 196616 | tf_op jit(solution)/shard_map/ppermute | solution.py:325
  29.5 9.4 %collective-permute-start.12 = (bf16[8,32,128]{2,1,0:T(8,128)(2,1)S(1)}, bf16[8,32,128]{2,1,0:T(8,128)(2,1)S(1)}, u32[]{:S(2)}, u32[]{:S(2)}) collective-permute-start(bf16[8,32,128]{2,1,0:T(8,128)(2,1)S(1)} %get-tuple-element.30), channel_id=1, source_target_pairs={{0,5},{1,4},{2,7},{3,6},{4,1},{5,0},{6,3},{7,2},{8,13},{9,12},{10,... | collective-permute-start | bytes 196616 | tf_op jit(solution)/shard_map/ppermute | solution.py:325
  32.8 6.9 %collective-permute-start.7 = (bf16[8,32,128]{2,1,0:T(8,128)(2,1)S(1)}, bf16[8,32,128]{2,1,0:T(8,128)(2,1)S(1)}, u32[]{:S(2)}, u32[]{:S(2)}) collective-permute-start(bf16[8,32,128]{2,1,0:T(8,128)(2,1)S(1)} %get-tuple-element.27), channel_id=1, source_target_pairs={{0,2},{1,3},{2,0},{3,1},{4,6},{5,7},{6,4},{7,5},{8,10},{9,11},{10,... | collective-permute-start | bytes 196616 | tf_op jit(solution)/shard_map/ppermute | solution.py:325
  36.1 5.0 %collective-permute-start.8 = (bf16[8,32,128]{2,1,0:T(8,128)(2,1)S(1)}, bf16[8,32,128]{2,1,0:T(8,128)(2,1)S(1)}, u32[]{:S(2)}, u32[]{:S(2)}) collective-permute-start(bf16[8,32,128]{2,1,0:T(8,128)(2,1)S(1)} %get-tuple-element.28), channel_id=1, source_target_pairs={{0,3},{1,2},{2,1},{3,0},{4,7},{5,6},{6,5},{7,4},{8,11},{9,10},{10,... | collective-permute-start | bytes 196616 | tf_op jit(solution)/shard_map/ppermute | solution.py:325
  36.4 4.7 %collective-permute-start.4 = (bf16[8,32,128]{2,1,0:T(8,128)(2,1)S(1)}, bf16[8,32,128]{2,1,0:T(8,128)(2,1)S(1)}, u32[]{:S(2)}, u32[]{:S(2)}) collective-permute-start(bf16[8,32,128]{2,1,0:T(8,128)(2,1)S(1)} %get-tuple-element.26), channel_id=1, source_target_pairs={{0,1},{1,0},{2,3},{3,2},{4,5},{5,4},{6,7},{7,6},{8,9},{9,8},{10,11... | collective-permute-start | bytes 196616 | tf_op jit(solution)/shard_map/ppermute | solution.py:325
  43.1 1.4 %collective-permute-start.17 = (bf16[2,8,32,128]{3,2,1,0:T(8,128)(2,1)S(1)}, bf16[2,8,32,128]{3,2,1,0:T(8,128)(2,1)S(1)}, u32[]{:S(2)}, u32[]{:S(2)}) collective-permute-start(bf16[2,8,32,128]{3,2,1,0:T(8,128)(2,1)S(1)} %get-tuple-element.33.own_ref), channel_id=1, source_target_pairs={{0,1},{1,0},{2,3},{3,2},{4,5},{5,4},{6,7},{7,6},{8,9},{9,8},{10,11... | collective-permute-start | bytes 393224 | tf_op jit(solution)/shard_map/ppermute | solution.py:325
  43.3 1.7 %collective-permute-start.18 = (bf16[2,8,32,128]{3,2,1,0:T(8,128)(2,1)S(1)}, bf16[2,8,32,128]{3,2,1,0:T(8,128)(2,1)S(1)}, u32[]{:S(2)}, u32[]{:S(2)}) collective-permute-start(bf16[2,8,32,128]{3,2,1,0:T(8,128)(2,1)S(1)} %get-tuple-element.34.own_ref), channel_id=1, source_target_pairs={{0,1},{1,0},{2,3},{3,2},{4,5},{5,4},{6,7},{7,6},{8,9},{9,8},{10,11... | collective-permute-start | bytes 393224 | tf_op jit(solution)/shard_map/ppermute | solution.py:325
  43.7 3.7 %collective-permute-start.20 = (bf16[2,8,32,128]{3,2,1,0:T(8,128)(2,1)S(1)}, bf16[2,8,32,128]{3,2,1,0:T(8,128)(2,1)S(1)}, u32[]{:S(2)}, u32[]{:S(2)}) collective-permute-start(bf16[2,8,32,128]{3,2,1,0:T(8,128)(2,1)S(1)} %get-tuple-element.35.own_ref), channel_id=1, source_target_pairs={{0,1},{1,0},{2,3},{3,2},{4,5},{5,4},{6,7},{7,6},{8,9},{9,8},{10,11... | collective-permute-start | bytes 393224 | tf_op jit(solution)/shard_map/ppermute | solution.py:325
  43.8 4.0 %collective-permute-start.21 = (bf16[2,8,32,128]{3,2,1,0:T(8,128)(2,1)S(1)}, bf16[2,8,32,128]{3,2,1,0:T(8,128)(2,1)S(1)}, u32[]{:S(2)}, u32[]{:S(2)}) collective-permute-start(bf16[2,8,32,128]{3,2,1,0:T(8,128)(2,1)S(1)} %get-tuple-element.36.own_ref), channel_id=1, source_target_pairs={{0,1},{1,0},{2,3},{3,2},{4,5},{5,4},{6,7},{7,6},{8,9},{9,8},{10,11... | collective-permute-start | bytes 393224 | tf_op jit(solution)/shard_map/ppermute | solution.py:325
  44.9 6.4 %collective-permute-start.24 = (bf16[2,8,32,128]{3,2,1,0:T(8,128)(2,1)S(1)}, bf16[2,8,32,128]{3,2,1,0:T(8,128)(2,1)S(1)}, u32[]{:S(2)}, u32[]{:S(2)}) collective-permute-start(bf16[2,8,32,128]{3,2,1,0:T(8,128)(2,1)S(1)} %shard_map.60.own_ref), channel_id=1, source_target_pairs={{0,2},{1,3},{2,0},{3,1},{4,6},{5,7},{6,4},{7,5},{8,10},{9,11},{10,... | collective-permute-start | bytes 393224 | tf_op jit(solution)/shard_map/ppermute | solution.py:325
  45.3 10.2 %collective-permute-start.19 = (bf16[2,8,32,128]{3,2,1,0:T(8,128)(2,1)S(1)}, bf16[2,8,32,128]{3,2,1,0:T(8,128)(2,1)S(1)}, u32[]{:S(2)}, u32[]{:S(2)}) collective-permute-start(bf16[2,8,32,128]{3,2,1,0:T(8,128)(2,1)S(1)} %shard_map.61.own_ref), channel_id=1, source_target_pairs={{0,2},{1,3},{2,0},{3,1},{4,6},{5,7},{6,4},{7,5},{8,10},{9,11},{10,... | collective-permute-start | bytes 393224 | tf_op jit(solution)/shard_map/ppermute | solution.py:325
  47.7 13.6 %collective-permute-start.25 = (bf16[2,8,32,128]{3,2,1,0:T(8,128)(2,1)S(1)}, bf16[2,8,32,128]{3,2,1,0:T(8,128)(2,1)S(1)}, u32[]{:S(2)}, u32[]{:S(2)}) collective-permute-start(bf16[2,8,32,128]{3,2,1,0:T(8,128)(2,1)S(1)} %shard_map.63.own_ref), channel_id=1, source_target_pairs={{0,2},{1,3},{2,0},{3,1},{4,6},{5,7},{6,4},{7,5},{8,10},{9,11},{10,... | collective-permute-start | bytes 393224 | tf_op jit(solution)/shard_map/ppermute | solution.py:325
  48.2 15.1 %collective-permute-start.22 = (bf16[2,8,32,128]{3,2,1,0:T(8,128)(2,1)S(1)}, bf16[2,8,32,128]{3,2,1,0:T(8,128)(2,1)S(1)}, u32[]{:S(2)}, u32[]{:S(2)}) collective-permute-start(bf16[2,8,32,128]{3,2,1,0:T(8,128)(2,1)S(1)} %shard_map.64.own_ref), channel_id=1, source_target_pairs={{0,2},{1,3},{2,0},{3,1},{4,6},{5,7},{6,4},{7,5},{8,10},{9,11},{10,... | collective-permute-start | bytes 393224 | tf_op jit(solution)/shard_map/ppermute | solution.py:325
  51.6 21.2 %collective-permute-start.28 = (bf16[2,8,32,128]{3,2,1,0:T(8,128)(2,1)S(1)}, bf16[2,8,32,128]{3,2,1,0:T(8,128)(2,1)S(1)}, u32[]{:S(2)}, u32[]{:S(2)}) collective-permute-start(bf16[2,8,32,128]{3,2,1,0:T(8,128)(2,1)S(1)} %shard_map.67.own_ref), channel_id=1, source_target_pairs={{0,4},{1,5},{2,6},{3,7},{4,0},{5,1},{6,2},{7,3},{8,12},{9,13},{10,... | collective-permute-start | bytes 393224 | tf_op jit(solution)/shard_map/ppermute | solution.py:325
  55.8 9.2 %copy-start.4 = (s32[1,128,8]{1,2,0:T(8,128)S(1)}, s32[1,128,8]{1,2,0:T(8,128)}, u32[]{:S(2)}) copy-start(s32[1,128,8]{1,2,0:T(8,128)} %param.7) | copy-start | bytes 12292
  55.9 18.2 %collective-permute-start.27 = (bf16[2,8,32,128]{3,2,1,0:T(8,128)(2,1)S(1)}, bf16[2,8,32,128]{3,2,1,0:T(8,128)(2,1)S(1)}, u32[]{:S(2)}, u32[]{:S(2)}) collective-permute-start(bf16[2,8,32,128]{3,2,1,0:T(8,128)(2,1)S(1)} %shard_map.62.own_ref), channel_id=1, source_target_pairs={{0,4},{1,5},{2,6},{3,7},{4,0},{5,1},{6,2},{7,3},{8,12},{9,13},{10,... | collective-permute-start | bytes 393224 | tf_op jit(solution)/shard_map/ppermute | solution.py:325
  61.6 14.7 %collective-permute-start.26 = (bf16[2,8,32,128]{3,2,1,0:T(8,128)(2,1)S(1)}, bf16[2,8,32,128]{3,2,1,0:T(8,128)(2,1)S(1)}, u32[]{:S(2)}, u32[]{:S(2)}) collective-permute-start(bf16[2,8,32,128]{3,2,1,0:T(8,128)(2,1)S(1)} %shard_map.68.own_ref), channel_id=1, source_target_pairs={{0,4},{1,5},{2,6},{3,7},{4,0},{5,1},{6,2},{7,3},{8,12},{9,13},{10,... | collective-permute-start | bytes 393224 | tf_op jit(solution)/shard_map/ppermute | solution.py:325
  63.6 14.3 %collective-permute-start.23 = (bf16[2,8,32,128]{3,2,1,0:T(8,128)(2,1)S(1)}, bf16[2,8,32,128]{3,2,1,0:T(8,128)(2,1)S(1)}, u32[]{:S(2)}, u32[]{:S(2)}) collective-permute-start(bf16[2,8,32,128]{3,2,1,0:T(8,128)(2,1)S(1)} %shard_map.65.own_ref), channel_id=1, source_target_pairs={{0,4},{1,5},{2,6},{3,7},{4,0},{5,1},{6,2},{7,3},{8,12},{9,13},{10,... | collective-permute-start | bytes 393224 | tf_op jit(solution)/shard_map/ppermute | solution.py:325
  65.1 2.2 %copy-start.3 = (bf16[1,128,32,512]{3,2,1,0:T(8,128)(2,1)S(1)}, bf16[1,128,32,512]{3,2,1,0:T(8,128)(2,1)}, u32[]{:S(2)}) copy-start(bf16[1,128,32,512]{3,2,1,0:T(8,128)(2,1)} %param.6) | copy-start | bytes 12582916
  (2 other events, 2.2 us)

commit v3 on v2

--- a/solution.py
+++ b/solution.py
@@ -110,36 +110,48 @@
     out_ref[...] = tall[...].astype(BF).reshape(out_ref.shape)
 
 
-def edge_kernel(rows, first_ref, last_ref, first_out, last_out, wide, tall):
-    pairs, rank, _ = first_out.shape
-    for ref, out, start in ((first_ref, first_out, 0), (last_ref, last_out, rows - HW)):
+def edge_kernel(rows, t, one_ref, two_ref, one_out, two_out, wide, tall):
+    pairs, rank, _ = one_out.shape
+    even_start = rows - HW
+    odd = t[0] % 2
+    starts = (even_start * (1 - odd), even_start * odd)
+    for ref, out, start in zip((one_ref, two_ref), (one_out, two_out), starts):
         for j in range(rank // 2):
             wide[j] = ref[:, pl.ds(j * 128, 128)].astype(F32)
         for j in range(rank // 2):
-            even = wide[j, pl.ds(start, pairs, stride=2), :]
-            odd = wide[j, pl.ds(start + 1, pairs, stride=2), :]
-            low = lane_of(even) < 64
-            tall[pl.ds(2 * j, pairs, stride=rank), :] = jnp.where(low, even, half_swap(odd))
-            tall[pl.ds(2 * j + 1, pairs, stride=rank), :] = jnp.where(low, half_swap(even), odd)
+            first = wide[j, pl.ds(start, pairs, stride=2), :]
+            second = wide[j, pl.ds(start + 1, pairs, stride=2), :]
+            low = lane_of(first) < 64
+            tall[pl.ds(2 * j, pairs, stride=rank), :] = jnp.where(low, first, half_swap(second))
+            tall[pl.ds(2 * j + 1, pairs, stride=rank), :] = jnp.where(
+                low, half_swap(first), second
+            )
         out[...] = tall[...].astype(BF).reshape(out.shape)
 
 
-def edge_pairs(incident, rank):
+def edge_pairs(tgt_index, incident, rank):
     blocks, width = incident.shape
     rows, pairs = 16, HW // 2
+    end = blocks // rows - 1
     shape = jax.ShapeDtypeStruct((pairs, rank, 128), BF)
     return pl.pallas_call(
         functools.partial(edge_kernel, rows),
-        grid=(1,),
-        in_specs=[
-            pl.BlockSpec((rows, width), lambda i: (0, 0)),
-            pl.BlockSpec((rows, width), lambda i: (blocks // rows - 1, 0)),
-        ],
-        out_specs=[pl.BlockSpec(shape.shape, lambda i: (0, 0, 0))] * 2,
         out_shape=[shape] * 2,
-        scratch_shapes=[pltpu.VMEM((rank // 2, rows, 128), F32), pltpu.VMEM((pairs * rank, 128), F32)],
+        grid_spec=pltpu.PrefetchScalarGridSpec(
+            num_scalar_prefetch=1,
+            grid=(1,),
+            in_specs=[
+                pl.BlockSpec((rows, width), lambda i, t: (end * (1 - t[0] % 2), 0)),
+                pl.BlockSpec((rows, width), lambda i, t: (end * (t[0] % 2), 0)),
+            ],
+            out_specs=[full(shape.shape)] * 2,
+            scratch_shapes=[
+                pltpu.VMEM((rank // 2, rows, 128), F32),
+                pltpu.VMEM((pairs * rank, 128), F32),
+            ],
+        ),
         compiler_params=params(),
-    )(incident, incident)
+    )(tgt_index, incident, incident)
 
 
 def level_kernel(G, lows, flip, t, own_ref, other_ref, w_ref, out_ref):
@@ -156,7 +168,7 @@
 
 def split_kernel(G, lows, low_bits, t, own_ref, other_ref, *rest):
     w_refs = rest[: 1 + low_bits]
-    out_refs = rest[1 + low_bits : 1 + low_bits + G]
+    out_ref = rest[1 + low_bits]
     half = lows // 2
     keys = [(b, m) for b in range(G) for m in range(half)]
     groups = [(t[0] % G) ^ b for b in range(G)]
@@ -177,7 +189,7 @@
         }
         pairs = {key: with_turn(x) for key, x in values.items()} if bit < low_bits - 1 else values
     for b, m in keys:
-        out_refs[b][m] = pairs[b, m]
+        out_ref[b, m] = pairs[b, m]
 
 
 def group_kernel(G, lows, groups, t, *refs):
@@ -242,7 +254,7 @@
 
 def near_kernel(G, lows, chunks, count, near_count, t, lists, *refs):
     v_refs = refs[:chunks]
-    below_ref, above_ref, mats_ref, out_ref, window = refs[chunks : chunks + 5]
+    one_ref, two_ref, mats_ref, out_ref, window = refs[chunks : chunks + 5]
     half = lows // 2
     rank = v_refs[0].shape[2]
 
@@ -271,9 +283,10 @@
 
     @pl.when(pl.program_id(0) == 0)
     def _():
-        put([2 * e for e in range(HW // 2)], below_ref[...])
         after = HW + G * chunks * lows
-        put([after + 2 * e for e in range(HW // 2)], above_ref[...])
+        odd = t[0] % 2
+        put([after * (1 - odd) + 2 * e for e in range(HW // 2)], one_ref[...])
+        put([after * odd + 2 * e for e in range(HW // 2)], two_ref[...])
         for r in range(chunks):
             for b in range(G):
                 group = t[0] ^ (r * G + b)
@@ -293,7 +306,7 @@
             out_ref[n // 2] = jnp.where(lane_of(res) < 64, last, res)
 
 
-def near_field(tgt_index, lists, mats, chunks, below, above, G, lows):
+def near_field(tgt_index, lists, mats, chunks, one, two, G, lows):
     blocks, rank, cols = mats.shape
     near_count = lists.shape[1]
     count = 32
@@ -310,14 +323,14 @@
             num_scalar_prefetch=2,
             grid=(blocks // count,),
             in_specs=[spec(v_shape) for _ in chunks]
-            + [spec(below.shape), spec(above.shape)]
+            + [spec(one.shape), spec(two.shape)]
             + [pl.BlockSpec((count, rank, cols), lambda i, t, o: (i, 0, 0))],
             out_specs=pl.BlockSpec((count // 2, rank, 128), lambda i, t, o: (i, 0, 0)),
             scratch_shapes=[pltpu.VMEM((blocks + 2 * HW, 2 * rank, 128), BF)],
         ),
         compiler_params=params(),
         cost_estimate=cost(6.0),
-    )(tgt_index, lists, *chunks, below, above, mats)
+    )(tgt_index, lists, *chunks, one, two, mats)
 
 
 def swapped_with(x, axis, distance):
@@ -346,7 +359,6 @@
 
     chunk_shape = (G, half, rank, 128)
     chunk_out = jax.ShapeDtypeStruct(chunk_shape, BF)
-    group_out = jax.ShapeDtypeStruct(chunk_shape[1:], BF)
 
     def chunk_rows(r, width):
         return pl.BlockSpec((G * lows, width), lambda i, t: ((t[0] // G) ^ r, 0))
@@ -367,11 +379,10 @@
             0.4,
         )
 
-    ups = [(i, i + 1) for i in range(groups - 1)]
-    downs = [(i + 1, i) for i in range(groups - 1)]
-    first, last = edge_pairs(incident[0], rank)
-    below = lax.ppermute(last, "tgt", ups)
-    above = lax.ppermute(first, "tgt", downs)
+    one, two = edge_pairs(tgt_index, incident[0], rank)
+    beside = [(i, i + 1) for i in range(1, groups - 1, 2)]
+    one = swapped_with(one, "tgt", 1)
+    two = lax.ppermute(two, "tgt", beside + [(j, i) for i, j in beside])
     width = incident.shape[2]
     v = [None] * chunks
     for r in order:
@@ -393,37 +404,36 @@
     level = 0
     for bit in range(src_bits - 1):
         others = [swapped_with(v[r], "src", 1 << bit) for r in order]
-        if bit == 0:
-            others[-1], below, above = lax.optimization_barrier((others[-1], below, above))
         for r, other in zip(order, others):
             v[r] = level_call(level, r, v[r], other)
         level += 1
     arrived = [None] * groups
     for r in order:
         partner = swapped_with(v[r], "src", 1 << (src_bits - 1))
-        parts = call(
+        mixed = call(
             functools.partial(split_kernel, G, lows, low_bits),
             tgt_index,
             (v[r], partner) + (weights,) * (1 + low_bits),
             [full(chunk_shape), full(chunk_shape)]
             + [wspec(level + k, r) for k in range(1 + low_bits)],
-            [group_out] * G,
-            [full(chunk_shape[1:])] * G,
+            chunk_out,
+            full(chunk_shape),
             [],
             1.5,
         )
+        moved = swapped_with(mixed, "tgt", r * G) if r else mixed
         for b in range(G):
-            g = r * G + b
-            arrived[g] = swapped_with(parts[b], "tgt", g) if g else parts[b]
+            arrived[r * G + b] = swapped_with(moved, "tgt", b) if b else moved
     level += 1 + low_bits
-
-    near = near_field(tgt_index, near_lists[0], near_blocks[0], start, below, above, G, lows)
 
     v = call(
         functools.partial(group_kernel, G, lows, groups),
         tgt_index,
         tuple(arrived) + (weights,) * tgt_bits,
-        [full(chunk_shape[1:])] * groups
+        [
+            pl.BlockSpec((None,) + chunk_shape[1:], functools.partial(lambda b, i, t: (b, 0, 0, 0), g % G))
+            for g in range(groups)
+        ]
         + [
             pl.BlockSpec(
                 (None, blocks, rank, 128), functools.partial(lambda l, i, t: (l, 0, 0, 0), level + k)
@@ -440,8 +450,12 @@
     for bit in range(tgt_bits - 1):
         distance = 1 << bit
         others = [swapped_with(v[r ^ (distance // G)], "tgt", distance) for r in range(chunks)]
+        if bit == tgt_bits - 2:
+            others[-1], one, two = lax.optimization_barrier((others[-1], one, two))
         v = [level_call(level, r, v[r], others[r], distance % G) for r in range(chunks)]
         level += 1
+    near = near_field(tgt_index, near_lists[0], near_blocks[0], start, one, two, G, lows)
+
     out = None
     distance = 1 << (tgt_bits - 1)
     others = [swapped_with(v[r ^ (distance // G)], "tgt", distance) for r in range(chunks)]

time: 79.4 us -> 75.1 us (0.946)
  waiting for transfers between devices: 17.5 us -> 15.7 us
  starting transfers between devices: 31.7 us -> 30.2 us
  local copies, waits for them, and re-layouts: 6.43 us -> 5.39 us
    ppermute x2 -> x1, starting transfers between devices: 2.58 us -> 0.83 us  [per_device(): two = lax.ppermute(two, 'tgt', beside + [(j, i) for i, j in beside])]
    unnamed x11, local copies, waits for them, and re-layouts: 4.53 us -> 3.49 us
    ppermute x27 -> x28, waiting for transfers between devices: 16.8 us -> 15.7 us  [swapped_with(): return lax.ppermute(x, axis, [(i, i ^ distance) for i in range(count)])]
    ppermute x27 -> x28, starting transfers between devices: 29.1 us -> 29.4 us  [swapped_with(): return lax.ppermute(x, axis, [(i, i ^ distance) for i in range(count)])]
  transfers between devices with their start and end apart: 29 -> 29, of which waited for: 12 -> 11; matrix products, arithmetic and copies ran while one was open for 3% -> 3% of each run, Pallas kernels for 25% -> 26%
where the time goes in v3:
time: 75.1 us; the launch traced here: 74.9 us
  starting transfers between devices  30.2 us (40%)
  Pallas kernels  23.2 us (31%)
  waiting for transfers between devices  15.7 us (21%)
  local copies, waits for them, and re-layouts  5.39 us (7%)
    ppermute x28, starting transfers between devices, swapped_with(): return lax.ppermute(x, axis, [(i, i ^ distance) for i in range(count)])  29.4 us
    pallas_call x25, Pallas kernels, call(): pl.pallas_call(kernel, out_shape=out_shapes, grid_spec=pltpu.PrefetchScal...  17.6 us
    ppermute x28, waiting for transfers between devices, swapped_with(): return lax.ppermute(x, axis, [(i, i ^ distance) for i in range(count)])  15.7 us
    pallas_call x1, Pallas kernels, near_field(): pl.pallas_call(functools.partial(near_kernel, G, lows, len(chunks), count...  5.49 us
    unnamed x11, local copies, waits for them, and re-layouts  3.49 us
    squeeze x1, local copies, waits for them, and re-layouts, per_device(): ends = {0: factors[:1, 0], factors.shape[0] - 1: factors[-1:, 0]}  1.9 us
  transfers between devices with their start and end apart: 29, of which 11 were waited for; matrix products, arithmetic and copies ran while one was open for 3% of the time, Pallas kernels for 26%

profile of v3, /device:TPU:0, one launch (start us, length us, event | category | flops | bytes accessed | tf_op | source)
XLA Modules:
  0.0 74.9 jit_solution(2454110741519088067)
XLA Ops:
  0.0 1.2 %copy-done.1 = bf16[1,128,2048]{2,1,0:T(8,128)(2,1)S(1)} copy-done((bf16[1,128,2048]{2,1,0:T(8,128)(2,1)S(1)}, bf16[1,128,2048]{2,1,0:T(8,128)(2,1)}, u32[]{:S(2)}) %copy-start.1) | copy-done | bytes 524312
  1.5 3.0 %collective-permute-start.11 = (bf16[2,8,32,128]{3,2,1,0:T(8,128)(2,1)S(1)}, bf16[2,8,32,128]{3,2,1,0:T(8,128)(2,1)S(1)}, u32[]{:S(2)}, u32[]{:S(2)}) collective-permute-start(bf16[2,8,32,128]{3,2,1,0:T(8,128)(2,1)S(1)} %shard_map.55.own_ref.refs_3_), channel_id=1, source_target_pairs={{0,8},{8,0},{16,24},{24,16},{1,9},{9,1},{17,25},{25,17},{2,10},{10... | collective-permute-start | bytes 393224 | tf_op jit(solution)/shard_map/ppermute | solution.py:338
  5.1 2.1 %collective-permute-start.3 = (bf16[2,8,32,128]{3,2,1,0:T(8,128)(2,1)S(1)}, bf16[2,8,32,128]{3,2,1,0:T(8,128)(2,1)S(1)}, u32[]{:S(2)}, u32[]{:S(2)}) collective-permute-start(bf16[2,8,32,128]{3,2,1,0:T(8,128)(2,1)S(1)} %shard_map.49.own_ref.refs_1_), channel_id=1, source_target_pairs={{0,8},{8,0},{16,24},{24,16},{1,9},{9,1},{17,25},{25,17},{2,10},{10... | collective-permute-start | bytes 393224 | tf_op jit(solution)/shard_map/ppermute | solution.py:338
  7.5 1.9 %slice_bitcast_fusion = (bf16[1,128,32,128]{3,2,1,0:T(8,128)(2,1)S(1)}, bf16[1,128,32,128]{3,2,1,0:T(8,128)(2,1)S(1)}) fusion(bf16[12,1,128,32,128]{4,3,2,1,0:T(8,128)(2,1)} %param.5), kind=kLoop, calls=%fused_computation | loop fusion | bytes 4194304 | tf_op jit(solution)/shard_map/squeeze | solution.py:355
  9.7 2.1 %collective-permute-start.12 = (bf16[2,8,32,128]{3,2,1,0:T(8,128)(2,1)S(1)}, bf16[2,8,32,128]{3,2,1,0:T(8,128)(2,1)S(1)}, u32[]{:S(2)}, u32[]{:S(2)}) collective-permute-start(bf16[2,8,32,128]{3,2,1,0:T(8,128)(2,1)S(1)} %shard_map.56.own_ref), channel_id=1, source_target_pairs={{0,16},{8,24},{16,0},{24,8},{1,17},{9,25},{17,1},{25,9},{2,18},{10... | collective-permute-start | bytes 393224 | tf_op jit(solution)/shard_map/ppermute | solution.py:338
  12.2 1.9 %collective-permute-start.8 = (bf16[2,8,32,128]{3,2,1,0:T(8,128)(2,1)S(1)}, bf16[2,8,32,128]{3,2,1,0:T(8,128)(2,1)S(1)}, u32[]{:S(2)}, u32[]{:S(2)}) collective-permute-start(bf16[2,8,32,128]{3,2,1,0:T(8,128)(2,1)S(1)} %shard_map.53.own_ref), channel_id=1, source_target_pairs={{0,16},{8,24},{16,0},{24,8},{1,17},{9,25},{17,1},{25,9},{2,18},{10... | collective-permute-start | bytes 393224 | tf_op jit(solution)/shard_map/ppermute | solution.py:338
  14.7 2.1 %collective-permute-start.4 = (bf16[2,8,32,128]{3,2,1,0:T(8,128)(2,1)S(1)}, bf16[2,8,32,128]{3,2,1,0:T(8,128)(2,1)S(1)}, u32[]{:S(2)}, u32[]{:S(2)}) collective-permute-start(bf16[2,8,32,128]{3,2,1,0:T(8,128)(2,1)S(1)} %shard_map.50.own_ref), channel_id=1, source_target_pairs={{0,16},{8,24},{16,0},{24,8},{1,17},{9,25},{17,1},{25,9},{2,18},{10... | collective-permute-start | bytes 393224 | tf_op jit(solution)/shard_map/ppermute | solution.py:338
  17.2 1.3 %collective-permute-start.1 = (bf16[2,8,32,128]{3,2,1,0:T(8,128)(2,1)S(1)}, bf16[2,8,32,128]{3,2,1,0:T(8,128)(2,1)S(1)}, u32[]{:S(2)}, u32[]{:S(2)}) collective-permute-start(bf16[2,8,32,128]{3,2,1,0:T(8,128)(2,1)S(1)} %shard_map.47.own_ref), channel_id=1, source_target_pairs={{0,16},{8,24},{16,0},{24,8},{1,17},{9,25},{17,1},{25,9},{2,18},{10... | collective-permute-start | bytes 393224 | tf_op jit(solution)/shard_map/ppermute | solution.py:338
  18.6 1.4 %shard_map.57 = bf16[2,8,32,128]{3,2,1,0:T(8,128)(2,1)S(1)} custom-call(s32[1]{0:T(128)} %bitcast.t, bf16[2,8,32,128]{3,2,1,0:T(8,128)(2,1)S(1)} %shard_map.56.own_ref, bf16[2,8,32,128]{3,2,1,0:T(8,128)(2,1)S(1)} %collective-permute-done.12.other_ref, bf16[12,128,32,128]{3,2,1,0:T(8,128)(2,1)S(1)} %bitcast.10, bf16[12,128,32,128]{3,2,1,0:T(8,128)(2,1)S(1)} %bitcast.11, ...), custom_call_target="tpu_custom_call" | custom-call | bytes 5400000 | tf_op jit(solution)/shard_map/pallas_call | solution.py:77
  20.0 3.7 %collective-permute-start.13 = (bf16[2,8,32,128]{3,2,1,0:T(8,128)(2,1)S(1)}, bf16[2,8,32,128]{3,2,1,0:T(8,128)(2,1)S(1)}, u32[]{:S(2)}, u32[]{:S(2)}) collective-permute-start(bf16[2,8,32,128]{3,2,1,0:T(8,128)(2,1)S(1)} %shard_map.57), channel_id=1, source_target_pairs={{0,6},{1,7},{2,4},{3,5},{4,2},{5,3},{6,0},{7,1},{8,14},{9,15},{10,... | collective-permute-start | bytes 393224 | tf_op jit(solution)/shard_map/ppermute | solution.py:338
  23.7 1.4 %shard_map.54 = bf16[2,8,32,128]{3,2,1,0:T(8,128)(2,1)S(1)} custom-call(s32[1]{0:T(128)} %bitcast.t, bf16[2,8,32,128]{3,2,1,0:T(8,128)(2,1)S(1)} %shard_map.53.own_ref, bf16[2,8,32,128]{3,2,1,0:T(8,128)(2,1)S(1)} %collective-permute-done.8.other_ref, bf16[12,128,32,128]{3,2,1,0:T(8,128)(2,1)S(1)} %bitcast.15, bf16[12,128,32,128]{3,2,1,0:T(8,128)(2,1)S(1)} %bitcast.16, ...), custom_call_target="tpu_custom_call" | custom-call | bytes 5400000 | tf_op jit(solution)/shard_map/pallas_call | solution.py:77
  25.2 1.4 %shard_map.51 = bf16[2,8,32,128]{3,2,1,0:T(8,128)(2,1)S(1)} custom-call(s32[1]{0:T(128)} %bitcast.t, bf16[2,8,32,128]{3,2,1,0:T(8,128)(2,1)S(1)} %shard_map.50.own_ref, bf16[2,8,32,128]{3,2,1,0:T(8,128)(2,1)S(1)} %collective-permute-done.4.other_ref, bf16[12,128,32,128]{3,2,1,0:T(8,128)(2,1)S(1)} %bitcast.24, bf16[12,128,32,128]{3,2,1,0:T(8,128)(2,1)S(1)} %bitcast.21, ...), custom_call_target="tpu_custom_call" | custom-call | bytes 5400000 | tf_op jit(solution)/shard_map/pallas_call | solution.py:77
  26.6 0.8 %collective-permute-start.5 = (bf16[2,8,32,128]{3,2,1,0:T(8,128)(2,1)S(1)}, bf16[2,8,32,128]{3,2,1,0:T(8,128)(2,1)S(1)}, u32[]{:S(2)}, u32[]{:S(2)}) collective-permute-start(bf16[2,8,32,128]{3,2,1,0:T(8,128)(2,1)S(1)} %shard_map.51), channel_id=1, source_target_pairs={{0,2},{1,3},{2,0},{3,1},{4,6},{5,7},{6,4},{7,5},{8,10},{9,11},{10,... | collective-permute-start | bytes 393224 | tf_op jit(solution)/shard_map/ppermute | solution.py:338
  27.4 1.4 %shard_map.48.refs_0_ = bf16[2,8,32,128]{3,2,1,0:T(8,128)(2,1)S(1)} custom-call(s32[1]{0:T(128)} %bitcast.t, bf16[2,8,32,128]{3,2,1,0:T(8,128)(2,1)S(1)} %shard_map.47.own_ref, bf16[2,8,32,128]{3,2,1,0:T(8,128)(2,1)S(1)} %collective-permute-done.1.other_ref, bf16[12,128,32,128]{3,2,1,0:T(8,128)(2,1)S(1)} %bitcast.25, ...), custom_call_target="tpu_custom_call" | custom-call | bytes 5400000 | tf_op jit(solution)/shard_map/pallas_call | solution.py:77
  29.4 4.2 %collective-permute-done.9.refs_4_ = bf16[2,8,32,128]{3,2,1,0:T(8,128)(2,1)S(1)} collective-permute-done((bf16[2,8,32,128]{3,2,1,0:T(8,128)(2,1)S(1)}, bf16[2,8,32,128]{3,2,1,0:T(8,128)(2,1)S(1)}, u32[]{:S(2)}, u32[]{:S(2)}) %collective-permute-start.9) | collective-permute-done | bytes 131104 | tf_op jit(solution)/shard_map/ppermute | solution.py:338
  35.5 2.1 %shard_map.58 = (bf16[2,8,32,128]{3,2,1,0:T(8,128)(2,1)S(1)}, bf16[2,8,32,128]{3,2,1,0:T(8,128)(2,1)S(1)}, bf16[2,8,32,128]{3,2,1,0:T(8,128)(2,1)S(1)}, bf16[2,8,32,128]{3,2,1,0:T(8,128)(2,1)S(1)}) custom-call(s32[1]{0:T(128)} %bitcast.t, bf16[2,8,32,128]{3,2,1,0:T(8,128)(2,1)S(1)} %shard_map.48.refs_0_, ...), custom_call_target="tpu_custom_call" | custom-call | bytes 9000000 | tf_op jit(solution)/shard_map/pallas_call | solution.py:77
  39.8 2.1 %collective-permute-start.17 = (bf16[2,8,32,128]{3,2,1,0:T(8,128)(2,1)S(1)}, bf16[2,8,32,128]{3,2,1,0:T(8,128)(2,1)S(1)}, u32[]{:S(2)}, u32[]{:S(2)}) collective-permute-start(bf16[2,8,32,128]{3,2,1,0:T(8,128)(2,1)S(1)} %shard_map.60.own_ref), channel_id=1, source_target_pairs={{0,2},{1,3},{2,0},{3,1},{4,6},{5,7},{6,4},{7,5},{8,10},{9,11},{10,... | collective-permute-start | bytes 393224 | tf_op jit(solution)/shard_map/ppermute | solution.py:338
  42.6 2.1 %collective-permute-start.22 = (bf16[2,8,32,128]{3,2,1,0:T(8,128)(2,1)S(1)}, bf16[2,8,32,128]{3,2,1,0:T(8,128)(2,1)S(1)}, u32[]{:S(2)}, u32[]{:S(2)}) collective-permute-start(bf16[2,8,32,128]{3,2,1,0:T(8,128)(2,1)S(1)} %shard_map.64.own_ref), channel_id=1, source_target_pairs={{0,2},{1,3},{2,0},{3,1},{4,6},{5,7},{6,4},{7,5},{8,10},{9,11},{10,... | collective-permute-start | bytes 393224 | tf_op jit(solution)/shard_map/ppermute | solution.py:338
  45.8 0.8 %collective-permute-start.19 = (bf16[2,32,128]{2,1,0:T(8,128)(2,1)S(1)}, bf16[2,32,128]{2,1,0:T(8,128)(2,1)S(1)}, u32[]{:S(2)}, u32[]{:S(2)}) collective-permute-start(bf16[2,32,128]{2,1,0:T(8,128)(2,1)S(1)} %get-tuple-element.17), channel_id=1, source_target_pairs={{1,2},{3,4},{5,6},{2,1},{4,3},{6,5},{9,10},{11,12},{13,14},{10,9},... | collective-permute-start | bytes 49160 | tf_op jit(solution)/shard_map/ppermute | solution.py:385
  47.0 2.4 %collective-permute-start.28 = (bf16[2,8,32,128]{3,2,1,0:T(8,128)(2,1)S(1)}, bf16[2,8,32,128]{3,2,1,0:T(8,128)(2,1)S(1)}, u32[]{:S(2)}, u32[]{:S(2)}) collective-permute-start(bf16[2,8,32,128]{3,2,1,0:T(8,128)(2,1)S(1)} %shard_map.67.own_ref), channel_id=1, source_target_pairs={{0,4},{1,5},{2,6},{3,7},{4,0},{5,1},{6,2},{7,3},{8,12},{9,13},{10,... | collective-permute-start | bytes 393224 | tf_op jit(solution)/shard_map/ppermute | solution.py:338
  49.7 2.6 %collective-permute-start.27 = (bf16[2,8,32,128]{3,2,1,0:T(8,128)(2,1)S(1)}, bf16[2,8,32,128]{3,2,1,0:T(8,128)(2,1)S(1)}, u32[]{:S(2)}, u32[]{:S(2)}) collective-permute-start(bf16[2,8,32,128]{3,2,1,0:T(8,128)(2,1)S(1)} %shard_map.62.own_ref), channel_id=1, source_target_pairs={{0,4},{1,5},{2,6},{3,7},{4,0},{5,1},{6,2},{7,3},{8,12},{9,13},{10,... | collective-permute-start | bytes 393224 | tf_op jit(solution)/shard_map/ppermute | solution.py:338
  52.6 1.0 %collective-permute-start.26 = (bf16[2,8,32,128]{3,2,1,0:T(8,128)(2,1)S(1)}, bf16[2,8,32,128]{3,2,1,0:T(8,128)(2,1)S(1)}, u32[]{:S(2)}, u32[]{:S(2)}) collective-permute-start(bf16[2,8,32,128]{3,2,1,0:T(8,128)(2,1)S(1)} %shard_map.68.own_ref), channel_id=1, source_target_pairs={{0,4},{1,5},{2,6},{3,7},{4,0},{5,1},{6,2},{7,3},{8,12},{9,13},{10,... | collective-permute-start | bytes 393224 | tf_op jit(solution)/shard_map/ppermute | solution.py:338
  53.7 2.9 %collective-permute-done.22.other_ref = bf16[2,8,32,128]{3,2,1,0:T(8,128)(2,1)S(1)} collective-permute-done((bf16[2,8,32,128]{3,2,1,0:T(8,128)(2,1)S(1)}, bf16[2,8,32,128]{3,2,1,0:T(8,128)(2,1)S(1)}, u32[]{:S(2)}, u32[]{:S(2)}) %collective-permute-start.22) | collective-permute-done | bytes 131104 | tf_op jit(solution)/shard_map/ppermute | solution.py:338
  57.1 2.2 %copy-done.3 = bf16[1,128,32,512]{3,2,1,0:T(8,128)(2,1)S(1)} copy-done((bf16[1,128,32,512]{3,2,1,0:T(8,128)(2,1)S(1)}, bf16[1,128,32,512]{3,2,1,0:T(8,128)(2,1)}, u32[]{:S(2)}) %copy-start.3) | copy-done | bytes 4194328
  59.2 5.5 %shard_map.66.near_ref = f32[64,32,128]{2,1,0:T(8,128)S(1)} custom-call(s32[1]{0:T(128)} %bitcast.t, s32[128,8]{1,0:T(8,128)S(1)} %bitcast.48, bf16[2,8,32,128]{3,2,1,0:T(8,128)(2,1)S(1)} %shard_map.46.own_ref.refs_0_, bf16[2,8,32,128]{3,2,1,0:T(8,128)(2,1)S(1)} %shard_map.49.own_ref.refs_1_, bf16[2,8,32,128]{3,2,1,0:T(8,128)(2,1)S(1)} %shard_map.52.own_ref.refs_2_, ...), custom_call_target="tpu_custom_call" | custom-call | bytes 21600000 | tf_op jit(solution)/shard_map/pallas_call | solution.py:319
  64.8 1.2 %shard_map.69.rest_0_ = f32[128,2048]{1,0:T(8,128)} custom-call(s32[1]{0:T(128)} %bitcast.t, bf16[2,8,32,128]{3,2,1,0:T(8,128)(2,1)S(1)} %shard_map.68.own_ref, bf16[2,8,32,128]{3,2,1,0:T(8,128)(2,1)S(1)} %collective-permute-done.28.other_ref, bf16[1,128,32,128]{3,2,1,0:T(8,128)(2,1)S(1)} %get-tuple-element.23.w_ref, f32[64,32,128]{2,1,0:T(8,128)S(1)} %shard_map.66.near_ref), custom_call_target="tpu_custom_call" | custom-call | bytes 4320000 | tf_op jit(solution)/shard_map/pallas_call | solution.py:77
  66.0 2.1 %collective-permute-done.27.other_ref = bf16[2,8,32,128]{3,2,1,0:T(8,128)(2,1)S(1)} collective-permute-done((bf16[2,8,32,128]{3,2,1,0:T(8,128)(2,1)S(1)}, bf16[2,8,32,128]{3,2,1,0:T(8,128)(2,1)S(1)}, u32[]{:S(2)}, u32[]{:S(2)}) %collective-permute-start.27) | collective-permute-done | bytes 131104 | tf_op jit(solution)/shard_map/ppermute | solution.py:338
  68.1 1.2 %shard_map.70.rest_0_ = f32[128,2048]{1,0:T(8,128)} custom-call(s32[1]{0:T(128)} %bitcast.t, bf16[2,8,32,128]{3,2,1,0:T(8,128)(2,1)S(1)} %shard_map.65.own_ref, bf16[2,8,32,128]{3,2,1,0:T(8,128)(2,1)S(1)} %collective-permute-done.27.other_ref, bf16[1,128,32,128]{3,2,1,0:T(8,128)(2,1)S(1)} %get-tuple-element.23.w_ref, ...), custom_call_target="tpu_custom_call", output_to_operand_aliasing={{}: (5, {})} | custom-call | bytes 4320000 | tf_op jit(solution)/shard_map/pallas_call | solution.py:77
  69.3 1.6 %collective-permute-done.26.other_ref = bf16[2,8,32,128]{3,2,1,0:T(8,128)(2,1)S(1)} collective-permute-done((bf16[2,8,32,128]{3,2,1,0:T(8,128)(2,1)S(1)}, bf16[2,8,32,128]{3,2,1,0:T(8,128)(2,1)S(1)}, u32[]{:S(2)}, u32[]{:S(2)}) %collective-permute-start.26) | collective-permute-done | bytes 131104 | tf_op jit(solution)/shard_map/ppermute | solution.py:338
  70.9 1.2 %shard_map.71.rest_0_ = f32[128,2048]{1,0:T(8,128)} custom-call(s32[1]{0:T(128)} %bitcast.t, bf16[2,8,32,128]{3,2,1,0:T(8,128)(2,1)S(1)} %shard_map.67.own_ref, bf16[2,8,32,128]{3,2,1,0:T(8,128)(2,1)S(1)} %collective-permute-done.26.other_ref, bf16[1,128,32,128]{3,2,1,0:T(8,128)(2,1)S(1)} %get-tuple-element.23.w_ref, ...), custom_call_target="tpu_custom_call", output_to_operand_aliasing={{}: (5, {})} | custom-call | bytes 4320000 | tf_op jit(solution)/shard_map/pallas_call | solution.py:77
  72.1 1.6 %collective-permute-done.23.other_ref = bf16[2,8,32,128]{3,2,1,0:T(8,128)(2,1)S(1)} collective-permute-done((bf16[2,8,32,128]{3,2,1,0:T(8,128)(2,1)S(1)}, bf16[2,8,32,128]{3,2,1,0:T(8,128)(2,1)S(1)}, u32[]{:S(2)}, u32[]{:S(2)}) %collective-permute-start.23) | collective-permute-done | bytes 131104 | tf_op jit(solution)/shard_map/ppermute | solution.py:338
  73.7 1.2 %shard_map.72 = f32[128,2048]{1,0:T(8,128)} custom-call(s32[1]{0:T(128)} %bitcast.t, bf16[2,8,32,128]{3,2,1,0:T(8,128)(2,1)S(1)} %shard_map.62.own_ref, bf16[2,8,32,128]{3,2,1,0:T(8,128)(2,1)S(1)} %collective-permute-done.23.other_ref, bf16[1,128,32,128]{3,2,1,0:T(8,128)(2,1)S(1)} %get-tuple-element.23.w_ref, ...), custom_call_target="tpu_custom_call", output_to_operand_aliasing={{}: (5, {})} | custom-call | bytes 4320000 | tf_op jit(solution)/shard_map/pallas_call | solution.py:77
  (65 shorter events, 10.8 us)
Async XLA Ops:
  0.0 18.6 %copy-start = (bf16[12,1,128,32,128]{4,3,2,1,0:T(8,128)(2,1)S(1)}, bf16[12,1,128,32,128]{4,3,2,1,0:T(8,128)(2,1)}, u32[]{:S(2)}) copy-start(bf16[12,1,128,32,128]{4,3,2,1,0:T(8,128)(2,1)} %param.5) | copy-start | bytes 37748740
  1.5 7.9 %collective-permute-start.11 = (bf16[2,8,32,128]{3,2,1,0:T(8,128)(2,1)S(1)}, bf16[2,8,32,128]{3,2,1,0:T(8,128)(2,1)S(1)}, u32[]{:S(2)}, u32[]{:S(2)}) collective-permute-start(bf16[2,8,32,128]{3,2,1,0:T(8,128)(2,1)S(1)} %shard_map.55.own_ref.refs_3_), channel_id=1, source_target_pairs={{0,8},{8,0},{16,24},{24,16},{1,9},{9,1},{17,25},{25,17},{2,10},{10... | collective-permute-start | bytes 393224 | tf_op jit(solution)/shard_map/ppermute | solution.py:338
  4.7 7.1 %collective-permute-start.7 = (bf16[2,8,32,128]{3,2,1,0:T(8,128)(2,1)S(1)}, bf16[2,8,32,128]{3,2,1,0:T(8,128)(2,1)S(1)}, u32[]{:S(2)}, u32[]{:S(2)}) collective-permute-start(bf16[2,8,32,128]{3,2,1,0:T(8,128)(2,1)S(1)} %shard_map.52.own_ref.refs_2_), channel_id=1, source_target_pairs={{0,8},{8,0},{16,24},{24,16},{1,9},{9,1},{17,25},{25,17},{2,10},{10... | collective-permute-start | bytes 393224 | tf_op jit(solution)/shard_map/ppermute | solution.py:338
  5.1 9.3 %collective-permute-start.3 = (bf16[2,8,32,128]{3,2,1,0:T(8,128)(2,1)S(1)}, bf16[2,8,32,128]{3,2,1,0:T(8,128)(2,1)S(1)}, u32[]{:S(2)}, u32[]{:S(2)}) collective-permute-start(bf16[2,8,32,128]{3,2,1,0:T(8,128)(2,1)S(1)} %shard_map.49.own_ref.refs_1_), channel_id=1, source_target_pairs={{0,8},{8,0},{16,24},{24,16},{1,9},{9,1},{17,25},{25,17},{2,10},{10... | collective-permute-start | bytes 393224 | tf_op jit(solution)/shard_map/ppermute | solution.py:338
  7.4 9.5 %collective-permute-start = (bf16[2,8,32,128]{3,2,1,0:T(8,128)(2,1)S(1)}, bf16[2,8,32,128]{3,2,1,0:T(8,128)(2,1)S(1)}, u32[]{:S(2)}, u32[]{:S(2)}) collective-permute-start(bf16[2,8,32,128]{3,2,1,0:T(8,128)(2,1)S(1)} %shard_map.46.own_ref.refs_0_), channel_id=1, source_target_pairs={{0,8},{8,0},{16,24},{24,16},{1,9},{9,1},{17,25},{25,17},{2,10},{10... | collective-permute-start | bytes 393224 | tf_op jit(solution)/shard_map/ppermute | solution.py:338
  9.7 8.8 %collective-permute-start.12 = (bf16[2,8,32,128]{3,2,1,0:T(8,128)(2,1)S(1)}, bf16[2,8,32,128]{3,2,1,0:T(8,128)(2,1)S(1)}, u32[]{:S(2)}, u32[]{:S(2)}) collective-permute-start(bf16[2,8,32,128]{3,2,1,0:T(8,128)(2,1)S(1)} %shard_map.56.own_ref), channel_id=1, source_target_pairs={{0,16},{8,24},{16,0},{24,8},{1,17},{9,25},{17,1},{25,9},{2,18},{10... | collective-permute-start | bytes 393224 | tf_op jit(solution)/shard_map/ppermute | solution.py:338
  12.2 11.5 %collective-permute-start.8 = (bf16[2,8,32,128]{3,2,1,0:T(8,128)(2,1)S(1)}, bf16[2,8,32,128]{3,2,1,0:T(8,128)(2,1)S(1)}, u32[]{:S(2)}, u32[]{:S(2)}) collective-permute-start(bf16[2,8,32,128]{3,2,1,0:T(8,128)(2,1)S(1)} %shard_map.53.own_ref), channel_id=1, source_target_pairs={{0,16},{8,24},{16,0},{24,8},{1,17},{9,25},{17,1},{25,9},{2,18},{10... | collective-permute-start | bytes 393224 | tf_op jit(solution)/shard_map/ppermute | solution.py:338
  14.7 10.4 %collective-permute-start.4 = (bf16[2,8,32,128]{3,2,1,0:T(8,128)(2,1)S(1)}, bf16[2,8,32,128]{3,2,1,0:T(8,128)(2,1)S(1)}, u32[]{:S(2)}, u32[]{:S(2)}) collective-permute-start(bf16[2,8,32,128]{3,2,1,0:T(8,128)(2,1)S(1)} %shard_map.50.own_ref), channel_id=1, source_target_pairs={{0,16},{8,24},{16,0},{24,8},{1,17},{9,25},{17,1},{25,9},{2,18},{10... | collective-permute-start | bytes 393224 | tf_op jit(solution)/shard_map/ppermute | solution.py:338
  17.2 10.2 %collective-permute-start.1 = (bf16[2,8,32,128]{3,2,1,0:T(8,128)(2,1)S(1)}, bf16[2,8,32,128]{3,2,1,0:T(8,128)(2,1)S(1)}, u32[]{:S(2)}, u32[]{:S(2)}) collective-permute-start(bf16[2,8,32,128]{3,2,1,0:T(8,128)(2,1)S(1)} %shard_map.47.own_ref), channel_id=1, source_target_pairs={{0,16},{8,24},{16,0},{24,8},{1,17},{9,25},{17,1},{25,9},{2,18},{10... | collective-permute-start | bytes 393224 | tf_op jit(solution)/shard_map/ppermute | solution.py:338
  20.0 9.0 %collective-permute-start.13 = (bf16[2,8,32,128]{3,2,1,0:T(8,128)(2,1)S(1)}, bf16[2,8,32,128]{3,2,1,0:T(8,128)(2,1)S(1)}, u32[]{:S(2)}, u32[]{:S(2)}) collective-permute-start(bf16[2,8,32,128]{3,2,1,0:T(8,128)(2,1)S(1)} %shard_map.57), channel_id=1, source_target_pairs={{0,6},{1,7},{2,4},{3,5},{4,2},{5,3},{6,0},{7,1},{8,14},{9,15},{10,... | collective-permute-start | bytes 393224 | tf_op jit(solution)/shard_map/ppermute | solution.py:338
  25.1 8.6 %collective-permute-start.9 = (bf16[2,8,32,128]{3,2,1,0:T(8,128)(2,1)S(1)}, bf16[2,8,32,128]{3,2,1,0:T(8,128)(2,1)S(1)}, u32[]{:S(2)}, u32[]{:S(2)}) collective-permute-start(bf16[2,8,32,128]{3,2,1,0:T(8,128)(2,1)S(1)} %shard_map.54), channel_id=1, source_target_pairs={{0,4},{1,5},{2,6},{3,7},{4,0},{5,1},{6,2},{7,3},{8,12},{9,13},{10,... | collective-permute-start | bytes 393224 | tf_op jit(solution)/shard_map/ppermute | solution.py:338
  26.6 7.6 %collective-permute-start.5 = (bf16[2,8,32,128]{3,2,1,0:T(8,128)(2,1)S(1)}, bf16[2,8,32,128]{3,2,1,0:T(8,128)(2,1)S(1)}, u32[]{:S(2)}, u32[]{:S(2)}) collective-permute-start(bf16[2,8,32,128]{3,2,1,0:T(8,128)(2,1)S(1)} %shard_map.51), channel_id=1, source_target_pairs={{0,2},{1,3},{2,0},{3,1},{4,6},{5,7},{6,4},{7,5},{8,10},{9,11},{10,... | collective-permute-start | bytes 393224 | tf_op jit(solution)/shard_map/ppermute | solution.py:338
  28.9 5.3 %collective-permute-start.2 = (bf16[2,8,32,128]{3,2,1,0:T(8,128)(2,1)S(1)}, bf16[2,8,32,128]{3,2,1,0:T(8,128)(2,1)S(1)}, u32[]{:S(2)}, u32[]{:S(2)}) collective-permute-start(bf16[2,8,32,128]{3,2,1,0:T(8,128)(2,1)S(1)} %shard_map.48.refs_0_), channel_id=1, source_target_pairs={{0,1},{1,0},{2,3},{3,2},{4,5},{5,4},{6,7},{7,6},{8,9},{9,8},{10,11... | collective-permute-start | bytes 393224 | tf_op jit(solution)/shard_map/ppermute | solution.py:338
  28.9 5.2 %collective-permute-start.14 = (bf16[2,8,32,128]{3,2,1,0:T(8,128)(2,1)S(1)}, bf16[2,8,32,128]{3,2,1,0:T(8,128)(2,1)S(1)}, u32[]{:S(2)}, u32[]{:S(2)}) collective-permute-start(bf16[2,8,32,128]{3,2,1,0:T(8,128)(2,1)S(1)} %collective-permute-done.13.refs_6_), channel_id=1, source_target_pairs={{0,1},{1,0},{2,3},{3,2},{4,5},{5,4},{6,7},{7,6},{8,9},{9,8},{10,11... | collective-permute-start | bytes 393224 | tf_op jit(solution)/shard_map/ppermute | solution.py:338
  33.7 1.3 %collective-permute-start.10 = (bf16[2,8,32,128]{3,2,1,0:T(8,128)(2,1)S(1)}, bf16[2,8,32,128]{3,2,1,0:T(8,128)(2,1)S(1)}, u32[]{:S(2)}, u32[]{:S(2)}) collective-permute-start(bf16[2,8,32,128]{3,2,1,0:T(8,128)(2,1)S(1)} %collective-permute-done.9.refs_4_), channel_id=1, source_target_pairs={{0,1},{1,0},{2,3},{3,2},{4,5},{5,4},{6,7},{7,6},{8,9},{9,8},{10,11... | collective-permute-start | bytes 393224 | tf_op jit(solution)/shard_map/ppermute | solution.py:338
  34.2 1.3 %collective-permute-start.6 = (bf16[2,8,32,128]{3,2,1,0:T(8,128)(2,1)S(1)}, bf16[2,8,32,128]{3,2,1,0:T(8,128)(2,1)S(1)}, u32[]{:S(2)}, u32[]{:S(2)}) collective-permute-start(bf16[2,8,32,128]{3,2,1,0:T(8,128)(2,1)S(1)} %collective-permute-done.5.refs_2_), channel_id=1, source_target_pairs={{0,1},{1,0},{2,3},{3,2},{4,5},{5,4},{6,7},{7,6},{8,9},{9,8},{10,11... | collective-permute-start | bytes 393224 | tf_op jit(solution)/shard_map/ppermute | solution.py:338
  37.6 1.4 %collective-permute-start.15 = (bf16[2,8,32,128]{3,2,1,0:T(8,128)(2,1)S(1)}, bf16[2,8,32,128]{3,2,1,0:T(8,128)(2,1)S(1)}, u32[]{:S(2)}, u32[]{:S(2)}) collective-permute-start(bf16[2,8,32,128]{3,2,1,0:T(8,128)(2,1)S(1)} %get-tuple-element.14.own_ref), channel_id=1, source_target_pairs={{0,1},{1,0},{2,3},{3,2},{4,5},{5,4},{6,7},{7,6},{8,9},{9,8},{10,11... | collective-permute-start | bytes 393224 | tf_op jit(solution)/shard_map/ppermute | solution.py:338
  37.8 1.6 %collective-permute-start.16 = (bf16[2,8,32,128]{3,2,1,0:T(8,128)(2,1)S(1)}, bf16[2,8,32,128]{3,2,1,0:T(8,128)(2,1)S(1)}, u32[]{:S(2)}, u32[]{:S(2)}) collective-permute-start(bf16[2,8,32,128]{3,2,1,0:T(8,128)(2,1)S(1)} %get-tuple-element.15.own_ref), channel_id=1, source_target_pairs={{0,1},{1,0},{2,3},{3,2},{4,5},{5,4},{6,7},{7,6},{8,9},{9,8},{10,11... | collective-permute-start | bytes 393224 | tf_op jit(solution)/shard_map/ppermute | solution.py:338
  38.2 3.7 %collective-permute-start.20 = (bf16[2,8,32,128]{3,2,1,0:T(8,128)(2,1)S(1)}, bf16[2,8,32,128]{3,2,1,0:T(8,128)(2,1)S(1)}, u32[]{:S(2)}, u32[]{:S(2)}) collective-permute-start(bf16[2,8,32,128]{3,2,1,0:T(8,128)(2,1)S(1)} %get-tuple-element.19.own_ref), channel_id=1, source_target_pairs={{0,1},{1,0},{2,3},{3,2},{4,5},{5,4},{6,7},{7,6},{8,9},{9,8},{10,11... | collective-permute-start | bytes 393224 | tf_op jit(solution)/shard_map/ppermute | solution.py:338
  38.3 4.0 %collective-permute-start.21 = (bf16[2,8,32,128]{3,2,1,0:T(8,128)(2,1)S(1)}, bf16[2,8,32,128]{3,2,1,0:T(8,128)(2,1)S(1)}, u32[]{:S(2)}, u32[]{:S(2)}) collective-permute-start(bf16[2,8,32,128]{3,2,1,0:T(8,128)(2,1)S(1)} %get-tuple-element.20.own_ref), channel_id=1, source_target_pairs={{0,1},{1,0},{2,3},{3,2},{4,5},{5,4},{6,7},{7,6},{8,9},{9,8},{10,11... | collective-permute-start | bytes 393224 | tf_op jit(solution)/shard_map/ppermute | solution.py:338
  39.4 6.4 %collective-permute-start.24 = (bf16[2,8,32,128]{3,2,1,0:T(8,128)(2,1)S(1)}, bf16[2,8,32,128]{3,2,1,0:T(8,128)(2,1)S(1)}, u32[]{:S(2)}, u32[]{:S(2)}) collective-permute-start(bf16[2,8,32,128]{3,2,1,0:T(8,128)(2,1)S(1)} %shard_map.59.own_ref), channel_id=1, source_target_pairs={{0,2},{1,3},{2,0},{3,1},{4,6},{5,7},{6,4},{7,5},{8,10},{9,11},{10,... | collective-permute-start | bytes 393224 | tf_op jit(solution)/shard_map/ppermute | solution.py:338
  39.8 4.9 %copy-start.2 = (bf16[1,128,2048]{2,1,0:T(8,128)(2,1)S(1)}, bf16[1,128,2048]{2,1,0:T(8,128)(2,1)}, u32[]{:S(2)}) copy-start(bf16[1,128,2048]{2,1,0:T(8,128)(2,1)} %param.4) | copy-start | bytes 1572868
  39.8 9.5 %collective-permute-start.17 = (bf16[2,8,32,128]{3,2,1,0:T(8,128)(2,1)S(1)}, bf16[2,8,32,128]{3,2,1,0:T(8,128)(2,1)S(1)}, u32[]{:S(2)}, u32[]{:S(2)}) collective-permute-start(bf16[2,8,32,128]{3,2,1,0:T(8,128)(2,1)S(1)} %shard_map.60.own_ref), channel_id=1, source_target_pairs={{0,2},{1,3},{2,0},{3,1},{4,6},{5,7},{6,4},{7,5},{8,10},{9,11},{10,... | collective-permute-start | bytes 393224 | tf_op jit(solution)/shard_map/ppermute | solution.py:338
  42.2 10.1 %collective-permute-start.25 = (bf16[2,8,32,128]{3,2,1,0:T(8,128)(2,1)S(1)}, bf16[2,8,32,128]{3,2,1,0:T(8,128)(2,1)S(1)}, u32[]{:S(2)}, u32[]{:S(2)}) collective-permute-start(bf16[2,8,32,128]{3,2,1,0:T(8,128)(2,1)S(1)} %shard_map.63.own_ref), channel_id=1, source_target_pairs={{0,2},{1,3},{2,0},{3,1},{4,6},{5,7},{6,4},{7,5},{8,10},{9,11},{10,... | collective-permute-start | bytes 393224 | tf_op jit(solution)/shard_map/ppermute | solution.py:338
  42.6 13.9 %collective-permute-start.22 = (bf16[2,8,32,128]{3,2,1,0:T(8,128)(2,1)S(1)}, bf16[2,8,32,128]{3,2,1,0:T(8,128)(2,1)S(1)}, u32[]{:S(2)}, u32[]{:S(2)}) collective-permute-start(bf16[2,8,32,128]{3,2,1,0:T(8,128)(2,1)S(1)} %shard_map.64.own_ref), channel_id=1, source_target_pairs={{0,2},{1,3},{2,0},{3,1},{4,6},{5,7},{6,4},{7,5},{8,10},{9,11},{10,... | collective-permute-start | bytes 393224 | tf_op jit(solution)/shard_map/ppermute | solution.py:338
  44.9 2.1 %collective-permute-start.18 = (bf16[2,32,128]{2,1,0:T(8,128)(2,1)S(1)}, bf16[2,32,128]{2,1,0:T(8,128)(2,1)S(1)}, u32[]{:S(2)}, u32[]{:S(2)}) collective-permute-start(bf16[2,32,128]{2,1,0:T(8,128)(2,1)S(1)} %get-tuple-element.16), channel_id=1, source_target_pairs={{0,1},{1,0},{2,3},{3,2},{4,5},{5,4},{6,7},{7,6},{8,9},{9,8},{10,11... | collective-permute-start | bytes 49160 | tf_op jit(solution)/shard_map/ppermute | solution.py:338
  45.8 3.6 %collective-permute-start.19 = (bf16[2,32,128]{2,1,0:T(8,128)(2,1)S(1)}, bf16[2,32,128]{2,1,0:T(8,128)(2,1)S(1)}, u32[]{:S(2)}, u32[]{:S(2)}) collective-permute-start(bf16[2,32,128]{2,1,0:T(8,128)(2,1)S(1)} %get-tuple-element.17), channel_id=1, source_target_pairs={{1,2},{3,4},{5,6},{2,1},{4,3},{6,5},{9,10},{11,12},{13,14},{10,9},... | collective-permute-start | bytes 49160 | tf_op jit(solution)/shard_map/ppermute | solution.py:385
  47.0 17.8 %collective-permute-start.28 = (bf16[2,8,32,128]{3,2,1,0:T(8,128)(2,1)S(1)}, bf16[2,8,32,128]{3,2,1,0:T(8,128)(2,1)S(1)}, u32[]{:S(2)}, u32[]{:S(2)}) collective-permute-start(bf16[2,8,32,128]{3,2,1,0:T(8,128)(2,1)S(1)} %shard_map.67.own_ref), channel_id=1, source_target_pairs={{0,4},{1,5},{2,6},{3,7},{4,0},{5,1},{6,2},{7,3},{8,12},{9,13},{10,... | collective-permute-start | bytes 393224 | tf_op jit(solution)/shard_map/ppermute | solution.py:338
  49.7 7.3 %copy-start.4 = (s32[1,128,8]{1,2,0:T(8,128)S(1)}, s32[1,128,8]{1,2,0:T(8,128)}, u32[]{:S(2)}) copy-start(s32[1,128,8]{1,2,0:T(8,128)} %param.7) | copy-start | bytes 12292
  49.7 18.4 %collective-permute-start.27 = (bf16[2,8,32,128]{3,2,1,0:T(8,128)(2,1)S(1)}, bf16[2,8,32,128]{3,2,1,0:T(8,128)(2,1)S(1)}, u32[]{:S(2)}, u32[]{:S(2)}) collective-permute-start(bf16[2,8,32,128]{3,2,1,0:T(8,128)(2,1)S(1)} %shard_map.62.own_ref), channel_id=1, source_target_pairs={{0,4},{1,5},{2,6},{3,7},{4,0},{5,1},{6,2},{7,3},{8,12},{9,13},{10,... | collective-permute-start | bytes 393224 | tf_op jit(solution)/shard_map/ppermute | solution.py:338
  52.6 18.3 %collective-permute-start.26 = (bf16[2,8,32,128]{3,2,1,0:T(8,128)(2,1)S(1)}, bf16[2,8,32,128]{3,2,1,0:T(8,128)(2,1)S(1)}, u32[]{:S(2)}, u32[]{:S(2)}) collective-permute-start(bf16[2,8,32,128]{3,2,1,0:T(8,128)(2,1)S(1)} %shard_map.68.own_ref), channel_id=1, source_target_pairs={{0,4},{1,5},{2,6},{3,7},{4,0},{5,1},{6,2},{7,3},{8,12},{9,13},{10,... | collective-permute-start | bytes 393224 | tf_op jit(solution)/shard_map/ppermute | solution.py:338
  56.9 16.8 %collective-permute-start.23 = (bf16[2,8,32,128]{3,2,1,0:T(8,128)(2,1)S(1)}, bf16[2,8,32,128]{3,2,1,0:T(8,128)(2,1)S(1)}, u32[]{:S(2)}, u32[]{:S(2)}) collective-permute-start(bf16[2,8,32,128]{3,2,1,0:T(8,128)(2,1)S(1)} %shard_map.65.own_ref), channel_id=1, source_target_pairs={{0,4},{1,5},{2,6},{3,7},{4,0},{5,1},{6,2},{7,3},{8,12},{9,13},{10,... | collective-permute-start | bytes 393224 | tf_op jit(solution)/shard_map/ppermute | solution.py:338
  (2 other events, 3.4 us)

commit v4 on v3

--- a/solution.py
+++ b/solution.py
@@ -199,7 +199,7 @@
     outs = refs[groups + bits : groups + bits + groups // G]
     half = lows // 2
 
-    width = max(1, min(half, 32 // groups))
+    width = max(1, min(half, 64 // groups))
     keys = [(k, g) for k in range(width) for g in range(groups)]
 
     def body(step, carry):

time: 75.1 us -> 74.9 us (level)
  no operation moved by 1% of the time
where the time goes in v4:
time: 74.9 us; the launch traced here: 74.7 us
  starting transfers between devices  30.2 us (40%)
  Pallas kernels  23 us (31%)
  waiting for transfers between devices  15.7 us (21%)
  local copies, waits for them, and re-layouts  5.39 us (7%)
    ppermute x28, starting transfers between devices, swapped_with(): return lax.ppermute(x, axis, [(i, i ^ distance) for i in range(count)])  29.4 us
    pallas_call x25, Pallas kernels, call(): pl.pallas_call(kernel, out_shape=out_shapes, grid_spec=pltpu.PrefetchScal...  17.4 us
    ppermute x28, waiting for transfers between devices, swapped_with(): return lax.ppermute(x, axis, [(i, i ^ distance) for i in range(count)])  15.7 us
    pallas_call x1, Pallas kernels, near_field(): pl.pallas_call(functools.partial(near_kernel, G, lows, len(chunks), count...  5.5 us
    unnamed x11, local copies, waits for them, and re-layouts  3.49 us
    squeeze x1, local copies, waits for them, and re-layouts, per_device(): ends = {0: factors[:1, 0], factors.shape[0] - 1: factors[-1:, 0]}  1.9 us
  transfers between devices with their start and end apart: 29, of which 11 were waited for; matrix products, arithmetic and copies ran while one was open for 3% of the time, Pallas kernels for 26%

profile of v4, /device:TPU:0, one launch (start us, length us, event | category | flops | bytes accessed | tf_op | source)
XLA Modules:
  0.0 74.7 jit_solution(7103001255835402450)
XLA Ops:
  0.0 1.2 %copy-done.1 = bf16[1,128,2048]{2,1,0:T(8,128)(2,1)S(1)} copy-done((bf16[1,128,2048]{2,1,0:T(8,128)(2,1)S(1)}, bf16[1,128,2048]{2,1,0:T(8,128)(2,1)}, u32[]{:S(2)}) %copy-start.1) | copy-done | bytes 524312
  1.5 3.0 %collective-permute-start.11 = (bf16[2,8,32,128]{3,2,1,0:T(8,128)(2,1)S(1)}, bf16[2,8,32,128]{3,2,1,0:T(8,128)(2,1)S(1)}, u32[]{:S(2)}, u32[]{:S(2)}) collective-permute-start(bf16[2,8,32,128]{3,2,1,0:T(8,128)(2,1)S(1)} %shard_map.55.own_ref.refs_3_), channel_id=1, source_target_pairs={{0,8},{8,0},{16,24},{24,16},{1,9},{9,1},{17,25},{25,17},{2,10},{10... | collective-permute-start | bytes 393224 | tf_op jit(solution)/shard_map/ppermute | solution.py:338
  5.1 2.1 %collective-permute-start.3 = (bf16[2,8,32,128]{3,2,1,0:T(8,128)(2,1)S(1)}, bf16[2,8,32,128]{3,2,1,0:T(8,128)(2,1)S(1)}, u32[]{:S(2)}, u32[]{:S(2)}) collective-permute-start(bf16[2,8,32,128]{3,2,1,0:T(8,128)(2,1)S(1)} %shard_map.49.own_ref.refs_1_), channel_id=1, source_target_pairs={{0,8},{8,0},{16,24},{24,16},{1,9},{9,1},{17,25},{25,17},{2,10},{10... | collective-permute-start | bytes 393224 | tf_op jit(solution)/shard_map/ppermute | solution.py:338
  7.5 1.9 %slice_bitcast_fusion = (bf16[1,128,32,128]{3,2,1,0:T(8,128)(2,1)S(1)}, bf16[1,128,32,128]{3,2,1,0:T(8,128)(2,1)S(1)}) fusion(bf16[12,1,128,32,128]{4,3,2,1,0:T(8,128)(2,1)} %param.5), kind=kLoop, calls=%fused_computation | loop fusion | bytes 4194304 | tf_op jit(solution)/shard_map/squeeze | solution.py:355
  9.7 2.1 %collective-permute-start.12 = (bf16[2,8,32,128]{3,2,1,0:T(8,128)(2,1)S(1)}, bf16[2,8,32,128]{3,2,1,0:T(8,128)(2,1)S(1)}, u32[]{:S(2)}, u32[]{:S(2)}) collective-permute-start(bf16[2,8,32,128]{3,2,1,0:T(8,128)(2,1)S(1)} %shard_map.56.own_ref), channel_id=1, source_target_pairs={{0,16},{8,24},{16,0},{24,8},{1,17},{9,25},{17,1},{25,9},{2,18},{10... | collective-permute-start | bytes 393224 | tf_op jit(solution)/shard_map/ppermute | solution.py:338
  12.2 1.9 %collective-permute-start.8 = (bf16[2,8,32,128]{3,2,1,0:T(8,128)(2,1)S(1)}, bf16[2,8,32,128]{3,2,1,0:T(8,128)(2,1)S(1)}, u32[]{:S(2)}, u32[]{:S(2)}) collective-permute-start(bf16[2,8,32,128]{3,2,1,0:T(8,128)(2,1)S(1)} %shard_map.53.own_ref), channel_id=1, source_target_pairs={{0,16},{8,24},{16,0},{24,8},{1,17},{9,25},{17,1},{25,9},{2,18},{10... | collective-permute-start | bytes 393224 | tf_op jit(solution)/shard_map/ppermute | solution.py:338
  14.7 2.1 %collective-permute-start.4 = (bf16[2,8,32,128]{3,2,1,0:T(8,128)(2,1)S(1)}, bf16[2,8,32,128]{3,2,1,0:T(8,128)(2,1)S(1)}, u32[]{:S(2)}, u32[]{:S(2)}) collective-permute-start(bf16[2,8,32,128]{3,2,1,0:T(8,128)(2,1)S(1)} %shard_map.50.own_ref), channel_id=1, source_target_pairs={{0,16},{8,24},{16,0},{24,8},{1,17},{9,25},{17,1},{25,9},{2,18},{10... | collective-permute-start | bytes 393224 | tf_op jit(solution)/shard_map/ppermute | solution.py:338
  17.2 1.3 %collective-permute-start.1 = (bf16[2,8,32,128]{3,2,1,0:T(8,128)(2,1)S(1)}, bf16[2,8,32,128]{3,2,1,0:T(8,128)(2,1)S(1)}, u32[]{:S(2)}, u32[]{:S(2)}) collective-permute-start(bf16[2,8,32,128]{3,2,1,0:T(8,128)(2,1)S(1)} %shard_map.47.own_ref), channel_id=1, source_target_pairs={{0,16},{8,24},{16,0},{24,8},{1,17},{9,25},{17,1},{25,9},{2,18},{10... | collective-permute-start | bytes 393224 | tf_op jit(solution)/shard_map/ppermute | solution.py:338
  18.6 1.4 %shard_map.57 = bf16[2,8,32,128]{3,2,1,0:T(8,128)(2,1)S(1)} custom-call(s32[1]{0:T(128)} %bitcast.t, bf16[2,8,32,128]{3,2,1,0:T(8,128)(2,1)S(1)} %shard_map.56.own_ref, bf16[2,8,32,128]{3,2,1,0:T(8,128)(2,1)S(1)} %collective-permute-done.12.other_ref, bf16[12,128,32,128]{3,2,1,0:T(8,128)(2,1)S(1)} %bitcast.10, bf16[12,128,32,128]{3,2,1,0:T(8,128)(2,1)S(1)} %bitcast.11, ...), custom_call_target="tpu_custom_call" | custom-call | bytes 5400000 | tf_op jit(solution)/shard_map/pallas_call | solution.py:77
  20.0 3.7 %collective-permute-start.13 = (bf16[2,8,32,128]{3,2,1,0:T(8,128)(2,1)S(1)}, bf16[2,8,32,128]{3,2,1,0:T(8,128)(2,1)S(1)}, u32[]{:S(2)}, u32[]{:S(2)}) collective-permute-start(bf16[2,8,32,128]{3,2,1,0:T(8,128)(2,1)S(1)} %shard_map.57), channel_id=1, source_target_pairs={{0,6},{1,7},{2,4},{3,5},{4,2},{5,3},{6,0},{7,1},{8,14},{9,15},{10,... | collective-permute-start | bytes 393224 | tf_op jit(solution)/shard_map/ppermute | solution.py:338
  23.7 1.4 %shard_map.54 = bf16[2,8,32,128]{3,2,1,0:T(8,128)(2,1)S(1)} custom-call(s32[1]{0:T(128)} %bitcast.t, bf16[2,8,32,128]{3,2,1,0:T(8,128)(2,1)S(1)} %shard_map.53.own_ref, bf16[2,8,32,128]{3,2,1,0:T(8,128)(2,1)S(1)} %collective-permute-done.8.other_ref, bf16[12,128,32,128]{3,2,1,0:T(8,128)(2,1)S(1)} %bitcast.15, bf16[12,128,32,128]{3,2,1,0:T(8,128)(2,1)S(1)} %bitcast.16, ...), custom_call_target="tpu_custom_call" | custom-call | bytes 5400000 | tf_op jit(solution)/shard_map/pallas_call | solution.py:77
  25.2 1.4 %shard_map.51 = bf16[2,8,32,128]{3,2,1,0:T(8,128)(2,1)S(1)} custom-call(s32[1]{0:T(128)} %bitcast.t, bf16[2,8,32,128]{3,2,1,0:T(8,128)(2,1)S(1)} %shard_map.50.own_ref, bf16[2,8,32,128]{3,2,1,0:T(8,128)(2,1)S(1)} %collective-permute-done.4.other_ref, bf16[12,128,32,128]{3,2,1,0:T(8,128)(2,1)S(1)} %bitcast.24, bf16[12,128,32,128]{3,2,1,0:T(8,128)(2,1)S(1)} %bitcast.21, ...), custom_call_target="tpu_custom_call" | custom-call | bytes 5400000 | tf_op jit(solution)/shard_map/pallas_call | solution.py:77
  26.6 0.8 %collective-permute-start.5 = (bf16[2,8,32,128]{3,2,1,0:T(8,128)(2,1)S(1)}, bf16[2,8,32,128]{3,2,1,0:T(8,128)(2,1)S(1)}, u32[]{:S(2)}, u32[]{:S(2)}) collective-permute-start(bf16[2,8,32,128]{3,2,1,0:T(8,128)(2,1)S(1)} %shard_map.51), channel_id=1, source_target_pairs={{0,2},{1,3},{2,0},{3,1},{4,6},{5,7},{6,4},{7,5},{8,10},{9,11},{10,... | collective-permute-start | bytes 393224 | tf_op jit(solution)/shard_map/ppermute | solution.py:338
  27.4 1.4 %shard_map.48.refs_0_ = bf16[2,8,32,128]{3,2,1,0:T(8,128)(2,1)S(1)} custom-call(s32[1]{0:T(128)} %bitcast.t, bf16[2,8,32,128]{3,2,1,0:T(8,128)(2,1)S(1)} %shard_map.47.own_ref, bf16[2,8,32,128]{3,2,1,0:T(8,128)(2,1)S(1)} %collective-permute-done.1.other_ref, bf16[12,128,32,128]{3,2,1,0:T(8,128)(2,1)S(1)} %bitcast.25, ...), custom_call_target="tpu_custom_call" | custom-call | bytes 5400000 | tf_op jit(solution)/shard_map/pallas_call | solution.py:77
  29.4 4.2 %collective-permute-done.9.refs_4_ = bf16[2,8,32,128]{3,2,1,0:T(8,128)(2,1)S(1)} collective-permute-done((bf16[2,8,32,128]{3,2,1,0:T(8,128)(2,1)S(1)}, bf16[2,8,32,128]{3,2,1,0:T(8,128)(2,1)S(1)}, u32[]{:S(2)}, u32[]{:S(2)}) %collective-permute-start.9) | collective-permute-done | bytes 131104 | tf_op jit(solution)/shard_map/ppermute | solution.py:338
  35.5 1.9 %shard_map.58 = (bf16[2,8,32,128]{3,2,1,0:T(8,128)(2,1)S(1)}, bf16[2,8,32,128]{3,2,1,0:T(8,128)(2,1)S(1)}, bf16[2,8,32,128]{3,2,1,0:T(8,128)(2,1)S(1)}, bf16[2,8,32,128]{3,2,1,0:T(8,128)(2,1)S(1)}) custom-call(s32[1]{0:T(128)} %bitcast.t, bf16[2,8,32,128]{3,2,1,0:T(8,128)(2,1)S(1)} %shard_map.48.refs_0_, ...), custom_call_target="tpu_custom_call" | custom-call | bytes 9000000 | tf_op jit(solution)/shard_map/pallas_call | solution.py:77
  39.6 2.1 %collective-permute-start.17 = (bf16[2,8,32,128]{3,2,1,0:T(8,128)(2,1)S(1)}, bf16[2,8,32,128]{3,2,1,0:T(8,128)(2,1)S(1)}, u32[]{:S(2)}, u32[]{:S(2)}) collective-permute-start(bf16[2,8,32,128]{3,2,1,0:T(8,128)(2,1)S(1)} %shard_map.60.own_ref), channel_id=1, source_target_pairs={{0,2},{1,3},{2,0},{3,1},{4,6},{5,7},{6,4},{7,5},{8,10},{9,11},{10,... | collective-permute-start | bytes 393224 | tf_op jit(solution)/shard_map/ppermute | solution.py:338
  42.4 2.1 %collective-permute-start.22 = (bf16[2,8,32,128]{3,2,1,0:T(8,128)(2,1)S(1)}, bf16[2,8,32,128]{3,2,1,0:T(8,128)(2,1)S(1)}, u32[]{:S(2)}, u32[]{:S(2)}) collective-permute-start(bf16[2,8,32,128]{3,2,1,0:T(8,128)(2,1)S(1)} %shard_map.64.own_ref), channel_id=1, source_target_pairs={{0,2},{1,3},{2,0},{3,1},{4,6},{5,7},{6,4},{7,5},{8,10},{9,11},{10,... | collective-permute-start | bytes 393224 | tf_op jit(solution)/shard_map/ppermute | solution.py:338
  45.6 0.8 %collective-permute-start.19 = (bf16[2,32,128]{2,1,0:T(8,128)(2,1)S(1)}, bf16[2,32,128]{2,1,0:T(8,128)(2,1)S(1)}, u32[]{:S(2)}, u32[]{:S(2)}) collective-permute-start(bf16[2,32,128]{2,1,0:T(8,128)(2,1)S(1)} %get-tuple-element.17), channel_id=1, source_target_pairs={{1,2},{3,4},{5,6},{2,1},{4,3},{6,5},{9,10},{11,12},{13,14},{10,9},... | collective-permute-start | bytes 49160 | tf_op jit(solution)/shard_map/ppermute | solution.py:385
  46.8 2.4 %collective-permute-start.28 = (bf16[2,8,32,128]{3,2,1,0:T(8,128)(2,1)S(1)}, bf16[2,8,32,128]{3,2,1,0:T(8,128)(2,1)S(1)}, u32[]{:S(2)}, u32[]{:S(2)}) collective-permute-start(bf16[2,8,32,128]{3,2,1,0:T(8,128)(2,1)S(1)} %shard_map.67.own_ref), channel_id=1, source_target_pairs={{0,4},{1,5},{2,6},{3,7},{4,0},{5,1},{6,2},{7,3},{8,12},{9,13},{10,... | collective-permute-start | bytes 393224 | tf_op jit(solution)/shard_map/ppermute | solution.py:338
  49.5 2.6 %collective-permute-start.27 = (bf16[2,8,32,128]{3,2,1,0:T(8,128)(2,1)S(1)}, bf16[2,8,32,128]{3,2,1,0:T(8,128)(2,1)S(1)}, u32[]{:S(2)}, u32[]{:S(2)}) collective-permute-start(bf16[2,8,32,128]{3,2,1,0:T(8,128)(2,1)S(1)} %shard_map.62.own_ref), channel_id=1, source_target_pairs={{0,4},{1,5},{2,6},{3,7},{4,0},{5,1},{6,2},{7,3},{8,12},{9,13},{10,... | collective-permute-start | bytes 393224 | tf_op jit(solution)/shard_map/ppermute | solution.py:338
  52.4 1.0 %collective-permute-start.26 = (bf16[2,8,32,128]{3,2,1,0:T(8,128)(2,1)S(1)}, bf16[2,8,32,128]{3,2,1,0:T(8,128)(2,1)S(1)}, u32[]{:S(2)}, u32[]{:S(2)}) collective-permute-start(bf16[2,8,32,128]{3,2,1,0:T(8,128)(2,1)S(1)} %shard_map.68.own_ref), channel_id=1, source_target_pairs={{0,4},{1,5},{2,6},{3,7},{4,0},{5,1},{6,2},{7,3},{8,12},{9,13},{10,... | collective-permute-start | bytes 393224 | tf_op jit(solution)/shard_map/ppermute | solution.py:338
  53.5 2.9 %collective-permute-done.22.other_ref = bf16[2,8,32,128]{3,2,1,0:T(8,128)(2,1)S(1)} collective-permute-done((bf16[2,8,32,128]{3,2,1,0:T(8,128)(2,1)S(1)}, bf16[2,8,32,128]{3,2,1,0:T(8,128)(2,1)S(1)}, u32[]{:S(2)}, u32[]{:S(2)}) %collective-permute-start.22) | collective-permute-done | bytes 131104 | tf_op jit(solution)/shard_map/ppermute | solution.py:338
  56.9 2.2 %copy-done.3 = bf16[1,128,32,512]{3,2,1,0:T(8,128)(2,1)S(1)} copy-done((bf16[1,128,32,512]{3,2,1,0:T(8,128)(2,1)S(1)}, bf16[1,128,32,512]{3,2,1,0:T(8,128)(2,1)}, u32[]{:S(2)}) %copy-start.3) | copy-done | bytes 4194328
  59.1 5.5 %shard_map.66.near_ref = f32[64,32,128]{2,1,0:T(8,128)S(1)} custom-call(s32[1]{0:T(128)} %bitcast.t, s32[128,8]{1,0:T(8,128)S(1)} %bitcast.48, bf16[2,8,32,128]{3,2,1,0:T(8,128)(2,1)S(1)} %shard_map.46.own_ref.refs_0_, bf16[2,8,32,128]{3,2,1,0:T(8,128)(2,1)S(1)} %shard_map.49.own_ref.refs_1_, bf16[2,8,32,128]{3,2,1,0:T(8,128)(2,1)S(1)} %shard_map.52.own_ref.refs_2_, ...), custom_call_target="tpu_custom_call" | custom-call | bytes 21600000 | tf_op jit(solution)/shard_map/pallas_call | solution.py:319
  64.6 1.2 %shard_map.69.rest_0_ = f32[128,2048]{1,0:T(8,128)} custom-call(s32[1]{0:T(128)} %bitcast.t, bf16[2,8,32,128]{3,2,1,0:T(8,128)(2,1)S(1)} %shard_map.68.own_ref, bf16[2,8,32,128]{3,2,1,0:T(8,128)(2,1)S(1)} %collective-permute-done.28.other_ref, bf16[1,128,32,128]{3,2,1,0:T(8,128)(2,1)S(1)} %get-tuple-element.23.w_ref, f32[64,32,128]{2,1,0:T(8,128)S(1)} %shard_map.66.near_ref), custom_call_target="tpu_custom_call" | custom-call | bytes 4320000 | tf_op jit(solution)/shard_map/pallas_call | solution.py:77
  65.8 2.1 %collective-permute-done.27.other_ref = bf16[2,8,32,128]{3,2,1,0:T(8,128)(2,1)S(1)} collective-permute-done((bf16[2,8,32,128]{3,2,1,0:T(8,128)(2,1)S(1)}, bf16[2,8,32,128]{3,2,1,0:T(8,128)(2,1)S(1)}, u32[]{:S(2)}, u32[]{:S(2)}) %collective-permute-start.27) | collective-permute-done | bytes 131104 | tf_op jit(solution)/shard_map/ppermute | solution.py:338
  67.9 1.2 %shard_map.70.rest_0_ = f32[128,2048]{1,0:T(8,128)} custom-call(s32[1]{0:T(128)} %bitcast.t, bf16[2,8,32,128]{3,2,1,0:T(8,128)(2,1)S(1)} %shard_map.65.own_ref, bf16[2,8,32,128]{3,2,1,0:T(8,128)(2,1)S(1)} %collective-permute-done.27.other_ref, bf16[1,128,32,128]{3,2,1,0:T(8,128)(2,1)S(1)} %get-tuple-element.23.w_ref, ...), custom_call_target="tpu_custom_call", output_to_operand_aliasing={{}: (5, {})} | custom-call | bytes 4320000 | tf_op jit(solution)/shard_map/pallas_call | solution.py:77
  69.1 1.6 %collective-permute-done.26.other_ref = bf16[2,8,32,128]{3,2,1,0:T(8,128)(2,1)S(1)} collective-permute-done((bf16[2,8,32,128]{3,2,1,0:T(8,128)(2,1)S(1)}, bf16[2,8,32,128]{3,2,1,0:T(8,128)(2,1)S(1)}, u32[]{:S(2)}, u32[]{:S(2)}) %collective-permute-start.26) | collective-permute-done | bytes 131104 | tf_op jit(solution)/shard_map/ppermute | solution.py:338
  70.7 1.2 %shard_map.71.rest_0_ = f32[128,2048]{1,0:T(8,128)} custom-call(s32[1]{0:T(128)} %bitcast.t, bf16[2,8,32,128]{3,2,1,0:T(8,128)(2,1)S(1)} %shard_map.67.own_ref, bf16[2,8,32,128]{3,2,1,0:T(8,128)(2,1)S(1)} %collective-permute-done.26.other_ref, bf16[1,128,32,128]{3,2,1,0:T(8,128)(2,1)S(1)} %get-tuple-element.23.w_ref, ...), custom_call_target="tpu_custom_call", output_to_operand_aliasing={{}: (5, {})} | custom-call | bytes 4320000 | tf_op jit(solution)/shard_map/pallas_call | solution.py:77
  71.9 1.6 %collective-permute-done.23.other_ref = bf16[2,8,32,128]{3,2,1,0:T(8,128)(2,1)S(1)} collective-permute-done((bf16[2,8,32,128]{3,2,1,0:T(8,128)(2,1)S(1)}, bf16[2,8,32,128]{3,2,1,0:T(8,128)(2,1)S(1)}, u32[]{:S(2)}, u32[]{:S(2)}) %collective-permute-start.23) | collective-permute-done | bytes 131104 | tf_op jit(solution)/shard_map/ppermute | solution.py:338
  73.5 1.2 %shard_map.72 = f32[128,2048]{1,0:T(8,128)} custom-call(s32[1]{0:T(128)} %bitcast.t, bf16[2,8,32,128]{3,2,1,0:T(8,128)(2,1)S(1)} %shard_map.62.own_ref, bf16[2,8,32,128]{3,2,1,0:T(8,128)(2,1)S(1)} %collective-permute-done.23.other_ref, bf16[1,128,32,128]{3,2,1,0:T(8,128)(2,1)S(1)} %get-tuple-element.23.w_ref, ...), custom_call_target="tpu_custom_call", output_to_operand_aliasing={{}: (5, {})} | custom-call | bytes 4320000 | tf_op jit(solution)/shard_map/pallas_call | solution.py:77
  (65 shorter events, 10.8 us)
Async XLA Ops:
  0.0 18.6 %copy-start = (bf16[12,1,128,32,128]{4,3,2,1,0:T(8,128)(2,1)S(1)}, bf16[12,1,128,32,128]{4,3,2,1,0:T(8,128)(2,1)}, u32[]{:S(2)}) copy-start(bf16[12,1,128,32,128]{4,3,2,1,0:T(8,128)(2,1)} %param.5) | copy-start | bytes 37748740
  1.5 7.9 %collective-permute-start.11 = (bf16[2,8,32,128]{3,2,1,0:T(8,128)(2,1)S(1)}, bf16[2,8,32,128]{3,2,1,0:T(8,128)(2,1)S(1)}, u32[]{:S(2)}, u32[]{:S(2)}) collective-permute-start(bf16[2,8,32,128]{3,2,1,0:T(8,128)(2,1)S(1)} %shard_map.55.own_ref.refs_3_), channel_id=1, source_target_pairs={{0,8},{8,0},{16,24},{24,16},{1,9},{9,1},{17,25},{25,17},{2,10},{10... | collective-permute-start | bytes 393224 | tf_op jit(solution)/shard_map/ppermute | solution.py:338
  4.7 7.1 %collective-permute-start.7 = (bf16[2,8,32,128]{3,2,1,0:T(8,128)(2,1)S(1)}, bf16[2,8,32,128]{3,2,1,0:T(8,128)(2,1)S(1)}, u32[]{:S(2)}, u32[]{:S(2)}) collective-permute-start(bf16[2,8,32,128]{3,2,1,0:T(8,128)(2,1)S(1)} %shard_map.52.own_ref.refs_2_), channel_id=1, source_target_pairs={{0,8},{8,0},{16,24},{24,16},{1,9},{9,1},{17,25},{25,17},{2,10},{10... | collective-permute-start | bytes 393224 | tf_op jit(solution)/shard_map/ppermute | solution.py:338
  5.1 9.3 %collective-permute-start.3 = (bf16[2,8,32,128]{3,2,1,0:T(8,128)(2,1)S(1)}, bf16[2,8,32,128]{3,2,1,0:T(8,128)(2,1)S(1)}, u32[]{:S(2)}, u32[]{:S(2)}) collective-permute-start(bf16[2,8,32,128]{3,2,1,0:T(8,128)(2,1)S(1)} %shard_map.49.own_ref.refs_1_), channel_id=1, source_target_pairs={{0,8},{8,0},{16,24},{24,16},{1,9},{9,1},{17,25},{25,17},{2,10},{10... | collective-permute-start | bytes 393224 | tf_op jit(solution)/shard_map/ppermute | solution.py:338
  7.4 9.5 %collective-permute-start = (bf16[2,8,32,128]{3,2,1,0:T(8,128)(2,1)S(1)}, bf16[2,8,32,128]{3,2,1,0:T(8,128)(2,1)S(1)}, u32[]{:S(2)}, u32[]{:S(2)}) collective-permute-start(bf16[2,8,32,128]{3,2,1,0:T(8,128)(2,1)S(1)} %shard_map.46.own_ref.refs_0_), channel_id=1, source_target_pairs={{0,8},{8,0},{16,24},{24,16},{1,9},{9,1},{17,25},{25,17},{2,10},{10... | collective-permute-start | bytes 393224 | tf_op jit(solution)/shard_map/ppermute | solution.py:338
  9.7 8.8 %collective-permute-start.12 = (bf16[2,8,32,128]{3,2,1,0:T(8,128)(2,1)S(1)}, bf16[2,8,32,128]{3,2,1,0:T(8,128)(2,1)S(1)}, u32[]{:S(2)}, u32[]{:S(2)}) collective-permute-start(bf16[2,8,32,128]{3,2,1,0:T(8,128)(2,1)S(1)} %shard_map.56.own_ref), channel_id=1, source_target_pairs={{0,16},{8,24},{16,0},{24,8},{1,17},{9,25},{17,1},{25,9},{2,18},{10... | collective-permute-start | bytes 393224 | tf_op jit(solution)/shard_map/ppermute | solution.py:338
  12.2 11.5 %collective-permute-start.8 = (bf16[2,8,32,128]{3,2,1,0:T(8,128)(2,1)S(1)}, bf16[2,8,32,128]{3,2,1,0:T(8,128)(2,1)S(1)}, u32[]{:S(2)}, u32[]{:S(2)}) collective-permute-start(bf16[2,8,32,128]{3,2,1,0:T(8,128)(2,1)S(1)} %shard_map.53.own_ref), channel_id=1, source_target_pairs={{0,16},{8,24},{16,0},{24,8},{1,17},{9,25},{17,1},{25,9},{2,18},{10... | collective-permute-start | bytes 393224 | tf_op jit(solution)/shard_map/ppermute | solution.py:338
  14.7 10.4 %collective-permute-start.4 = (bf16[2,8,32,128]{3,2,1,0:T(8,128)(2,1)S(1)}, bf16[2,8,32,128]{3,2,1,0:T(8,128)(2,1)S(1)}, u32[]{:S(2)}, u32[]{:S(2)}) collective-permute-start(bf16[2,8,32,128]{3,2,1,0:T(8,128)(2,1)S(1)} %shard_map.50.own_ref), channel_id=1, source_target_pairs={{0,16},{8,24},{16,0},{24,8},{1,17},{9,25},{17,1},{25,9},{2,18},{10... | collective-permute-start | bytes 393224 | tf_op jit(solution)/shard_map/ppermute | solution.py:338
  17.2 10.2 %collective-permute-start.1 = (bf16[2,8,32,128]{3,2,1,0:T(8,128)(2,1)S(1)}, bf16[2,8,32,128]{3,2,1,0:T(8,128)(2,1)S(1)}, u32[]{:S(2)}, u32[]{:S(2)}) collective-permute-start(bf16[2,8,32,128]{3,2,1,0:T(8,128)(2,1)S(1)} %shard_map.47.own_ref), channel_id=1, source_target_pairs={{0,16},{8,24},{16,0},{24,8},{1,17},{9,25},{17,1},{25,9},{2,18},{10... | collective-permute-start | bytes 393224 | tf_op jit(solution)/shard_map/ppermute | solution.py:338
  20.0 9.0 %collective-permute-start.13 = (bf16[2,8,32,128]{3,2,1,0:T(8,128)(2,1)S(1)}, bf16[2,8,32,128]{3,2,1,0:T(8,128)(2,1)S(1)}, u32[]{:S(2)}, u32[]{:S(2)}) collective-permute-start(bf16[2,8,32,128]{3,2,1,0:T(8,128)(2,1)S(1)} %shard_map.57), channel_id=1, source_target_pairs={{0,6},{1,7},{2,4},{3,5},{4,2},{5,3},{6,0},{7,1},{8,14},{9,15},{10,... | collective-permute-start | bytes 393224 | tf_op jit(solution)/shard_map/ppermute | solution.py:338
  25.1 8.6 %collective-permute-start.9 = (bf16[2,8,32,128]{3,2,1,0:T(8,128)(2,1)S(1)}, bf16[2,8,32,128]{3,2,1,0:T(8,128)(2,1)S(1)}, u32[]{:S(2)}, u32[]{:S(2)}) collective-permute-start(bf16[2,8,32,128]{3,2,1,0:T(8,128)(2,1)S(1)} %shard_map.54), channel_id=1, source_target_pairs={{0,4},{1,5},{2,6},{3,7},{4,0},{5,1},{6,2},{7,3},{8,12},{9,13},{10,... | collective-permute-start | bytes 393224 | tf_op jit(solution)/shard_map/ppermute | solution.py:338
  26.6 7.6 %collective-permute-start.5 = (bf16[2,8,32,128]{3,2,1,0:T(8,128)(2,1)S(1)}, bf16[2,8,32,128]{3,2,1,0:T(8,128)(2,1)S(1)}, u32[]{:S(2)}, u32[]{:S(2)}) collective-permute-start(bf16[2,8,32,128]{3,2,1,0:T(8,128)(2,1)S(1)} %shard_map.51), channel_id=1, source_target_pairs={{0,2},{1,3},{2,0},{3,1},{4,6},{5,7},{6,4},{7,5},{8,10},{9,11},{10,... | collective-permute-start | bytes 393224 | tf_op jit(solution)/shard_map/ppermute | solution.py:338
  28.9 5.3 %collective-permute-start.2 = (bf16[2,8,32,128]{3,2,1,0:T(8,128)(2,1)S(1)}, bf16[2,8,32,128]{3,2,1,0:T(8,128)(2,1)S(1)}, u32[]{:S(2)}, u32[]{:S(2)}) collective-permute-start(bf16[2,8,32,128]{3,2,1,0:T(8,128)(2,1)S(1)} %shard_map.48.refs_0_), channel_id=1, source_target_pairs={{0,1},{1,0},{2,3},{3,2},{4,5},{5,4},{6,7},{7,6},{8,9},{9,8},{10,11... | collective-permute-start | bytes 393224 | tf_op jit(solution)/shard_map/ppermute | solution.py:338
  28.9 5.2 %collective-permute-start.14 = (bf16[2,8,32,128]{3,2,1,0:T(8,128)(2,1)S(1)}, bf16[2,8,32,128]{3,2,1,0:T(8,128)(2,1)S(1)}, u32[]{:S(2)}, u32[]{:S(2)}) collective-permute-start(bf16[2,8,32,128]{3,2,1,0:T(8,128)(2,1)S(1)} %collective-permute-done.13.refs_6_), channel_id=1, source_target_pairs={{0,1},{1,0},{2,3},{3,2},{4,5},{5,4},{6,7},{7,6},{8,9},{9,8},{10,11... | collective-permute-start | bytes 393224 | tf_op jit(solution)/shard_map/ppermute | solution.py:338
  33.7 1.3 %collective-permute-start.10 = (bf16[2,8,32,128]{3,2,1,0:T(8,128)(2,1)S(1)}, bf16[2,8,32,128]{3,2,1,0:T(8,128)(2,1)S(1)}, u32[]{:S(2)}, u32[]{:S(2)}) collective-permute-start(bf16[2,8,32,128]{3,2,1,0:T(8,128)(2,1)S(1)} %collective-permute-done.9.refs_4_), channel_id=1, source_target_pairs={{0,1},{1,0},{2,3},{3,2},{4,5},{5,4},{6,7},{7,6},{8,9},{9,8},{10,11... | collective-permute-start | bytes 393224 | tf_op jit(solution)/shard_map/ppermute | solution.py:338
  34.2 1.3 %collective-permute-start.6 = (bf16[2,8,32,128]{3,2,1,0:T(8,128)(2,1)S(1)}, bf16[2,8,32,128]{3,2,1,0:T(8,128)(2,1)S(1)}, u32[]{:S(2)}, u32[]{:S(2)}) collective-permute-start(bf16[2,8,32,128]{3,2,1,0:T(8,128)(2,1)S(1)} %collective-permute-done.5.refs_2_), channel_id=1, source_target_pairs={{0,1},{1,0},{2,3},{3,2},{4,5},{5,4},{6,7},{7,6},{8,9},{9,8},{10,11... | collective-permute-start | bytes 393224 | tf_op jit(solution)/shard_map/ppermute | solution.py:338
  37.4 1.4 %collective-permute-start.15 = (bf16[2,8,32,128]{3,2,1,0:T(8,128)(2,1)S(1)}, bf16[2,8,32,128]{3,2,1,0:T(8,128)(2,1)S(1)}, u32[]{:S(2)}, u32[]{:S(2)}) collective-permute-start(bf16[2,8,32,128]{3,2,1,0:T(8,128)(2,1)S(1)} %get-tuple-element.14.own_ref), channel_id=1, source_target_pairs={{0,1},{1,0},{2,3},{3,2},{4,5},{5,4},{6,7},{7,6},{8,9},{9,8},{10,11... | collective-permute-start | bytes 393224 | tf_op jit(solution)/shard_map/ppermute | solution.py:338
  37.6 1.6 %collective-permute-start.16 = (bf16[2,8,32,128]{3,2,1,0:T(8,128)(2,1)S(1)}, bf16[2,8,32,128]{3,2,1,0:T(8,128)(2,1)S(1)}, u32[]{:S(2)}, u32[]{:S(2)}) collective-permute-start(bf16[2,8,32,128]{3,2,1,0:T(8,128)(2,1)S(1)} %get-tuple-element.15.own_ref), channel_id=1, source_target_pairs={{0,1},{1,0},{2,3},{3,2},{4,5},{5,4},{6,7},{7,6},{8,9},{9,8},{10,11... | collective-permute-start | bytes 393224 | tf_op jit(solution)/shard_map/ppermute | solution.py:338
  38.0 3.7 %collective-permute-start.20 = (bf16[2,8,32,128]{3,2,1,0:T(8,128)(2,1)S(1)}, bf16[2,8,32,128]{3,2,1,0:T(8,128)(2,1)S(1)}, u32[]{:S(2)}, u32[]{:S(2)}) collective-permute-start(bf16[2,8,32,128]{3,2,1,0:T(8,128)(2,1)S(1)} %get-tuple-element.19.own_ref), channel_id=1, source_target_pairs={{0,1},{1,0},{2,3},{3,2},{4,5},{5,4},{6,7},{7,6},{8,9},{9,8},{10,11... | collective-permute-start | bytes 393224 | tf_op jit(solution)/shard_map/ppermute | solution.py:338
  38.1 4.0 %collective-permute-start.21 = (bf16[2,8,32,128]{3,2,1,0:T(8,128)(2,1)S(1)}, bf16[2,8,32,128]{3,2,1,0:T(8,128)(2,1)S(1)}, u32[]{:S(2)}, u32[]{:S(2)}) collective-permute-start(bf16[2,8,32,128]{3,2,1,0:T(8,128)(2,1)S(1)} %get-tuple-element.20.own_ref), channel_id=1, source_target_pairs={{0,1},{1,0},{2,3},{3,2},{4,5},{5,4},{6,7},{7,6},{8,9},{9,8},{10,11... | collective-permute-start | bytes 393224 | tf_op jit(solution)/shard_map/ppermute | solution.py:338
  39.2 6.4 %collective-permute-start.24 = (bf16[2,8,32,128]{3,2,1,0:T(8,128)(2,1)S(1)}, bf16[2,8,32,128]{3,2,1,0:T(8,128)(2,1)S(1)}, u32[]{:S(2)}, u32[]{:S(2)}) collective-permute-start(bf16[2,8,32,128]{3,2,1,0:T(8,128)(2,1)S(1)} %shard_map.59.own_ref), channel_id=1, source_target_pairs={{0,2},{1,3},{2,0},{3,1},{4,6},{5,7},{6,4},{7,5},{8,10},{9,11},{10,... | collective-permute-start | bytes 393224 | tf_op jit(solution)/shard_map/ppermute | solution.py:338
  39.6 4.9 %copy-start.2 = (bf16[1,128,2048]{2,1,0:T(8,128)(2,1)S(1)}, bf16[1,128,2048]{2,1,0:T(8,128)(2,1)}, u32[]{:S(2)}) copy-start(bf16[1,128,2048]{2,1,0:T(8,128)(2,1)} %param.4) | copy-start | bytes 1572868
  39.6 9.5 %collective-permute-start.17 = (bf16[2,8,32,128]{3,2,1,0:T(8,128)(2,1)S(1)}, bf16[2,8,32,128]{3,2,1,0:T(8,128)(2,1)S(1)}, u32[]{:S(2)}, u32[]{:S(2)}) collective-permute-start(bf16[2,8,32,128]{3,2,1,0:T(8,128)(2,1)S(1)} %shard_map.60.own_ref), channel_id=1, source_target_pairs={{0,2},{1,3},{2,0},{3,1},{4,6},{5,7},{6,4},{7,5},{8,10},{9,11},{10,... | collective-permute-start | bytes 393224 | tf_op jit(solution)/shard_map/ppermute | solution.py:338
  42.0 10.1 %collective-permute-start.25 = (bf16[2,8,32,128]{3,2,1,0:T(8,128)(2,1)S(1)}, bf16[2,8,32,128]{3,2,1,0:T(8,128)(2,1)S(1)}, u32[]{:S(2)}, u32[]{:S(2)}) collective-permute-start(bf16[2,8,32,128]{3,2,1,0:T(8,128)(2,1)S(1)} %shard_map.63.own_ref), channel_id=1, source_target_pairs={{0,2},{1,3},{2,0},{3,1},{4,6},{5,7},{6,4},{7,5},{8,10},{9,11},{10,... | collective-permute-start | bytes 393224 | tf_op jit(solution)/shard_map/ppermute | solution.py:338
  42.4 13.9 %collective-permute-start.22 = (bf16[2,8,32,128]{3,2,1,0:T(8,128)(2,1)S(1)}, bf16[2,8,32,128]{3,2,1,0:T(8,128)(2,1)S(1)}, u32[]{:S(2)}, u32[]{:S(2)}) collective-permute-start(bf16[2,8,32,128]{3,2,1,0:T(8,128)(2,1)S(1)} %shard_map.64.own_ref), channel_id=1, source_target_pairs={{0,2},{1,3},{2,0},{3,1},{4,6},{5,7},{6,4},{7,5},{8,10},{9,11},{10,... | collective-permute-start | bytes 393224 | tf_op jit(solution)/shard_map/ppermute | solution.py:338
  44.7 2.1 %collective-permute-start.18 = (bf16[2,32,128]{2,1,0:T(8,128)(2,1)S(1)}, bf16[2,32,128]{2,1,0:T(8,128)(2,1)S(1)}, u32[]{:S(2)}, u32[]{:S(2)}) collective-permute-start(bf16[2,32,128]{2,1,0:T(8,128)(2,1)S(1)} %get-tuple-element.16), channel_id=1, source_target_pairs={{0,1},{1,0},{2,3},{3,2},{4,5},{5,4},{6,7},{7,6},{8,9},{9,8},{10,11... | collective-permute-start | bytes 49160 | tf_op jit(solution)/shard_map/ppermute | solution.py:338
  45.6 3.6 %collective-permute-start.19 = (bf16[2,32,128]{2,1,0:T(8,128)(2,1)S(1)}, bf16[2,32,128]{2,1,0:T(8,128)(2,1)S(1)}, u32[]{:S(2)}, u32[]{:S(2)}) collective-permute-start(bf16[2,32,128]{2,1,0:T(8,128)(2,1)S(1)} %get-tuple-element.17), channel_id=1, source_target_pairs={{1,2},{3,4},{5,6},{2,1},{4,3},{6,5},{9,10},{11,12},{13,14},{10,9},... | collective-permute-start | bytes 49160 | tf_op jit(solution)/shard_map/ppermute | solution.py:385
  46.8 17.8 %collective-permute-start.28 = (bf16[2,8,32,128]{3,2,1,0:T(8,128)(2,1)S(1)}, bf16[2,8,32,128]{3,2,1,0:T(8,128)(2,1)S(1)}, u32[]{:S(2)}, u32[]{:S(2)}) collective-permute-start(bf16[2,8,32,128]{3,2,1,0:T(8,128)(2,1)S(1)} %shard_map.67.own_ref), channel_id=1, source_target_pairs={{0,4},{1,5},{2,6},{3,7},{4,0},{5,1},{6,2},{7,3},{8,12},{9,13},{10,... | collective-permute-start | bytes 393224 | tf_op jit(solution)/shard_map/ppermute | solution.py:338
  49.5 7.3 %copy-start.4 = (s32[1,128,8]{1,2,0:T(8,128)S(1)}, s32[1,128,8]{1,2,0:T(8,128)}, u32[]{:S(2)}) copy-start(s32[1,128,8]{1,2,0:T(8,128)} %param.7) | copy-start | bytes 12292
  49.5 18.4 %collective-permute-start.27 = (bf16[2,8,32,128]{3,2,1,0:T(8,128)(2,1)S(1)}, bf16[2,8,32,128]{3,2,1,0:T(8,128)(2,1)S(1)}, u32[]{:S(2)}, u32[]{:S(2)}) collective-permute-start(bf16[2,8,32,128]{3,2,1,0:T(8,128)(2,1)S(1)} %shard_map.62.own_ref), channel_id=1, source_target_pairs={{0,4},{1,5},{2,6},{3,7},{4,0},{5,1},{6,2},{7,3},{8,12},{9,13},{10,... | collective-permute-start | bytes 393224 | tf_op jit(solution)/shard_map/ppermute | solution.py:338
  52.4 18.3 %collective-permute-start.26 = (bf16[2,8,32,128]{3,2,1,0:T(8,128)(2,1)S(1)}, bf16[2,8,32,128]{3,2,1,0:T(8,128)(2,1)S(1)}, u32[]{:S(2)}, u32[]{:S(2)}) collective-permute-start(bf16[2,8,32,128]{3,2,1,0:T(8,128)(2,1)S(1)} %shard_map.68.own_ref), channel_id=1, source_target_pairs={{0,4},{1,5},{2,6},{3,7},{4,0},{5,1},{6,2},{7,3},{8,12},{9,13},{10,... | collective-permute-start | bytes 393224 | tf_op jit(solution)/shard_map/ppermute | solution.py:338
  56.7 16.8 %collective-permute-start.23 = (bf16[2,8,32,128]{3,2,1,0:T(8,128)(2,1)S(1)}, bf16[2,8,32,128]{3,2,1,0:T(8,128)(2,1)S(1)}, u32[]{:S(2)}, u32[]{:S(2)}) collective-permute-start(bf16[2,8,32,128]{3,2,1,0:T(8,128)(2,1)S(1)} %shard_map.65.own_ref), channel_id=1, source_target_pairs={{0,4},{1,5},{2,6},{3,7},{4,0},{5,1},{6,2},{7,3},{8,12},{9,13},{10,... | collective-permute-start | bytes 393224 | tf_op jit(solution)/shard_map/ppermute | solution.py:338
  (2 other events, 3.4 us)

commit v5 on v4

--- a/solution.py
+++ b/solution.py
@@ -349,7 +349,7 @@
     low_bits = lows.bit_length() - 1
     G = 2
     chunks = groups // G
-    order = list(range(chunks))[::-1]
+    order = list(range(1, chunks)) + [0]
     tgt_index = lax.axis_index("tgt").astype(jnp.int32).reshape(1)
     weights = factors[:, 0]
     ends = {0: factors[:1, 0], factors.shape[0] - 1: factors[-1:, 0]}

time: 74.9 us -> 74.9 us (level)
  no operation moved by 1% of the time
where the time goes in v5:
time: 74.9 us; the launch traced here: 74.7 us
  starting transfers between devices  30.2 us (40%)
  Pallas kernels  23 us (31%)
  waiting for transfers between devices  15.7 us (21%)
  local copies, waits for them, and re-layouts  5.39 us (7%)
    ppermute x28, starting transfers between devices, swapped_with(): return lax.ppermute(x, axis, [(i, i ^ distance) for i in range(count)])  29.4 us
    pallas_call x25, Pallas kernels, call(): pl.pallas_call(kernel, out_shape=out_shapes, grid_spec=pltpu.PrefetchScal...  17.4 us
    ppermute x28, waiting for transfers between devices, swapped_with(): return lax.ppermute(x, axis, [(i, i ^ distance) for i in range(count)])  15.7 us
    pallas_call x1, Pallas kernels, near_field(): pl.pallas_call(functools.partial(near_kernel, G, lows, len(chunks), count...  5.5 us
    unnamed x11, local copies, waits for them, and re-layouts  3.49 us
    squeeze x1, local copies, waits for them, and re-layouts, per_device(): ends = {0: factors[:1, 0], factors.shape[0] - 1: factors[-1:, 0]}  1.9 us
  transfers between devices with their start and end apart: 29, of which 11 were waited for; matrix products, arithmetic and copies ran while one was open for 3% of the time, Pallas kernels for 26%

profile of v5, /device:TPU:0, one launch (start us, length us, event | category | flops | bytes accessed | tf_op | source)
XLA Modules:
  0.0 74.7 jit_solution(7103001255835402450)
XLA Ops:
  0.0 1.2 %copy-done.1 = bf16[1,128,2048]{2,1,0:T(8,128)(2,1)S(1)} copy-done((bf16[1,128,2048]{2,1,0:T(8,128)(2,1)S(1)}, bf16[1,128,2048]{2,1,0:T(8,128)(2,1)}, u32[]{:S(2)}) %copy-start.1) | copy-done | bytes 524312
  1.5 3.0 %collective-permute-start.11 = (bf16[2,8,32,128]{3,2,1,0:T(8,128)(2,1)S(1)}, bf16[2,8,32,128]{3,2,1,0:T(8,128)(2,1)S(1)}, u32[]{:S(2)}, u32[]{:S(2)}) collective-permute-start(bf16[2,8,32,128]{3,2,1,0:T(8,128)(2,1)S(1)} %shard_map.55.own_ref.refs_3_), channel_id=1, source_target_pairs={{0,8},{8,0},{16,24},{24,16},{1,9},{9,1},{17,25},{25,17},{2,10},{10... | collective-permute-start | bytes 393224 | tf_op jit(solution)/shard_map/ppermute | solution.py:338
  5.1 2.1 %collective-permute-start.3 = (bf16[2,8,32,128]{3,2,1,0:T(8,128)(2,1)S(1)}, bf16[2,8,32,128]{3,2,1,0:T(8,128)(2,1)S(1)}, u32[]{:S(2)}, u32[]{:S(2)}) collective-permute-start(bf16[2,8,32,128]{3,2,1,0:T(8,128)(2,1)S(1)} %shard_map.49.own_ref.refs_1_), channel_id=1, source_target_pairs={{0,8},{8,0},{16,24},{24,16},{1,9},{9,1},{17,25},{25,17},{2,10},{10... | collective-permute-start | bytes 393224 | tf_op jit(solution)/shard_map/ppermute | solution.py:338
  7.5 1.9 %slice_bitcast_fusion = (bf16[1,128,32,128]{3,2,1,0:T(8,128)(2,1)S(1)}, bf16[1,128,32,128]{3,2,1,0:T(8,128)(2,1)S(1)}) fusion(bf16[12,1,128,32,128]{4,3,2,1,0:T(8,128)(2,1)} %param.5), kind=kLoop, calls=%fused_computation | loop fusion | bytes 4194304 | tf_op jit(solution)/shard_map/squeeze | solution.py:355
  9.7 2.1 %collective-permute-start.12 = (bf16[2,8,32,128]{3,2,1,0:T(8,128)(2,1)S(1)}, bf16[2,8,32,128]{3,2,1,0:T(8,128)(2,1)S(1)}, u32[]{:S(2)}, u32[]{:S(2)}) collective-permute-start(bf16[2,8,32,128]{3,2,1,0:T(8,128)(2,1)S(1)} %shard_map.56.own_ref), channel_id=1, source_target_pairs={{0,16},{8,24},{16,0},{24,8},{1,17},{9,25},{17,1},{25,9},{2,18},{10... | collective-permute-start | bytes 393224 | tf_op jit(solution)/shard_map/ppermute | solution.py:338
  12.2 1.9 %collective-permute-start.8 = (bf16[2,8,32,128]{3,2,1,0:T(8,128)(2,1)S(1)}, bf16[2,8,32,128]{3,2,1,0:T(8,128)(2,1)S(1)}, u32[]{:S(2)}, u32[]{:S(2)}) collective-permute-start(bf16[2,8,32,128]{3,2,1,0:T(8,128)(2,1)S(1)} %shard_map.53.own_ref), channel_id=1, source_target_pairs={{0,16},{8,24},{16,0},{24,8},{1,17},{9,25},{17,1},{25,9},{2,18},{10... | collective-permute-start | bytes 393224 | tf_op jit(solution)/shard_map/ppermute | solution.py:338
  14.7 2.1 %collective-permute-start.4 = (bf16[2,8,32,128]{3,2,1,0:T(8,128)(2,1)S(1)}, bf16[2,8,32,128]{3,2,1,0:T(8,128)(2,1)S(1)}, u32[]{:S(2)}, u32[]{:S(2)}) collective-permute-start(bf16[2,8,32,128]{3,2,1,0:T(8,128)(2,1)S(1)} %shard_map.50.own_ref), channel_id=1, source_target_pairs={{0,16},{8,24},{16,0},{24,8},{1,17},{9,25},{17,1},{25,9},{2,18},{10... | collective-permute-start | bytes 393224 | tf_op jit(solution)/shard_map/ppermute | solution.py:338
  17.2 1.3 %collective-permute-start.1 = (bf16[2,8,32,128]{3,2,1,0:T(8,128)(2,1)S(1)}, bf16[2,8,32,128]{3,2,1,0:T(8,128)(2,1)S(1)}, u32[]{:S(2)}, u32[]{:S(2)}) collective-permute-start(bf16[2,8,32,128]{3,2,1,0:T(8,128)(2,1)S(1)} %shard_map.47.own_ref), channel_id=1, source_target_pairs={{0,16},{8,24},{16,0},{24,8},{1,17},{9,25},{17,1},{25,9},{2,18},{10... | collective-permute-start | bytes 393224 | tf_op jit(solution)/shard_map/ppermute | solution.py:338
  18.6 1.4 %shard_map.57 = bf16[2,8,32,128]{3,2,1,0:T(8,128)(2,1)S(1)} custom-call(s32[1]{0:T(128)} %bitcast.t, bf16[2,8,32,128]{3,2,1,0:T(8,128)(2,1)S(1)} %shard_map.56.own_ref, bf16[2,8,32,128]{3,2,1,0:T(8,128)(2,1)S(1)} %collective-permute-done.12.other_ref, bf16[12,128,32,128]{3,2,1,0:T(8,128)(2,1)S(1)} %bitcast.10, bf16[12,128,32,128]{3,2,1,0:T(8,128)(2,1)S(1)} %bitcast.11, ...), custom_call_target="tpu_custom_call" | custom-call | bytes 5400000 | tf_op jit(solution)/shard_map/pallas_call | solution.py:77
  20.0 3.7 %collective-permute-start.13 = (bf16[2,8,32,128]{3,2,1,0:T(8,128)(2,1)S(1)}, bf16[2,8,32,128]{3,2,1,0:T(8,128)(2,1)S(1)}, u32[]{:S(2)}, u32[]{:S(2)}) collective-permute-start(bf16[2,8,32,128]{3,2,1,0:T(8,128)(2,1)S(1)} %shard_map.57), channel_id=1, source_target_pairs={{0,6},{1,7},{2,4},{3,5},{4,2},{5,3},{6,0},{7,1},{8,14},{9,15},{10,... | collective-permute-start | bytes 393224 | tf_op jit(solution)/shard_map/ppermute | solution.py:338
  23.7 1.4 %shard_map.54 = bf16[2,8,32,128]{3,2,1,0:T(8,128)(2,1)S(1)} custom-call(s32[1]{0:T(128)} %bitcast.t, bf16[2,8,32,128]{3,2,1,0:T(8,128)(2,1)S(1)} %shard_map.53.own_ref, bf16[2,8,32,128]{3,2,1,0:T(8,128)(2,1)S(1)} %collective-permute-done.8.other_ref, bf16[12,128,32,128]{3,2,1,0:T(8,128)(2,1)S(1)} %bitcast.15, bf16[12,128,32,128]{3,2,1,0:T(8,128)(2,1)S(1)} %bitcast.16, ...), custom_call_target="tpu_custom_call" | custom-call | bytes 5400000 | tf_op jit(solution)/shard_map/pallas_call | solution.py:77
  25.2 1.4 %shard_map.51 = bf16[2,8,32,128]{3,2,1,0:T(8,128)(2,1)S(1)} custom-call(s32[1]{0:T(128)} %bitcast.t, bf16[2,8,32,128]{3,2,1,0:T(8,128)(2,1)S(1)} %shard_map.50.own_ref, bf16[2,8,32,128]{3,2,1,0:T(8,128)(2,1)S(1)} %collective-permute-done.4.other_ref, bf16[12,128,32,128]{3,2,1,0:T(8,128)(2,1)S(1)} %bitcast.24, bf16[12,128,32,128]{3,2,1,0:T(8,128)(2,1)S(1)} %bitcast.21, ...), custom_call_target="tpu_custom_call" | custom-call | bytes 5400000 | tf_op jit(solution)/shard_map/pallas_call | solution.py:77
  26.6 0.8 %collective-permute-start.5 = (bf16[2,8,32,128]{3,2,1,0:T(8,128)(2,1)S(1)}, bf16[2,8,32,128]{3,2,1,0:T(8,128)(2,1)S(1)}, u32[]{:S(2)}, u32[]{:S(2)}) collective-permute-start(bf16[2,8,32,128]{3,2,1,0:T(8,128)(2,1)S(1)} %shard_map.51), channel_id=1, source_target_pairs={{0,2},{1,3},{2,0},{3,1},{4,6},{5,7},{6,4},{7,5},{8,10},{9,11},{10,... | collective-permute-start | bytes 393224 | tf_op jit(solution)/shard_map/ppermute | solution.py:338
  27.4 1.4 %shard_map.48.refs_0_ = bf16[2,8,32,128]{3,2,1,0:T(8,128)(2,1)S(1)} custom-call(s32[1]{0:T(128)} %bitcast.t, bf16[2,8,32,128]{3,2,1,0:T(8,128)(2,1)S(1)} %shard_map.47.own_ref, bf16[2,8,32,128]{3,2,1,0:T(8,128)(2,1)S(1)} %collective-permute-done.1.other_ref, bf16[12,128,32,128]{3,2,1,0:T(8,128)(2,1)S(1)} %bitcast.25, ...), custom_call_target="tpu_custom_call" | custom-call | bytes 5400000 | tf_op jit(solution)/shard_map/pallas_call | solution.py:77
  29.4 4.2 %collective-permute-done.9.refs_4_ = bf16[2,8,32,128]{3,2,1,0:T(8,128)(2,1)S(1)} collective-permute-done((bf16[2,8,32,128]{3,2,1,0:T(8,128)(2,1)S(1)}, bf16[2,8,32,128]{3,2,1,0:T(8,128)(2,1)S(1)}, u32[]{:S(2)}, u32[]{:S(2)}) %collective-permute-start.9) | collective-permute-done | bytes 131104 | tf_op jit(solution)/shard_map/ppermute | solution.py:338
  35.5 1.9 %shard_map.58 = (bf16[2,8,32,128]{3,2,1,0:T(8,128)(2,1)S(1)}, bf16[2,8,32,128]{3,2,1,0:T(8,128)(2,1)S(1)}, bf16[2,8,32,128]{3,2,1,0:T(8,128)(2,1)S(1)}, bf16[2,8,32,128]{3,2,1,0:T(8,128)(2,1)S(1)}) custom-call(s32[1]{0:T(128)} %bitcast.t, bf16[2,8,32,128]{3,2,1,0:T(8,128)(2,1)S(1)} %shard_map.48.refs_0_, ...), custom_call_target="tpu_custom_call" | custom-call | bytes 9000000 | tf_op jit(solution)/shard_map/pallas_call | solution.py:77
  39.6 2.1 %collective-permute-start.17 = (bf16[2,8,32,128]{3,2,1,0:T(8,128)(2,1)S(1)}, bf16[2,8,32,128]{3,2,1,0:T(8,128)(2,1)S(1)}, u32[]{:S(2)}, u32[]{:S(2)}) collective-permute-start(bf16[2,8,32,128]{3,2,1,0:T(8,128)(2,1)S(1)} %shard_map.60.own_ref), channel_id=1, source_target_pairs={{0,2},{1,3},{2,0},{3,1},{4,6},{5,7},{6,4},{7,5},{8,10},{9,11},{10,... | collective-permute-start | bytes 393224 | tf_op jit(solution)/shard_map/ppermute | solution.py:338
  42.4 2.1 %collective-permute-start.22 = (bf16[2,8,32,128]{3,2,1,0:T(8,128)(2,1)S(1)}, bf16[2,8,32,128]{3,2,1,0:T(8,128)(2,1)S(1)}, u32[]{:S(2)}, u32[]{:S(2)}) collective-permute-start(bf16[2,8,32,128]{3,2,1,0:T(8,128)(2,1)S(1)} %shard_map.64.own_ref), channel_id=1, source_target_pairs={{0,2},{1,3},{2,0},{3,1},{4,6},{5,7},{6,4},{7,5},{8,10},{9,11},{10,... | collective-permute-start | bytes 393224 | tf_op jit(solution)/shard_map/ppermute | solution.py:338
  45.6 0.8 %collective-permute-start.19 = (bf16[2,32,128]{2,1,0:T(8,128)(2,1)S(1)}, bf16[2,32,128]{2,1,0:T(8,128)(2,1)S(1)}, u32[]{:S(2)}, u32[]{:S(2)}) collective-permute-start(bf16[2,32,128]{2,1,0:T(8,128)(2,1)S(1)} %get-tuple-element.17), channel_id=1, source_target_pairs={{1,2},{3,4},{5,6},{2,1},{4,3},{6,5},{9,10},{11,12},{13,14},{10,9},... | collective-permute-start | bytes 49160 | tf_op jit(solution)/shard_map/ppermute | solution.py:385
  46.8 2.4 %collective-permute-start.28 = (bf16[2,8,32,128]{3,2,1,0:T(8,128)(2,1)S(1)}, bf16[2,8,32,128]{3,2,1,0:T(8,128)(2,1)S(1)}, u32[]{:S(2)}, u32[]{:S(2)}) collective-permute-start(bf16[2,8,32,128]{3,2,1,0:T(8,128)(2,1)S(1)} %shard_map.67.own_ref), channel_id=1, source_target_pairs={{0,4},{1,5},{2,6},{3,7},{4,0},{5,1},{6,2},{7,3},{8,12},{9,13},{10,... | collective-permute-start | bytes 393224 | tf_op jit(solution)/shard_map/ppermute | solution.py:338
  49.5 2.6 %collective-permute-start.27 = (bf16[2,8,32,128]{3,2,1,0:T(8,128)(2,1)S(1)}, bf16[2,8,32,128]{3,2,1,0:T(8,128)(2,1)S(1)}, u32[]{:S(2)}, u32[]{:S(2)}) collective-permute-start(bf16[2,8,32,128]{3,2,1,0:T(8,128)(2,1)S(1)} %shard_map.62.own_ref), channel_id=1, source_target_pairs={{0,4},{1,5},{2,6},{3,7},{4,0},{5,1},{6,2},{7,3},{8,12},{9,13},{10,... | collective-permute-start | bytes 393224 | tf_op jit(solution)/shard_map/ppermute | solution.py:338
  52.4 1.0 %collective-permute-start.26 = (bf16[2,8,32,128]{3,2,1,0:T(8,128)(2,1)S(1)}, bf16[2,8,32,128]{3,2,1,0:T(8,128)(2,1)S(1)}, u32[]{:S(2)}, u32[]{:S(2)}) collective-permute-start(bf16[2,8,32,128]{3,2,1,0:T(8,128)(2,1)S(1)} %shard_map.68.own_ref), channel_id=1, source_target_pairs={{0,4},{1,5},{2,6},{3,7},{4,0},{5,1},{6,2},{7,3},{8,12},{9,13},{10,... | collective-permute-start | bytes 393224 | tf_op jit(solution)/shard_map/ppermute | solution.py:338
  53.5 2.9 %collective-permute-done.22.other_ref = bf16[2,8,32,128]{3,2,1,0:T(8,128)(2,1)S(1)} collective-permute-done((bf16[2,8,32,128]{3,2,1,0:T(8,128)(2,1)S(1)}, bf16[2,8,32,128]{3,2,1,0:T(8,128)(2,1)S(1)}, u32[]{:S(2)}, u32[]{:S(2)}) %collective-permute-start.22) | collective-permute-done | bytes 131104 | tf_op jit(solution)/shard_map/ppermute | solution.py:338
  56.9 2.2 %copy-done.3 = bf16[1,128,32,512]{3,2,1,0:T(8,128)(2,1)S(1)} copy-done((bf16[1,128,32,512]{3,2,1,0:T(8,128)(2,1)S(1)}, bf16[1,128,32,512]{3,2,1,0:T(8,128)(2,1)}, u32[]{:S(2)}) %copy-start.3) | copy-done | bytes 4194328
  59.1 5.5 %shard_map.66.near_ref = f32[64,32,128]{2,1,0:T(8,128)S(1)} custom-call(s32[1]{0:T(128)} %bitcast.t, s32[128,8]{1,0:T(8,128)S(1)} %bitcast.48, bf16[2,8,32,128]{3,2,1,0:T(8,128)(2,1)S(1)} %shard_map.46.own_ref.refs_0_, bf16[2,8,32,128]{3,2,1,0:T(8,128)(2,1)S(1)} %shard_map.49.own_ref.refs_1_, bf16[2,8,32,128]{3,2,1,0:T(8,128)(2,1)S(1)} %shard_map.52.own_ref.refs_2_, ...), custom_call_target="tpu_custom_call" | custom-call | bytes 21600000 | tf_op jit(solution)/shard_map/pallas_call | solution.py:319
  64.6 1.2 %shard_map.69.rest_0_ = f32[128,2048]{1,0:T(8,128)} custom-call(s32[1]{0:T(128)} %bitcast.t, bf16[2,8,32,128]{3,2,1,0:T(8,128)(2,1)S(1)} %shard_map.68.own_ref, bf16[2,8,32,128]{3,2,1,0:T(8,128)(2,1)S(1)} %collective-permute-done.28.other_ref, bf16[1,128,32,128]{3,2,1,0:T(8,128)(2,1)S(1)} %get-tuple-element.23.w_ref, f32[64,32,128]{2,1,0:T(8,128)S(1)} %shard_map.66.near_ref), custom_call_target="tpu_custom_call" | custom-call | bytes 4320000 | tf_op jit(solution)/shard_map/pallas_call | solution.py:77
  65.8 2.1 %collective-permute-done.27.other_ref = bf16[2,8,32,128]{3,2,1,0:T(8,128)(2,1)S(1)} collective-permute-done((bf16[2,8,32,128]{3,2,1,0:T(8,128)(2,1)S(1)}, bf16[2,8,32,128]{3,2,1,0:T(8,128)(2,1)S(1)}, u32[]{:S(2)}, u32[]{:S(2)}) %collective-permute-start.27) | collective-permute-done | bytes 131104 | tf_op jit(solution)/shard_map/ppermute | solution.py:338
  67.9 1.2 %shard_map.70.rest_0_ = f32[128,2048]{1,0:T(8,128)} custom-call(s32[1]{0:T(128)} %bitcast.t, bf16[2,8,32,128]{3,2,1,0:T(8,128)(2,1)S(1)} %shard_map.65.own_ref, bf16[2,8,32,128]{3,2,1,0:T(8,128)(2,1)S(1)} %collective-permute-done.27.other_ref, bf16[1,128,32,128]{3,2,1,0:T(8,128)(2,1)S(1)} %get-tuple-element.23.w_ref, ...), custom_call_target="tpu_custom_call", output_to_operand_aliasing={{}: (5, {})} | custom-call | bytes 4320000 | tf_op jit(solution)/shard_map/pallas_call | solution.py:77
  69.1 1.6 %collective-permute-done.26.other_ref = bf16[2,8,32,128]{3,2,1,0:T(8,128)(2,1)S(1)} collective-permute-done((bf16[2,8,32,128]{3,2,1,0:T(8,128)(2,1)S(1)}, bf16[2,8,32,128]{3,2,1,0:T(8,128)(2,1)S(1)}, u32[]{:S(2)}, u32[]{:S(2)}) %collective-permute-start.26) | collective-permute-done | bytes 131104 | tf_op jit(solution)/shard_map/ppermute | solution.py:338
  70.7 1.2 %shard_map.71.rest_0_ = f32[128,2048]{1,0:T(8,128)} custom-call(s32[1]{0:T(128)} %bitcast.t, bf16[2,8,32,128]{3,2,1,0:T(8,128)(2,1)S(1)} %shard_map.67.own_ref, bf16[2,8,32,128]{3,2,1,0:T(8,128)(2,1)S(1)} %collective-permute-done.26.other_ref, bf16[1,128,32,128]{3,2,1,0:T(8,128)(2,1)S(1)} %get-tuple-element.23.w_ref, ...), custom_call_target="tpu_custom_call", output_to_operand_aliasing={{}: (5, {})} | custom-call | bytes 4320000 | tf_op jit(solution)/shard_map/pallas_call | solution.py:77
  71.9 1.6 %collective-permute-done.23.other_ref = bf16[2,8,32,128]{3,2,1,0:T(8,128)(2,1)S(1)} collective-permute-done((bf16[2,8,32,128]{3,2,1,0:T(8,128)(2,1)S(1)}, bf16[2,8,32,128]{3,2,1,0:T(8,128)(2,1)S(1)}, u32[]{:S(2)}, u32[]{:S(2)}) %collective-permute-start.23) | collective-permute-done | bytes 131104 | tf_op jit(solution)/shard_map/ppermute | solution.py:338
  73.5 1.2 %shard_map.72 = f32[128,2048]{1,0:T(8,128)} custom-call(s32[1]{0:T(128)} %bitcast.t, bf16[2,8,32,128]{3,2,1,0:T(8,128)(2,1)S(1)} %shard_map.62.own_ref, bf16[2,8,32,128]{3,2,1,0:T(8,128)(2,1)S(1)} %collective-permute-done.23.other_ref, bf16[1,128,32,128]{3,2,1,0:T(8,128)(2,1)S(1)} %get-tuple-element.23.w_ref, ...), custom_call_target="tpu_custom_call", output_to_operand_aliasing={{}: (5, {})} | custom-call | bytes 4320000 | tf_op jit(solution)/shard_map/pallas_call | solution.py:77
  (65 shorter events, 10.8 us)
Async XLA Ops:
  0.0 18.6 %copy-start = (bf16[12,1,128,32,128]{4,3,2,1,0:T(8,128)(2,1)S(1)}, bf16[12,1,128,32,128]{4,3,2,1,0:T(8,128)(2,1)}, u32[]{:S(2)}) copy-start(bf16[12,1,128,32,128]{4,3,2,1,0:T(8,128)(2,1)} %param.5) | copy-start | bytes 37748740
  1.5 7.9 %collective-permute-start.11 = (bf16[2,8,32,128]{3,2,1,0:T(8,128)(2,1)S(1)}, bf16[2,8,32,128]{3,2,1,0:T(8,128)(2,1)S(1)}, u32[]{:S(2)}, u32[]{:S(2)}) collective-permute-start(bf16[2,8,32,128]{3,2,1,0:T(8,128)(2,1)S(1)} %shard_map.55.own_ref.refs_3_), channel_id=1, source_target_pairs={{0,8},{8,0},{16,24},{24,16},{1,9},{9,1},{17,25},{25,17},{2,10},{10... | collective-permute-start | bytes 393224 | tf_op jit(solution)/shard_map/ppermute | solution.py:338
  4.7 7.1 %collective-permute-start.7 = (bf16[2,8,32,128]{3,2,1,0:T(8,128)(2,1)S(1)}, bf16[2,8,32,128]{3,2,1,0:T(8,128)(2,1)S(1)}, u32[]{:S(2)}, u32[]{:S(2)}) collective-permute-start(bf16[2,8,32,128]{3,2,1,0:T(8,128)(2,1)S(1)} %shard_map.52.own_ref.refs_2_), channel_id=1, source_target_pairs={{0,8},{8,0},{16,24},{24,16},{1,9},{9,1},{17,25},{25,17},{2,10},{10... | collective-permute-start | bytes 393224 | tf_op jit(solution)/shard_map/ppermute | solution.py:338
  5.1 9.3 %collective-permute-start.3 = (bf16[2,8,32,128]{3,2,1,0:T(8,128)(2,1)S(1)}, bf16[2,8,32,128]{3,2,1,0:T(8,128)(2,1)S(1)}, u32[]{:S(2)}, u32[]{:S(2)}) collective-permute-start(bf16[2,8,32,128]{3,2,1,0:T(8,128)(2,1)S(1)} %shard_map.49.own_ref.refs_1_), channel_id=1, source_target_pairs={{0,8},{8,0},{16,24},{24,16},{1,9},{9,1},{17,25},{25,17},{2,10},{10... | collective-permute-start | bytes 393224 | tf_op jit(solution)/shard_map/ppermute | solution.py:338
  7.4 9.5 %collective-permute-start = (bf16[2,8,32,128]{3,2,1,0:T(8,128)(2,1)S(1)}, bf16[2,8,32,128]{3,2,1,0:T(8,128)(2,1)S(1)}, u32[]{:S(2)}, u32[]{:S(2)}) collective-permute-start(bf16[2,8,32,128]{3,2,1,0:T(8,128)(2,1)S(1)} %shard_map.46.own_ref.refs_0_), channel_id=1, source_target_pairs={{0,8},{8,0},{16,24},{24,16},{1,9},{9,1},{17,25},{25,17},{2,10},{10... | collective-permute-start | bytes 393224 | tf_op jit(solution)/shard_map/ppermute | solution.py:338
  9.7 8.8 %collective-permute-start.12 = (bf16[2,8,32,128]{3,2,1,0:T(8,128)(2,1)S(1)}, bf16[2,8,32,128]{3,2,1,0:T(8,128)(2,1)S(1)}, u32[]{:S(2)}, u32[]{:S(2)}) collective-permute-start(bf16[2,8,32,128]{3,2,1,0:T(8,128)(2,1)S(1)} %shard_map.56.own_ref), channel_id=1, source_target_pairs={{0,16},{8,24},{16,0},{24,8},{1,17},{9,25},{17,1},{25,9},{2,18},{10... | collective-permute-start | bytes 393224 | tf_op jit(solution)/shard_map/ppermute | solution.py:338
  12.2 11.5 %collective-permute-start.8 = (bf16[2,8,32,128]{3,2,1,0:T(8,128)(2,1)S(1)}, bf16[2,8,32,128]{3,2,1,0:T(8,128)(2,1)S(1)}, u32[]{:S(2)}, u32[]{:S(2)}) collective-permute-start(bf16[2,8,32,128]{3,2,1,0:T(8,128)(2,1)S(1)} %shard_map.53.own_ref), channel_id=1, source_target_pairs={{0,16},{8,24},{16,0},{24,8},{1,17},{9,25},{17,1},{25,9},{2,18},{10... | collective-permute-start | bytes 393224 | tf_op jit(solution)/shard_map/ppermute | solution.py:338
  14.7 10.4 %collective-permute-start.4 = (bf16[2,8,32,128]{3,2,1,0:T(8,128)(2,1)S(1)}, bf16[2,8,32,128]{3,2,1,0:T(8,128)(2,1)S(1)}, u32[]{:S(2)}, u32[]{:S(2)}) collective-permute-start(bf16[2,8,32,128]{3,2,1,0:T(8,128)(2,1)S(1)} %shard_map.50.own_ref), channel_id=1, source_target_pairs={{0,16},{8,24},{16,0},{24,8},{1,17},{9,25},{17,1},{25,9},{2,18},{10... | collective-permute-start | bytes 393224 | tf_op jit(solution)/shard_map/ppermute | solution.py:338
  17.2 10.2 %collective-permute-start.1 = (bf16[2,8,32,128]{3,2,1,0:T(8,128)(2,1)S(1)}, bf16[2,8,32,128]{3,2,1,0:T(8,128)(2,1)S(1)}, u32[]{:S(2)}, u32[]{:S(2)}) collective-permute-start(bf16[2,8,32,128]{3,2,1,0:T(8,128)(2,1)S(1)} %shard_map.47.own_ref), channel_id=1, source_target_pairs={{0,16},{8,24},{16,0},{24,8},{1,17},{9,25},{17,1},{25,9},{2,18},{10... | collective-permute-start | bytes 393224 | tf_op jit(solution)/shard_map/ppermute | solution.py:338
  20.0 9.0 %collective-permute-start.13 = (bf16[2,8,32,128]{3,2,1,0:T(8,128)(2,1)S(1)}, bf16[2,8,32,128]{3,2,1,0:T(8,128)(2,1)S(1)}, u32[]{:S(2)}, u32[]{:S(2)}) collective-permute-start(bf16[2,8,32,128]{3,2,1,0:T(8,128)(2,1)S(1)} %shard_map.57), channel_id=1, source_target_pairs={{0,6},{1,7},{2,4},{3,5},{4,2},{5,3},{6,0},{7,1},{8,14},{9,15},{10,... | collective-permute-start | bytes 393224 | tf_op jit(solution)/shard_map/ppermute | solution.py:338
  25.1 8.6 %collective-permute-start.9 = (bf16[2,8,32,128]{3,2,1,0:T(8,128)(2,1)S(1)}, bf16[2,8,32,128]{3,2,1,0:T(8,128)(2,1)S(1)}, u32[]{:S(2)}, u32[]{:S(2)}) collective-permute-start(bf16[2,8,32,128]{3,2,1,0:T(8,128)(2,1)S(1)} %shard_map.54), channel_id=1, source_target_pairs={{0,4},{1,5},{2,6},{3,7},{4,0},{5,1},{6,2},{7,3},{8,12},{9,13},{10,... | collective-permute-start | bytes 393224 | tf_op jit(solution)/shard_map/ppermute | solution.py:338
  26.6 7.6 %collective-permute-start.5 = (bf16[2,8,32,128]{3,2,1,0:T(8,128)(2,1)S(1)}, bf16[2,8,32,128]{3,2,1,0:T(8,128)(2,1)S(1)}, u32[]{:S(2)}, u32[]{:S(2)}) collective-permute-start(bf16[2,8,32,128]{3,2,1,0:T(8,128)(2,1)S(1)} %shard_map.51), channel_id=1, source_target_pairs={{0,2},{1,3},{2,0},{3,1},{4,6},{5,7},{6,4},{7,5},{8,10},{9,11},{10,... | collective-permute-start | bytes 393224 | tf_op jit(solution)/shard_map/ppermute | solution.py:338
  28.9 5.3 %collective-permute-start.2 = (bf16[2,8,32,128]{3,2,1,0:T(8,128)(2,1)S(1)}, bf16[2,8,32,128]{3,2,1,0:T(8,128)(2,1)S(1)}, u32[]{:S(2)}, u32[]{:S(2)}) collective-permute-start(bf16[2,8,32,128]{3,2,1,0:T(8,128)(2,1)S(1)} %shard_map.48.refs_0_), channel_id=1, source_target_pairs={{0,1},{1,0},{2,3},{3,2},{4,5},{5,4},{6,7},{7,6},{8,9},{9,8},{10,11... | collective-permute-start | bytes 393224 | tf_op jit(solution)/shard_map/ppermute | solution.py:338
  28.9 5.2 %collective-permute-start.14 = (bf16[2,8,32,128]{3,2,1,0:T(8,128)(2,1)S(1)}, bf16[2,8,32,128]{3,2,1,0:T(8,128)(2,1)S(1)}, u32[]{:S(2)}, u32[]{:S(2)}) collective-permute-start(bf16[2,8,32,128]{3,2,1,0:T(8,128)(2,1)S(1)} %collective-permute-done.13.refs_6_), channel_id=1, source_target_pairs={{0,1},{1,0},{2,3},{3,2},{4,5},{5,4},{6,7},{7,6},{8,9},{9,8},{10,11... | collective-permute-start | bytes 393224 | tf_op jit(solution)/shard_map/ppermute | solution.py:338
  33.7 1.3 %collective-permute-start.10 = (bf16[2,8,32,128]{3,2,1,0:T(8,128)(2,1)S(1)}, bf16[2,8,32,128]{3,2,1,0:T(8,128)(2,1)S(1)}, u32[]{:S(2)}, u32[]{:S(2)}) collective-permute-start(bf16[2,8,32,128]{3,2,1,0:T(8,128)(2,1)S(1)} %collective-permute-done.9.refs_4_), channel_id=1, source_target_pairs={{0,1},{1,0},{2,3},{3,2},{4,5},{5,4},{6,7},{7,6},{8,9},{9,8},{10,11... | collective-permute-start | bytes 393224 | tf_op jit(solution)/shard_map/ppermute | solution.py:338
  34.2 1.3 %collective-permute-start.6 = (bf16[2,8,32,128]{3,2,1,0:T(8,128)(2,1)S(1)}, bf16[2,8,32,128]{3,2,1,0:T(8,128)(2,1)S(1)}, u32[]{:S(2)}, u32[]{:S(2)}) collective-permute-start(bf16[2,8,32,128]{3,2,1,0:T(8,128)(2,1)S(1)} %collective-permute-done.5.refs_2_), channel_id=1, source_target_pairs={{0,1},{1,0},{2,3},{3,2},{4,5},{5,4},{6,7},{7,6},{8,9},{9,8},{10,11... | collective-permute-start | bytes 393224 | tf_op jit(solution)/shard_map/ppermute | solution.py:338
  37.4 1.4 %collective-permute-start.15 = (bf16[2,8,32,128]{3,2,1,0:T(8,128)(2,1)S(1)}, bf16[2,8,32,128]{3,2,1,0:T(8,128)(2,1)S(1)}, u32[]{:S(2)}, u32[]{:S(2)}) collective-permute-start(bf16[2,8,32,128]{3,2,1,0:T(8,128)(2,1)S(1)} %get-tuple-element.14.own_ref), channel_id=1, source_target_pairs={{0,1},{1,0},{2,3},{3,2},{4,5},{5,4},{6,7},{7,6},{8,9},{9,8},{10,11... | collective-permute-start | bytes 393224 | tf_op jit(solution)/shard_map/ppermute | solution.py:338
  37.6 1.6 %collective-permute-start.16 = (bf16[2,8,32,128]{3,2,1,0:T(8,128)(2,1)S(1)}, bf16[2,8,32,128]{3,2,1,0:T(8,128)(2,1)S(1)}, u32[]{:S(2)}, u32[]{:S(2)}) collective-permute-start(bf16[2,8,32,128]{3,2,1,0:T(8,128)(2,1)S(1)} %get-tuple-element.15.own_ref), channel_id=1, source_target_pairs={{0,1},{1,0},{2,3},{3,2},{4,5},{5,4},{6,7},{7,6},{8,9},{9,8},{10,11... | collective-permute-start | bytes 393224 | tf_op jit(solution)/shard_map/ppermute | solution.py:338
  38.0 3.7 %collective-permute-start.20 = (bf16[2,8,32,128]{3,2,1,0:T(8,128)(2,1)S(1)}, bf16[2,8,32,128]{3,2,1,0:T(8,128)(2,1)S(1)}, u32[]{:S(2)}, u32[]{:S(2)}) collective-permute-start(bf16[2,8,32,128]{3,2,1,0:T(8,128)(2,1)S(1)} %get-tuple-element.19.own_ref), channel_id=1, source_target_pairs={{0,1},{1,0},{2,3},{3,2},{4,5},{5,4},{6,7},{7,6},{8,9},{9,8},{10,11... | collective-permute-start | bytes 393224 | tf_op jit(solution)/shard_map/ppermute | solution.py:338
  38.1 4.0 %collective-permute-start.21 = (bf16[2,8,32,128]{3,2,1,0:T(8,128)(2,1)S(1)}, bf16[2,8,32,128]{3,2,1,0:T(8,128)(2,1)S(1)}, u32[]{:S(2)}, u32[]{:S(2)}) collective-permute-start(bf16[2,8,32,128]{3,2,1,0:T(8,128)(2,1)S(1)} %get-tuple-element.20.own_ref), channel_id=1, source_target_pairs={{0,1},{1,0},{2,3},{3,2},{4,5},{5,4},{6,7},{7,6},{8,9},{9,8},{10,11... | collective-permute-start | bytes 393224 | tf_op jit(solution)/shard_map/ppermute | solution.py:338
  39.2 6.4 %collective-permute-start.24 = (bf16[2,8,32,128]{3,2,1,0:T(8,128)(2,1)S(1)}, bf16[2,8,32,128]{3,2,1,0:T(8,128)(2,1)S(1)}, u32[]{:S(2)}, u32[]{:S(2)}) collective-permute-start(bf16[2,8,32,128]{3,2,1,0:T(8,128)(2,1)S(1)} %shard_map.59.own_ref), channel_id=1, source_target_pairs={{0,2},{1,3},{2,0},{3,1},{4,6},{5,7},{6,4},{7,5},{8,10},{9,11},{10,... | collective-permute-start | bytes 393224 | tf_op jit(solution)/shard_map/ppermute | solution.py:338
  39.6 4.9 %copy-start.2 = (bf16[1,128,2048]{2,1,0:T(8,128)(2,1)S(1)}, bf16[1,128,2048]{2,1,0:T(8,128)(2,1)}, u32[]{:S(2)}) copy-start(bf16[1,128,2048]{2,1,0:T(8,128)(2,1)} %param.4) | copy-start | bytes 1572868
  39.6 9.5 %collective-permute-start.17 = (bf16[2,8,32,128]{3,2,1,0:T(8,128)(2,1)S(1)}, bf16[2,8,32,128]{3,2,1,0:T(8,128)(2,1)S(1)}, u32[]{:S(2)}, u32[]{:S(2)}) collective-permute-start(bf16[2,8,32,128]{3,2,1,0:T(8,128)(2,1)S(1)} %shard_map.60.own_ref), channel_id=1, source_target_pairs={{0,2},{1,3},{2,0},{3,1},{4,6},{5,7},{6,4},{7,5},{8,10},{9,11},{10,... | collective-permute-start | bytes 393224 | tf_op jit(solution)/shard_map/ppermute | solution.py:338
  42.0 10.1 %collective-permute-start.25 = (bf16[2,8,32,128]{3,2,1,0:T(8,128)(2,1)S(1)}, bf16[2,8,32,128]{3,2,1,0:T(8,128)(2,1)S(1)}, u32[]{:S(2)}, u32[]{:S(2)}) collective-permute-start(bf16[2,8,32,128]{3,2,1,0:T(8,128)(2,1)S(1)} %shard_map.63.own_ref), channel_id=1, source_target_pairs={{0,2},{1,3},{2,0},{3,1},{4,6},{5,7},{6,4},{7,5},{8,10},{9,11},{10,... | collective-permute-start | bytes 393224 | tf_op jit(solution)/shard_map/ppermute | solution.py:338
  42.4 13.9 %collective-permute-start.22 = (bf16[2,8,32,128]{3,2,1,0:T(8,128)(2,1)S(1)}, bf16[2,8,32,128]{3,2,1,0:T(8,128)(2,1)S(1)}, u32[]{:S(2)}, u32[]{:S(2)}) collective-permute-start(bf16[2,8,32,128]{3,2,1,0:T(8,128)(2,1)S(1)} %shard_map.64.own_ref), channel_id=1, source_target_pairs={{0,2},{1,3},{2,0},{3,1},{4,6},{5,7},{6,4},{7,5},{8,10},{9,11},{10,... | collective-permute-start | bytes 393224 | tf_op jit(solution)/shard_map/ppermute | solution.py:338
  44.7 2.1 %collective-permute-start.18 = (bf16[2,32,128]{2,1,0:T(8,128)(2,1)S(1)}, bf16[2,32,128]{2,1,0:T(8,128)(2,1)S(1)}, u32[]{:S(2)}, u32[]{:S(2)}) collective-permute-start(bf16[2,32,128]{2,1,0:T(8,128)(2,1)S(1)} %get-tuple-element.16), channel_id=1, source_target_pairs={{0,1},{1,0},{2,3},{3,2},{4,5},{5,4},{6,7},{7,6},{8,9},{9,8},{10,11... | collective-permute-start | bytes 49160 | tf_op jit(solution)/shard_map/ppermute | solution.py:338
  45.6 3.6 %collective-permute-start.19 = (bf16[2,32,128]{2,1,0:T(8,128)(2,1)S(1)}, bf16[2,32,128]{2,1,0:T(8,128)(2,1)S(1)}, u32[]{:S(2)}, u32[]{:S(2)}) collective-permute-start(bf16[2,32,128]{2,1,0:T(8,128)(2,1)S(1)} %get-tuple-element.17), channel_id=1, source_target_pairs={{1,2},{3,4},{5,6},{2,1},{4,3},{6,5},{9,10},{11,12},{13,14},{10,9},... | collective-permute-start | bytes 49160 | tf_op jit(solution)/shard_map/ppermute | solution.py:385
  46.8 17.8 %collective-permute-start.28 = (bf16[2,8,32,128]{3,2,1,0:T(8,128)(2,1)S(1)}, bf16[2,8,32,128]{3,2,1,0:T(8,128)(2,1)S(1)}, u32[]{:S(2)}, u32[]{:S(2)}) collective-permute-start(bf16[2,8,32,128]{3,2,1,0:T(8,128)(2,1)S(1)} %shard_map.67.own_ref), channel_id=1, source_target_pairs={{0,4},{1,5},{2,6},{3,7},{4,0},{5,1},{6,2},{7,3},{8,12},{9,13},{10,... | collective-permute-start | bytes 393224 | tf_op jit(solution)/shard_map/ppermute | solution.py:338
  49.5 7.3 %copy-start.4 = (s32[1,128,8]{1,2,0:T(8,128)S(1)}, s32[1,128,8]{1,2,0:T(8,128)}, u32[]{:S(2)}) copy-start(s32[1,128,8]{1,2,0:T(8,128)} %param.7) | copy-start | bytes 12292
  49.5 18.4 %collective-permute-start.27 = (bf16[2,8,32,128]{3,2,1,0:T(8,128)(2,1)S(1)}, bf16[2,8,32,128]{3,2,1,0:T(8,128)(2,1)S(1)}, u32[]{:S(2)}, u32[]{:S(2)}) collective-permute-start(bf16[2,8,32,128]{3,2,1,0:T(8,128)(2,1)S(1)} %shard_map.62.own_ref), channel_id=1, source_target_pairs={{0,4},{1,5},{2,6},{3,7},{4,0},{5,1},{6,2},{7,3},{8,12},{9,13},{10,... | collective-permute-start | bytes 393224 | tf_op jit(solution)/shard_map/ppermute | solution.py:338
  52.4 18.3 %collective-permute-start.26 = (bf16[2,8,32,128]{3,2,1,0:T(8,128)(2,1)S(1)}, bf16[2,8,32,128]{3,2,1,0:T(8,128)(2,1)S(1)}, u32[]{:S(2)}, u32[]{:S(2)}) collective-permute-start(bf16[2,8,32,128]{3,2,1,0:T(8,128)(2,1)S(1)} %shard_map.68.own_ref), channel_id=1, source_target_pairs={{0,4},{1,5},{2,6},{3,7},{4,0},{5,1},{6,2},{7,3},{8,12},{9,13},{10,... | collective-permute-start | bytes 393224 | tf_op jit(solution)/shard_map/ppermute | solution.py:338
  56.7 16.8 %collective-permute-start.23 = (bf16[2,8,32,128]{3,2,1,0:T(8,128)(2,1)S(1)}, bf16[2,8,32,128]{3,2,1,0:T(8,128)(2,1)S(1)}, u32[]{:S(2)}, u32[]{:S(2)}) collective-permute-start(bf16[2,8,32,128]{3,2,1,0:T(8,128)(2,1)S(1)} %shard_map.65.own_ref), channel_id=1, source_target_pairs={{0,4},{1,5},{2,6},{3,7},{4,0},{5,1},{6,2},{7,3},{8,12},{9,13},{10,... | collective-permute-start | bytes 393224 | tf_op jit(solution)/shard_map/ppermute | solution.py:338
  (2 other events, 3.4 us)
